TPU v7x, 512 devices: a whole 4x4x16 slice. The times are simulated.
512 devices in a mesh: img: 128 (over x, z, core), tok: 4 (over y).
Axes of the slice: x: 4, y: 4, z: 16, core: 2. Of those that a mesh axis runs over, the one named last changes fastest.
Arguments:
- tokens: bfloat16 [128, 32, 4, 8, 1024], P('img', None, 'tok'), may hold values from -6 to 6
- pair_list: int32 [128, 2], replicated, may hold values from 0 to 127, as said below
- owner_base: int32 [128], replicated, may hold values from 0 to 127, as said below
- embed_weight: bfloat16 [1024, 768], P('img'), may hold values from -0.1875 to 0.1875
- self_project: bfloat16 [768, 1152], P('img'), may hold values from -0.375 to 0.375
- self_output: bfloat16 [384, 768], P('img'), may hold values from -0.3125 to 0.3125
- cross_query: bfloat16 [768, 384], P('img'), may hold values from -0.375 to 0.375
- cross_keyval: bfloat16 [768, 768], P('img'), may hold values from -0.375 to 0.375
- cross_output: bfloat16 [384, 768], P('img'), may hold values from -0.3125 to 0.3125
Outputs:
- features: bfloat16 [128, 32, 4, 8, 768], P('img', None, 'tok')
Inputs may be any that keep to these rules, and one draw needn't show every extreme that they name: owner_base is a permutation: block g of image i is held by img index (owner_base[i] + g) mod 128. `pair_list`: every image is the first image of exactly one row; the owner_base values of a row's two images differ by 32 to 128 - 32 modulo 128.
All inputs are finite; a program needn't handle non-finite values.
Results may differ from a plain program's by a relative error of at most 0.027.
Values may be sent and summed in bfloat16 or wider, within the bound.
No kernel may reach another device: no remote copies, remote signals or barrier semaphores. Data moves between devices by JAX's collectives and lax.ppermute only.
A program may use at most 64 MiB of HBM per device.

v0:
```python
import math

import jax
import jax.numpy as jnp
from jax import lax
from jax.sharding import PartitionSpec as P

HEADS = 6
HD = 64


def normalize(values):
    mean_value = jnp.mean(values, axis=-1, keepdims=True)
    centred = values - mean_value
    variance = jnp.mean(centred * centred, axis=-1, keepdims=True)
    return centred * lax.rsqrt(variance + 1e-06)


def make_folder(query_heads, swapped, piece):
    keys_in, values_in = piece
    if swapped:
        keys_in = keys_in[::-1]
        values_in = values_in[::-1]
    branches = keys_in.shape[0]
    others = keys_in.shape[1]
    key_heads = keys_in.reshape(branches, others, HEADS, HD)
    value_heads = values_in.reshape(branches, others, HEADS, HD)
    scores = jnp.einsum(
        "brhd,bkhd->bhrk", query_heads, key_heads, preferred_element_type=jnp.float32
    ) / math.sqrt(HD)
    weights = jnp.exp(scores)
    numer = jnp.einsum(
        "bhrk,bkhd->brhd",
        weights.astype(jnp.bfloat16),
        value_heads,
        preferred_element_type=jnp.float32,
    )
    denom = jnp.sum(weights, axis=-1)
    return (numer, denom)


def finish(carry):
    numer, denom = carry
    branches, length = (numer.shape[0], numer.shape[1])
    return (
        (numer / jnp.transpose(denom, (0, 2, 1))[..., None])
        .astype(jnp.bfloat16)
        .reshape(branches, length, HEADS * HD)
    )


def shards(
    tokens,
    pair_list,
    owner_base,
    embed_weight,
    self_project,
    self_output,
    cross_query,
    cross_keyval,
    cross_output,
):
    holders_count = lax.axis_size("img")
    device = lax.axis_index("img")
    spread = tokens.shape[1]
    block_rows = tokens.shape[3]
    held = tokens.reshape(spread, block_rows, tokens.shape[4])
    embed_full, project_full, self_out_full, query_full, keyval_full, cross_out_full = (
        lax.all_gather(embed_weight, "img", axis=0, tiled=True),
        lax.all_gather(self_project, "img", axis=0, tiled=True),
        lax.all_gather(self_output, "img", axis=0, tiled=True),
        lax.all_gather(cross_query, "img", axis=0, tiled=True),
        lax.all_gather(cross_keyval, "img", axis=0, tiled=True),
        lax.all_gather(cross_output, "img", axis=0, tiled=True),
    )
    width = self_out_full.shape[0]
    model_width = self_out_full.shape[1]
    peer_ids = jnp.arange(holders_count, dtype=jnp.int32)
    spread_ids = jnp.arange(spread, dtype=jnp.int32)
    first_slot = (device - owner_base[pair_list[:, 0]]) % holders_count
    second_slot = (device - owner_base[pair_list[:, 1]]) % holders_count
    held_slot = jnp.where(
        first_slot < spread, first_slot, jnp.where(second_slot < spread, second_slot, -1)
    )
    slot_live = held_slot >= 0
    slot_index = jnp.clip(held_slot, 0, spread - 1)
    outgoing = jnp.where(
        slot_live[:, None, None], jnp.take(held, slot_index, axis=0), jnp.zeros((), jnp.bfloat16)
    )
    arrived = lax.all_to_all(outgoing, "img", split_axis=0, concat_axis=0, tiled=True)
    my_pair = pair_list[device]
    pair_bases = owner_base[my_pair]
    sources = (pair_bases[:, None] + spread_ids[None, :]) % holders_count
    gathered_rows = jnp.take(arrived, sources.reshape(-1), axis=0)
    gathered_rows = gathered_rows.reshape(2, spread * block_rows, arrived.shape[2])
    embedded = jnp.einsum(
        "bre,ed->brd", gathered_rows, embed_full, preferred_element_type=jnp.float32
    ).astype(jnp.bfloat16)
    length = embedded.shape[1]
    normed = normalize(embedded.astype(jnp.float32)).astype(jnp.bfloat16)
    self_queries = jnp.einsum(
        "brd,de->bre", normed, project_full[:, :width], preferred_element_type=jnp.float32
    ).astype(jnp.bfloat16)
    self_heads = self_queries.reshape(2, length, HEADS, HD)
    own_self = jnp.einsum(
        "brd,de->bre", normed, project_full[:, width:], preferred_element_type=jnp.float32
    ).astype(jnp.bfloat16)
    own_cross = jnp.einsum(
        "brd,de->bre", normed, keyval_full, preferred_element_type=jnp.float32
    ).astype(jnp.bfloat16)
    self_carry = make_folder(
        self_heads,
        False,
        (
            lax.all_gather(own_self[..., :width], "tok", axis=1, tiled=True),
            lax.all_gather(own_self[..., width:], "tok", axis=1, tiled=True),
        ),
    )
    attended = finish(self_carry)
    after_self = embedded.astype(jnp.float32) + jnp.einsum(
        "bre,ed->brd", attended, self_out_full, preferred_element_type=jnp.float32
    )
    second_normed = normalize(after_self).astype(jnp.bfloat16)
    cross_queries = jnp.einsum(
        "brd,de->bre", second_normed, query_full, preferred_element_type=jnp.float32
    ).astype(jnp.bfloat16)
    cross_heads = cross_queries.reshape(2, length, HEADS, HD)
    cross_carry = make_folder(
        cross_heads,
        True,
        (
            lax.all_gather(own_cross[..., :width], "tok", axis=1, tiled=True),
            lax.all_gather(own_cross[..., width:], "tok", axis=1, tiled=True),
        ),
    )
    cross_attended = finish(cross_carry)
    mixed = after_self + jnp.einsum(
        "bre,ed->brd", cross_attended, cross_out_full, preferred_element_type=jnp.float32
    )
    result_rows = mixed.astype(jnp.bfloat16).reshape(2, spread, block_rows, model_width)
    first_back = (peer_ids - pair_bases[0]) % holders_count
    second_back = (peer_ids - pair_bases[1]) % holders_count
    first_part = jnp.take(result_rows[0], jnp.clip(first_back, 0, spread - 1), axis=0)
    second_part = jnp.take(result_rows[1], jnp.clip(second_back, 0, spread - 1), axis=0)
    backward = jnp.where(
        (first_back < spread)[:, None, None],
        first_part,
        jnp.where((second_back < spread)[:, None, None], second_part, jnp.zeros((), jnp.bfloat16)),
    )
    returned = lax.all_to_all(backward, "img", split_axis=0, concat_axis=0, tiled=True)
    selector = (held_slot[None, :] == spread_ids[:, None]).astype(jnp.bfloat16)
    summed = jnp.einsum(
        "ge,ebd->gbd", selector, returned, preferred_element_type=jnp.float32
    ).astype(jnp.bfloat16)
    return summed.reshape(1, spread, 1, block_rows, model_width)


def solution(mesh):
    placed = (
        P("img", None, "tok", None, None),
        P(),
        P(),
        P("img", None),
        P("img", None),
        P("img", None),
        P("img", None),
        P("img", None),
        P("img", None),
    )
    return jax.shard_map(
        shards,
        mesh=mesh,
        in_specs=placed,
        out_specs=P("img", None, "tok", None, None),
        check_vma=False,
    )
```

profile of v0, /device:TPU:24, one launch (start us, length us, event | category | flops | bytes accessed | tf_op | source)
XLA Modules:
  0.0 904.3 jit_solution(11284459768907891292)
XLA Ops:
  7.3 1.6 gather_fusion
  8.9 1.6 gather_fusion.1
  11.3 1.7 select_select_fusion
  13.0 19.9 %all-to-all-start = ((bf16[128,8,1024]{2,1,0:T(8,128)(2,1)}), bf16[128,8,1024]{2,1,0:T(8,128)(2,1)S(1)}, u32[]{:S(2)}, u32[]{:S(2)}) async-start(bf16[128,8,1024]{2,1,0:T(8,128)(2,1)} %select_select_fusion), calls=%async_computation | async-start | bytes 4194304 | tf_op jit(solution)/shard_map/all_to_all | solution.py:90
  36.5 149.6 %all-gather.23.cloned.1.call-done = bf16[128,6,1152]{2,1,0:T(8,128)(2,1)} async-done(((bf16[1,6,1152]{2,1,0:T(8,128)(2,1)}), bf16[128,6,1152]{2,1,0:T(8,128)(2,1)}) %all-gather.23.cloned.1.call-update) | async-done | bytes 1769488 | tf_op jit(solution)/shard_map/all_gather | solution.py:70
  186.1 3.9 reshape.451
  191.7 132.7 %all-gather.13.cloned.1.call-done = bf16[1024,768]{1,0:T(8,128)(2,1)} async-done(((bf16[8,768]{1,0:T(8,128)(2,1)}), bf16[1024,768]{1,0:T(8,128)(2,1)}) %all-gather.13.cloned.1.call-update) | async-done | bytes 1572880 | tf_op jit(solution)/shard_map/all_gather | solution.py:69
  324.4 2.8 convert_reduce_fusion
  330.0 132.6 %all-gather.25.cloned.1.call-done = bf16[128,6,768]{2,1,0:T(8,128)(2,1)} async-done(((bf16[1,6,768]{2,1,0:T(8,128)(2,1)}), bf16[128,6,768]{2,1,0:T(8,128)(2,1)}) %all-gather.25.cloned.1.call-update) | async-done | bytes 1179664 | tf_op jit(solution)/shard_map/all_gather | solution.py:73
  462.6 3.2 reshape.468
  465.8 2.1 convolution_convert_fusion
  469.0 94.3 %all-gather.1 = bf16[128,3,768]{2,1,0:T(4,128)(2,1)S(1)} all-gather(bf16[1,3,768]{2,1,0:T(4,128)(2,1)S(1)} %bitcast.102), channel_id=1, replica_groups=mesh['img'=128,'tok'=4] {'img'}, dimensions={0}, use_global_device_ids=true | all-gather | bytes 594432 | tf_op jit(solution)/shard_map/all_gather | solution.py:71
  563.4 1.2 reshape.467
  564.6 94.0 %all-gather.3 = bf16[128,6,384]{2,1,0:T(8,128)(2,1)S(1)} all-gather(bf16[1,6,384]{2,1,0:T(8,128)(2,1)S(1)} %bitcast.103), channel_id=1, replica_groups=mesh['img'=128,'tok'=4] {'img'}, dimensions={0}, use_global_device_ids=true | all-gather | bytes 594432 | tf_op jit(solution)/shard_map/all_gather | solution.py:72
  659.5 92.9 %all-gather.4 = bf16[128,3,768]{2,1,0:T(4,128)(2,1)S(1)} all-gather(bf16[1,3,768]{2,1,0:T(4,128)(2,1)S(1)} %bitcast.104), channel_id=1, replica_groups=mesh['img'=128,'tok'=4] {'img'}, dimensions={0}, use_global_device_ids=true | all-gather | bytes 594432 | tf_op jit(solution)/shard_map/all_gather | solution.py:74
  752.5 1.2 reshape.470
  755.7 1.2 compare_and_fusion
  756.9 1.3 compare_and_fusion.1
  759.0 1.7 copy.32
  760.8 1.7 copy.30
  762.5 2.3 fusion
  764.8 2.1 fusion.43
  769.5 1.6 rev.7
  771.1 1.7 copy.36
  772.8 14.3 %all-gather.19.cloned.1.call-done = bf16[2,1024,384]{2,1,0:T(8,128)(2,1)} async-done(((bf16[2,256,384]{2,1,0:T(8,128)(2,1)}), bf16[2,1024,384]{2,1,0:T(8,128)(2,1)}) %all-gather.19.cloned.1.call-update) | async-done | bytes 1572880 | tf_op jit(solution)/shard_map/all_gather | solution.py:133
  787.1 1.6 rev.6
  788.7 1.6 copy.34
  790.3 4.0 fusion.2
  794.3 2.1 fusion.37
  797.7 1.8 gather_fusion.6
  799.6 2.8 fusion.18
  802.3 93.7 %all_to_all.10 = bf16[128,8,768]{2,1,0:T(8,128)(2,1)S(1)} all-to-all(bf16[128,8,768]{2,1,0:T(8,128)(2,1)S(1)} %fusion.18), channel_id=1, replica_groups=mesh['img'=128,'tok'=4] {'img'}, dimensions={0} | all-to-all | bytes 3145728 | tf_op jit(solution)/shard_map/all_to_all | solution.py:150
  (97 shorter events, 19.8 us)
Async XLA Ops:
  6.5 4.0 copy-start
  13.0 22.2 %copy-start.13 = (s32[128,2]{0,1:T(2,128)S(1)}, s32[128,2]{0,1:T(2,128)}, u32[]{:S(2)}) copy-start(s32[128,2]{0,1:T(2,128)} %param.12) | copy-start | bytes 3076
  13.0 22.4 %copy-start.2 = (s32[128]{0:T(128)S(1)}, s32[128]{0:T(128)}, u32[]{:S(2)}) copy-start(s32[128]{0:T(128)} %param.13) | copy-start | bytes 1540
  13.0 177.0 %all-to-all-start = ((bf16[128,8,1024]{2,1,0:T(8,128)(2,1)}), bf16[128,8,1024]{2,1,0:T(8,128)(2,1)S(1)}, u32[]{:S(2)}, u32[]{:S(2)}) async-start(bf16[128,8,1024]{2,1,0:T(8,128)(2,1)} %select_select_fusion), calls=%async_computation | async-start | bytes 4194304 | tf_op jit(solution)/shard_map/all_to_all | solution.py:90
  32.9 153.1 %all-gather.23.cloned.1.call-start = ((), (), s32[]{:S(2)}) async-start(), calls=%async_computation.7 | async-start | bytes 2377728 | tf_op jit(solution)/shard_map/all_gather | solution.py:70
  33.6 290.7 %all-gather.13.cloned.1.call-start = ((), (), s32[]{:S(2)}) async-start(), calls=%async_computation.2 | async-start | bytes 1585152 | tf_op jit(solution)/shard_map/all_gather | solution.py:69
  34.4 428.2 %all-gather.25.cloned.1.call-start = ((), (), s32[]{:S(2)}) async-start(), calls=%async_computation.8 | async-start | bytes 1585152 | tf_op jit(solution)/shard_map/all_gather | solution.py:73
  35.1 723.9 %all-gather.17.cloned.1.call-start = ((), (), s32[]{:S(2)}) async-start(), calls=%async_computation.4 | async-start | bytes 1966080 | tf_op jit(solution)/shard_map/all_gather | solution.py:115
  191.7 135.9 %copy-start.8 = (bf16[768,1152]{1,0:T(8,128)(2,1)S(1)}, bf16[768,1152]{1,0:T(8,128)(2,1)}, u32[]{:S(2)}) copy-start(bf16[768,1152]{1,0:T(8,128)(2,1)} %reshape.451) | copy-start | bytes 5308420
  327.2 431.0 %copy-start.4 = (bf16[2,256,768]{2,1,0:T(8,128)(2,1)}, bf16[2,256,768]{2,1,0:T(8,128)(2,1)S(1)}, u32[]{:S(2)}) copy-start(bf16[2,256,768]{2,1,0:T(8,128)(2,1)S(1)} %get-tuple-element.19) | copy-start | bytes 2359300
  329.4 431.4 %all-gather.15.cloned.1.call-start = ((), (), s32[]{:S(2)}) async-start(), calls=%async_computation.3 | async-start | bytes 1966080 | tf_op jit(solution)/shard_map/all_gather | solution.py:116
  330.0 439.5 %all-gather.21.cloned.1.call-start = ((), (), s32[]{:S(2)}) async-start(), calls=%async_computation.6 | async-start | bytes 1966080 | tf_op jit(solution)/shard_map/all_gather | solution.py:132
  468.0 1.1 copy-start.10
  469.0 95.6 %copy-start.11 = (bf16[6,384]{1,0:T(8,128)(2,1)S(1)}, bf16[6,384]{1,0:T(8,128)(2,1)}, u32[]{:S(2)}) copy-start(bf16[6,384]{1,0:T(8,128)(2,1)} %param.17) | copy-start | bytes 13828
  469.0 318.1 %all-gather.19.cloned.1.call-start = ((), (), s32[]{:S(2)}) async-start(), calls=%async_computation.5 | async-start | bytes 1966080 | tf_op jit(solution)/shard_map/all_gather | solution.py:133
  563.3 96.2 %copy-start.12 = (bf16[3,768]{1,0:T(4,128)(2,1)S(1)}, bf16[3,768]{1,0:T(4,128)(2,1)}, u32[]{:S(2)}) copy-start(bf16[3,768]{1,0:T(4,128)(2,1)} %param.19) | copy-start | bytes 13828
  764.8 2.1 copy-start.5
  764.8 2.1 copy-start.7
  767.5 1.1 copy-start.9
  790.3 4.0 copy-start.3
  794.3 2.1 copy-start.6
  797.7 1.9 copy-start.14
  797.7 1.9 copy-start.15
  797.7 1.9 copy-start.16
  802.3 95.1 %copy-start.1 = (bf16[1,32,1,8,1024]{4,3,2,1,0:T(8,128)(2,1)S(1)}, bf16[1,32,1,8,1024]{4,3,2,1,0:T(8,128)(2,1)}, u32[]{:S(2)}) copy-start(bf16[1,32,1,8,1024]{4,3,2,1,0:T(8,128)(2,1)} %param.11) | copy-start | bytes 1572868
Sparse Core Ops, SparseCore 0:
  36.8 149.2 all-gather.22
  189.1 135.2 all-gather.12
  327.4 135.1 all-gather.24
  464.6 29.2 all-gather.16
  495.8 34.3 all-gather.14
  532.2 34.3 all-gather.20
  759.1 27.9 all-gather.18
where the time goes:
time: 907 us; the launch traced here: 904 us
  waiting for transfers between devices  432 us (48%)
  blocking collectives  375 us (41%)
  local copies, waits for them, and re-layouts  33.3 us (4%)
  starting transfers between devices  20.2 us (2%)
  matrix products  19.1 us (2%)
  between operations  13.9 us (2%)
  other arithmetic  11.2 us (1%)
    all_gather x1, waiting for transfers between devices, shards(): lax.all_gather(self_project, 'img', axis=0, tiled=True)  150 us
    all_gather x1, waiting for transfers between devices, shards(): lax.all_gather(embed_weight, 'img', axis=0, tiled=True)  133 us
    all_gather x1, waiting for transfers between devices, shards(): lax.all_gather(cross_keyval, 'img', axis=0, tiled=True)  133 us
    all_gather x1, blocking collectives, shards(): lax.all_gather(self_output, 'img', axis=0, tiled=True)  94.3 us
    all_gather x1, blocking collectives, shards(): lax.all_gather(cross_query, 'img', axis=0, tiled=True)  94 us
    all_to_all x1, blocking collectives, shards(): lax.all_to_all(backward, 'img', split_axis=0, concat_axis=0, tiled=True)  93.7 us
    all_gather x1, blocking collectives, shards(): lax.all_gather(cross_output, 'img', axis=0, tiled=True)  92.9 us
    all_to_all x1, starting transfers between devices, shards(): lax.all_to_all(outgoing, 'img', split_axis=0, concat_axis=0, tiled=True)  19.9 us
  transfers between devices with their start and end apart: 8, of which 4 were waited for; matrix products, arithmetic and copies ran while one was open for 4% of the time, Pallas kernels for 0%

commit v1 on v0

v1 whole, which is shorter than its diff:
```python
import math

import jax
import jax.numpy as jnp
import numpy as np
from jax import lax
from jax.sharding import Mesh, PartitionSpec as P

HEADS = 6
HD = 64
LANES = 128
IMG = ("x", "z", "c")

SECTIONS = (
    ("embed", 8, 6),
    ("project", 6, 9),
    ("self_out", 3, 6),
    ("query", 6, 3),
    ("keyval", 6, 6),
    ("cross_out", 3, 6),
)
PACKED = sum(rows * tiles for _, rows, tiles in SECTIONS)


def normalize(values):
    mean_value = jnp.mean(values, axis=-1, keepdims=True)
    centred = values - mean_value
    variance = jnp.mean(centred * centred, axis=-1, keepdims=True)
    return centred * lax.rsqrt(variance + 1e-06)


def row_orders(toks, z_low, cores):
    quarter = PACKED // toks
    tiles = []
    at = 0
    for _, rows, count in SECTIONS:
        for _ in range(count):
            tiles.append((at, rows))
            at += rows
    orders = np.zeros((toks, quarter * z_low * cores), np.int32)
    places = []
    for tok in range(toks):
        out = 0
        for start, rows in tiles:
            if start // quarter != tok:
                continue
            assert (start + rows - 1) // quarter == tok
            places.append((tok, out, rows * z_low * cores))
            for z in range(z_low):
                for core in range(cores):
                    for row in range(rows):
                        orders[tok, out] = (core * z_low + z) * quarter + start - tok * quarter + row
                        out += 1
    return orders, places


def pack(shards_in):
    pieces = []
    for shard in shards_in:
        rows, width = shard.shape
        pieces.append(
            jnp.transpose(shard.reshape(rows, width // LANES, LANES), (1, 0, 2)).reshape(-1, LANES)
        )
    return jnp.concatenate(pieces, axis=0)


def spread_to(value, axis):
    count = lax.axis_size(axis)
    return lax.all_to_all(
        jnp.broadcast_to(value[None], (count,) + value.shape), axis, 0, 0, tiled=True
    )


def gather_weights(shards_in):
    toks, cores, depth = lax.axis_size("tok"), lax.axis_size("c"), lax.axis_size("z")
    tok = lax.axis_index("tok")
    quarter = PACKED // toks
    z_low = depth // cores
    orders, places = row_orders(toks, z_low, cores)
    mine = lax.dynamic_slice_in_dim(pack(shards_in), tok * quarter, quarter, axis=0)
    along_z = spread_to(mine, "z")
    halves = lax.all_to_all(
        along_z.reshape(cores, z_low, quarter, LANES), "c", 0, 0, tiled=True
    )
    order = lax.dynamic_index_in_dim(jnp.asarray(orders), tok, axis=0, keepdims=False)
    count = orders.shape[1]
    mover = (order[:, None] == jnp.arange(count, dtype=jnp.int32)[None, :]).astype(jnp.bfloat16)
    ordered = jnp.dot(
        mover, halves.reshape(count, LANES), preferred_element_type=jnp.float32
    ).astype(jnp.bfloat16)
    along_x = spread_to(ordered, "x")
    along_y = spread_to(along_x, "tok")
    everything = spread_to(along_y, "c")
    full = []
    next_tile = 0
    for _, _, tiles in SECTIONS:
        columns = []
        for place_tok, start, rows in places[next_tile : next_tile + tiles]:
            part = everything[:, place_tok, :, start : start + rows, :]
            columns.append(jnp.transpose(part, (1, 0, 2, 3)).reshape(-1, LANES))
        full.append(jnp.concatenate(columns, axis=1))
        next_tile += tiles
    return full


def round_ring(own):
    count = lax.axis_size("tok")
    right = [(i, (i + 1) % count) for i in range(count)]
    left = [(i, (i - 1) % count) for i in range(count)]
    half = own.shape[1] // 2
    from_left = lax.ppermute(own, "tok", right)
    from_right = lax.ppermute(own, "tok", left)
    far_low = lax.ppermute(from_left[:, :half], "tok", right)
    far_high = lax.ppermute(from_right[:, half:], "tok", left)
    return [own, from_left, from_right, far_low, far_high]


def attend(queries, keys_in, values_in):
    branches, length = queries.shape[:2]
    others = keys_in.shape[1]
    query_heads = queries.reshape(branches, length, HEADS, HD)
    key_heads = keys_in.reshape(branches, others, HEADS, HD)
    value_heads = values_in.reshape(branches, others, HEADS, HD)
    scores = jnp.einsum(
        "brhd,bkhd->bhrk", query_heads, key_heads, preferred_element_type=jnp.float32
    ) / math.sqrt(HD)
    weights = jnp.exp(scores)
    numer = jnp.einsum(
        "bhrk,bkhd->brhd",
        weights.astype(jnp.bfloat16),
        value_heads,
        preferred_element_type=jnp.float32,
    )
    denom = jnp.sum(weights, axis=-1)
    return (
        (numer / jnp.transpose(denom, (0, 2, 1))[..., None])
        .astype(jnp.bfloat16)
        .reshape(branches, length, HEADS * HD)
    )


def multiply(rows, matrix):
    return jnp.einsum("brd,de->bre", rows, matrix, preferred_element_type=jnp.float32)


def shards(tokens, pair_list, owner_base, *weight_shards):
    groups = lax.axis_size("x")
    row_devices = lax.axis_size("z") * lax.axis_size("c")
    devices = groups * row_devices
    column = lax.axis_index("z") * lax.axis_size("c") + lax.axis_index("c")
    spread, block_rows, encoder = tokens.shape[1], tokens.shape[3], tokens.shape[4]
    held = tokens.reshape(spread, block_rows, encoder)
    part = encoder // groups

    parted = jnp.transpose(held.reshape(spread, block_rows, groups, part), (2, 0, 1, 3))
    pieces = lax.all_to_all(parted, "x", 0, 0, tiled=True).reshape(devices, block_rows, part)
    full = gather_weights(weight_shards)
    embed_full, project_full, self_out_full, query_full, keyval_full, cross_out_full = full
    width, model_width = self_out_full.shape

    bases = owner_base[pair_list]
    slot = (column - bases) % spread
    source = ((bases + slot - column) // row_devices) % groups
    place = source * spread + slot
    outgoing = jnp.take(pieces, place.reshape(-1), axis=0).reshape(
        devices, 2, block_rows, part
    )
    arrived = lax.all_to_all(outgoing, IMG, 0, 0, tiled=True)
    arrived = arrived.reshape(groups, row_devices, 2, block_rows, part)
    rows_in = jnp.transpose(arrived, (2, 1, 3, 0, 4)).reshape(2, row_devices * block_rows, encoder)
    embedded = multiply(rows_in, embed_full).astype(jnp.bfloat16)
    all_embedded = jnp.concatenate(round_ring(embedded), axis=1)
    all_normed = normalize(all_embedded.astype(jnp.float32)).astype(jnp.bfloat16)
    length = embedded.shape[1]
    normed = all_normed[:, :length]
    queries = multiply(normed, project_full[:, :width]).astype(jnp.bfloat16)
    keys = multiply(all_normed, project_full[:, width : 2 * width]).astype(jnp.bfloat16)
    values = multiply(all_normed, project_full[:, 2 * width :]).astype(jnp.bfloat16)
    cross_keys = multiply(all_normed, keyval_full[:, :width]).astype(jnp.bfloat16)
    cross_values = multiply(all_normed, keyval_full[:, width:]).astype(jnp.bfloat16)
    attended = attend(queries, keys, values)
    after_self = embedded.astype(jnp.float32) + multiply(attended, self_out_full)
    second_normed = normalize(after_self).astype(jnp.bfloat16)
    cross_queries = multiply(second_normed, query_full).astype(jnp.bfloat16)
    cross_attended = attend(cross_queries[::-1], cross_keys, cross_values)[::-1]
    mixed = after_self + multiply(cross_attended, cross_out_full)

    halves = groups // 2
    result = mixed.astype(jnp.bfloat16).reshape(
        2, row_devices, block_rows, halves, model_width // halves
    )
    backward = jnp.transpose(result, (0, 3, 1, 2, 4)).reshape(
        devices, block_rows, model_width // halves
    )
    returned = lax.all_to_all(backward, IMG, 0, 0, tiled=True)
    my_half = lax.axis_index("x") // halves
    my_bases = lax.dynamic_index_in_dim(bases, my_half, axis=1, keepdims=False)
    my_slot = (column - my_bases) % spread
    my_place = ((my_bases + my_slot - column) // row_devices) % groups * spread + my_slot
    selector = (
        my_place[None, :] == jnp.arange(devices, dtype=jnp.int32)[:, None]
    ).astype(jnp.bfloat16)
    partial = jnp.einsum(
        "ge,ebd->gbd", selector, returned, preferred_element_type=jnp.float32
    ).astype(jnp.bfloat16)
    home = lax.all_to_all(
        partial.reshape(groups, spread, block_rows, model_width // halves), "x", 0, 0, tiled=True
    )
    home = home.reshape(2, halves, spread, block_rows, model_width // halves)
    total = home[0].astype(jnp.float32) + home[1].astype(jnp.float32)
    summed = jnp.transpose(total.astype(jnp.bfloat16), (1, 2, 0, 3))
    return summed.reshape(1, spread, 1, block_rows, model_width)


def solution(mesh):
    chips = Mesh(mesh.devices.reshape(4, 16, 2, 4), ("x", "z", "c", "tok"))
    rows = P(IMG, None)
    tokens = P(IMG, None, "tok", None, None)
    return jax.shard_map(
        shards,
        mesh=chips,
        in_specs=(tokens, P(), P()) + (rows,) * 6,
        out_specs=tokens,
        check_vma=False,
    )
```

time: 907 us -> 372 us (0.41)
  blocking collectives: 375 us -> 43.3 us
  waiting for transfers between devices: 432 us -> 146 us
  local copies, waits for them, and re-layouts: 33.3 us -> 91.6 us
  starting transfers between devices: 20.2 us -> 53.7 us
  between operations: 13.9 us -> 0.92 us
    all_gather x7 -> x0, waiting for transfers between devices: 429 us -> none  [the longest x1 150 us: shards(): lax.all_gather(self_project, 'img', axis=0, tiled=True)]
    all_gather x3 -> x0, blocking collectives: 281 us -> none  [the longest x1 94.3 us: shards(): lax.all_gather(self_output, 'img', axis=0, tiled=True)]
    all_to_all x1 -> x5, waiting for transfers between devices: 0.01 us -> 140 us  [the longest x1 47.3 us: shards(): arrived = lax.all_to_all(outgoing, IMG, 0, 0, tiled=True)]
    all_to_all x1 -> x4, blocking collectives: 93.7 us -> 43.3 us  [the longest x2 24.1 us: spread_to(): lax.all_to_all(jnp.broadcast_to(value[None], (count,) + value.shape), axi...]
    reshape x0 -> x19, local copies, waits for them, and re-layouts: none -> 23.2 us  [the longest x12 19.3 us: gather_weights(): columns.append(jnp.transpose(part, (1, 0, 2, 3)).reshape(-1, LANES))]
    all_to_all x1 -> x5, starting transfers between devices: 19.9 us -> 40.5 us  [the longest x2 20 us: spread_to(): lax.all_to_all(jnp.broadcast_to(value[None], (count,) + value.shape), axi...]
    unnamed x39 -> x103, local copies, waits for them, and re-layouts: 11.4 us -> 31.4 us
    transpose x0 -> x30, local copies, waits for them, and re-layouts: none -> 14.8 us  [the longest x26 12.5 us: gather_weights(): columns.append(jnp.transpose(part, (1, 0, 2, 3)).reshape(-1, LANES))]
  transfers between devices with their start and end apart: 8 -> 9, of which waited for: 4 -> 6; matrix products, arithmetic and copies ran while one was open for 4% -> 21% of each run, Pallas kernels for 0% -> 0%
where the time goes in v1:
time: 372 us; the launch traced here: 368 us
  waiting for transfers between devices  146 us (39%)
  local copies, waits for them, and re-layouts  91.6 us (25%)
  starting transfers between devices  53.7 us (14%)
  blocking collectives  43.3 us (12%)
  matrix products  26.5 us (7%)
  other arithmetic  5.46 us (1%)
    all_to_all x1, waiting for transfers between devices, shards(): arrived = lax.all_to_all(outgoing, IMG, 0, 0, tiled=True)  47.3 us
    all_to_all x1, waiting for transfers between devices, shards(): returned = lax.all_to_all(backward, IMG, 0, 0, tiled=True)  44.1 us
    all_to_all x2, waiting for transfers between devices, spread_to(): lax.all_to_all(jnp.broadcast_to(value[None], (count,) + value.shape), axi...  39.9 us
    unnamed x103, local copies, waits for them, and re-layouts  31.4 us
    all_to_all x2, blocking collectives, spread_to(): lax.all_to_all(jnp.broadcast_to(value[None], (count,) + value.shape), axi...  24.1 us
    all_to_all x2, starting transfers between devices, spread_to(): lax.all_to_all(jnp.broadcast_to(value[None], (count,) + value.shape), axi...  20 us
    reshape x12, local copies, waits for them, and re-layouts, gather_weights(): columns.append(jnp.transpose(part, (1, 0, 2, 3)).reshape(-1, LANES))  19.3 us
    dot_general x9, matrix products, multiply(): jnp.einsum('brd,de->bre', rows, matrix, preferred_element_type=jnp.float32)  16.8 us
  transfers between devices with their start and end apart: 9, of which 6 were waited for; matrix products, arithmetic and copies ran while one was open for 21% of the time, Pallas kernels for 0%

profile of v1, /device:TPU:24, one launch (start us, length us, event | category | flops | bytes accessed | tf_op | source)
XLA Modules:
  0.0 367.9 jit_solution(718881146622679932)
XLA Ops:
  5.4 15.2 %all-to-all-start.2 = ((bf16[16,48,128]{2,1,0:T(8,128)(2,1)}), bf16[16,48,128]{2,1,0:T(8,128)(2,1)S(1)}, u32[]{:S(2)}, u32[]{:S(2)}) async-start(bf16[16,48,128]{2,1,0:T(8,128)(2,1)} %broadcast_in_dim.20), calls=%async_computation.2 | async-start | bytes 393216 | tf_op jit(solution)/shard_map/all_to_all | solution.py:69
  23.0 14.1 %all-to-all-done.2 = bf16[16,48,128]{2,1,0:T(8,128)(2,1)S(1)} async-done(((bf16[16,48,128]{2,1,0:T(8,128)(2,1)}), bf16[16,48,128]{2,1,0:T(8,128)(2,1)S(1)}, u32[]{:S(2)}, u32[]{:S(2)}) %all-to-all-start.2) | async-done | bytes 196640 | tf_op jit(solution)/shard_map/all_to_all | solution.py:69
  37.1 3.9 %all_to_all.45 = bf16[2,8,48,128]{3,2,1,0:T(8,128)(2,1)S(1)} all-to-all(bf16[2,8,48,128]{3,2,1,0:T(8,128)(2,1)S(1)} %bitcast.315), channel_id=1, replica_groups=mesh['x'=4,'z'=16,'c'=2,'tok'=4] {'c'}, dimensions={0} | all-to-all | bytes 393216 | tf_op jit(solution)/shard_map/all_to_all | solution.py:82
  41.0 4.3 %all-to-all-start = ((bf16[4,32,8,256]{3,2,1,0:T(8,128)(2,1)}), bf16[4,32,8,256]{3,2,1,0:T(8,128)(2,1)S(1)}, u32[]{:S(2)}, u32[]{:S(2)}) async-start(bf16[4,32,8,256]{3,2,1,0:T(8,128)(2,1)} %copy.158), calls=%async_computation | async-start | bytes 1048576 | tf_op jit(solution)/shard_map/all_to_all | solution.py:156
  46.6 8.5 %all-to-all-done = bf16[4,32,8,256]{3,2,1,0:T(8,128)(2,1)S(1)} async-done(((bf16[4,32,8,256]{3,2,1,0:T(8,128)(2,1)}), bf16[4,32,8,256]{3,2,1,0:T(8,128)(2,1)S(1)}, u32[]{:S(2)}, u32[]{:S(2)}) %all-to-all-start) | async-done | bytes 524320 | tf_op jit(solution)/shard_map/all_to_all | solution.py:156
  55.2 14.1 %all_to_all.46 = bf16[4,768,128]{2,1,0:T(8,128)(2,1)S(1)} all-to-all(bf16[4,768,128]{2,1,0:T(8,128)(2,1)S(1)} %broadcast_in_dim.21), channel_id=1, replica_groups=mesh['x'=4,'z'=16,'c'=2,'tok'=4] {'x'}, dimensions={0} | all-to-all | bytes 1572864 | tf_op jit(solution)/shard_map/all_to_all | solution.py:69
  69.3 2.2 broadcast_in_dim.25
  71.5 4.8 %all-to-all-start.5 = ((bf16[4,4,768,128]{3,2,1,0:T(8,128)(2,1)}), bf16[4,4,768,128]{3,2,1,0:T(8,128)(2,1)S(1)}, u32[]{:S(2)}, u32[]{:S(2)}) async-start(bf16[4,4,768,128]{3,2,1,0:T(8,128)(2,1)} %broadcast_in_dim.25), calls=%async_computation.5 | async-start | bytes 6291456 | tf_op jit(solution)/shard_map/all_to_all | solution.py:69
  76.9 1.9 gather_fusion
  79.1 2.8 gather_fusion.1
  81.9 2.3 broadcast_select_fusion
  84.2 25.7 %all-to-all-done.5 = bf16[4,4,768,128]{3,2,1,0:T(8,128)(2,1)S(1)} async-done(((bf16[4,4,768,128]{3,2,1,0:T(8,128)(2,1)}), bf16[4,4,768,128]{3,2,1,0:T(8,128)(2,1)S(1)}, u32[]{:S(2)}, u32[]{:S(2)}) %all-to-all-start.5) | async-done | bytes 3145760 | tf_op jit(solution)/shard_map/all_to_all | solution.py:69
  111.4 10.0 %all_to_all.47 = bf16[2,4,4,768,128]{4,3,2,1,0:T(8,128)(2,1)} all-to-all(bf16[2,4,4,768,128]{4,3,2,1,0:T(8,128)(2,1)S(1)} %broadcast_in_dim.26), channel_id=1, replica_groups=mesh['x'=4,'z'=16,'c'=2,'tok'=4] {'c'}, dimensions={0} | all-to-all | bytes 12582912 | tf_op jit(solution)/shard_map/all_to_all | solution.py:69
  121.3 7.6 %all-to-all-start.1 = ((bf16[128,2,8,256]{3,2,1,0:T(8,128)(2,1)}), bf16[128,2,8,256]{3,2,1,0:T(8,128)(2,1)S(1)}, u32[]{:S(2)}, u32[]{:S(2)}) async-start(bf16[128,2,8,256]{3,2,1,0:T(8,128)(2,1)} %broadcast_select_fusion), calls=%async_computation.1 | async-start | bytes 2097152 | tf_op jit(solution)/shard_map/all_to_all | solution.py:168
  129.0 2.2 slice_bitcast_fusion.12
  137.3 47.3 %all-to-all-done.1 = bf16[128,2,8,256]{3,2,1,0:T(8,128)(2,1)S(1)} async-done(((bf16[128,2,8,256]{3,2,1,0:T(8,128)(2,1)}), bf16[128,2,8,256]{3,2,1,0:T(8,128)(2,1)S(1)}, u32[]{:S(2)}, u32[]{:S(2)}) %all-to-all-start.1) | async-done | bytes 1048608 | tf_op jit(solution)/shard_map/all_to_all | solution.py:168
  184.8 2.4 constant_dynamic-update-slice_fusion.10
  187.2 4.0 %collective-permute-start = (bf16[2,256,768]{2,1,0:T(8,128)(2,1)S(1)}, bf16[2,256,768]{2,1,0:T(8,128)(2,1)S(1)}, u32[]{:S(2)}, u32[]{:S(2)}) collective-permute-start(bf16[2,256,768]{2,1,0:T(8,128)(2,1)S(1)} %get-tuple-element.42), channel_id=1, source_target_pairs={{0,1},{1,2},{2,3},{3,0},{4,5},{5,6},{6,7},{7,4},{8,9},{9,10},{10,1... | collective-permute-start | bytes 2359304 | tf_op jit(solution)/shard_map/ppermute | solution.py:111
  191.9 1.9 collective-permute-start.1
  196.5 3.7 %fusion.97 = (bf16[2,1,4,96,128]{4,3,2,1,0:T(8,128)(2,1)S(1)}, bf16[2,1,4,96,128]{4,3,2,1,0:T(8,128)(2,1)}, bf16[2,1,4,96,128]{4,3,2,1,0:T(8,128)(2,1)}, bf16[2,...) fusion(bf16[2,4,4,768,128]{4,3,2,1,0:T(8,128)(2,1)} %all_to_all.47), kind=kLoop, calls=%fused_computation.200 | loop fusion | bytes 7077888 | tf_op jit(solution)/shard_map/slice | solution.py:99
  200.3 6.6 %collective-permute-done = bf16[2,256,768]{2,1,0:T(8,128)(2,1)S(1)} collective-permute-done((bf16[2,256,768]{2,1,0:T(8,128)(2,1)S(1)}, bf16[2,256,768]{2,1,0:T(8,128)(2,1)S(1)}, u32[]{:S(2)}, u32[]{:S(2)}) %collective-permute-start) | collective-permute-done | bytes 786464 | tf_op jit(solution)/shard_map/ppermute | solution.py:111
  208.6 5.2 %collective-permute-start.2 = (bf16[2,128,768]{2,1,0:T(8,128)(2,1)}, bf16[2,128,768]{2,1,0:T(8,128)(2,1)}, u32[]{:S(2)}, u32[]{:S(2)}) collective-permute-start(bf16[2,128,768]{2,1,0:T(8,128)(2,1)} %slice.186), channel_id=1, source_target_pairs={{0,1},{1,2},{2,3},{3,0},{4,5},{5,6},{6,7},{7,4},{8,9},{9,10},{10,1... | collective-permute-start | bytes 1179656 | tf_op jit(solution)/shard_map/ppermute | solution.py:113
  216.1 2.1 collective-permute-start.3
  272.1 3.4 convolution_convert_fusion.2
  275.5 2.3 fusion
  279.2 2.1 fusion.37
  285.2 3.4 convolution_convert_fusion
  288.6 2.3 fusion.2
  292.6 2.1 fusion.31
  297.6 8.6 %all-to-all-start.7 = ((bf16[128,8,384]{2,1,0:T(8,128)(2,1)}), bf16[128,8,384]{2,1,0:T(8,128)(2,1)S(1)}, u32[]{:S(2)}, u32[]{:S(2)}) async-start(bf16[128,8,384]{2,1,0:T(8,128)(2,1)} %bitcast.155), calls=%async_computation.7 | async-start | bytes 1572864 | tf_op jit(solution)/shard_map/all_to_all | solution.py:195
  306.4 44.1 %all-to-all-done.7 = bf16[128,8,384]{2,1,0:T(8,128)(2,1)S(1)} async-done(((bf16[128,8,384]{2,1,0:T(8,128)(2,1)}), bf16[128,8,384]{2,1,0:T(8,128)(2,1)S(1)}, u32[]{:S(2)}, u32[]{:S(2)}) %all-to-all-start.7) | async-done | bytes 786464 | tf_op jit(solution)/shard_map/all_to_all | solution.py:195
  351.0 15.4 %all_to_all.48 = bf16[4,32,8,384]{3,1,2,0:T(8,128)(2,1)S(1)} all-to-all(bf16[4,32,8,384]{3,1,2,0:T(8,128)(2,1)S(1)} %copy.218), channel_id=1, replica_groups=mesh['x'=4,'z'=16,'c'=2,'tok'=4] {'x'}, dimensions={0} | all-to-all | bytes 1572864 | tf_op jit(solution)/shard_map/all_to_all | solution.py:206
  (202 shorter events, 90.7 us)
Async XLA Ops:
  0.0 76.9 %copy-start = (s32[128]{0:T(128)S(1)}, s32[128]{0:T(128)}, u32[]{:S(2)}) copy-start(s32[128]{0:T(128)} %param.12) | copy-start | bytes 1540
  5.4 31.6 %all-to-all-start.2 = ((bf16[16,48,128]{2,1,0:T(8,128)(2,1)}), bf16[16,48,128]{2,1,0:T(8,128)(2,1)S(1)}, u32[]{:S(2)}, u32[]{:S(2)}) async-start(bf16[16,48,128]{2,1,0:T(8,128)(2,1)} %broadcast_in_dim.20), calls=%async_computation.2 | async-start | bytes 393216 | tf_op jit(solution)/shard_map/all_to_all | solution.py:69
  41.0 14.1 %all-to-all-start = ((bf16[4,32,8,256]{3,2,1,0:T(8,128)(2,1)}), bf16[4,32,8,256]{3,2,1,0:T(8,128)(2,1)S(1)}, u32[]{:S(2)}, u32[]{:S(2)}) async-start(bf16[4,32,8,256]{3,2,1,0:T(8,128)(2,1)} %copy.158), calls=%async_computation | async-start | bytes 1048576 | tf_op jit(solution)/shard_map/all_to_all | solution.py:156
  55.1 16.5 %copy-start.2 = (bf16[4,32,8,256]{3,2,1,0:T(8,128)(2,1)}, bf16[4,32,8,256]{3,2,1,0:T(8,128)(2,1)S(1)}, u32[]{:S(2)}) copy-start(bf16[4,32,8,256]{3,2,1,0:T(8,128)(2,1)S(1)} %all-to-all-done) | copy-start | bytes 1572868
  71.5 4.8 %copy-start.35 = (s32[128,2]{0,1:T(2,128)S(1)}, s32[128,2]{0,1:T(2,128)}, u32[]{:S(2)}) copy-start(s32[128,2]{0,1:T(2,128)} %param.11) | copy-start | bytes 3076
  71.5 38.4 %all-to-all-start.5 = ((bf16[4,4,768,128]{3,2,1,0:T(8,128)(2,1)}), bf16[4,4,768,128]{3,2,1,0:T(8,128)(2,1)S(1)}, u32[]{:S(2)}, u32[]{:S(2)}) async-start(bf16[4,4,768,128]{3,2,1,0:T(8,128)(2,1)} %broadcast_in_dim.25), calls=%async_computation.5 | async-start | bytes 6291456 | tf_op jit(solution)/shard_map/all_to_all | solution.py:69
  78.9 5.3 %copy-start.12 = (s32[128,2]{1,0:T(8,128)}, s32[128,2]{1,0:T(8,128)S(1)}, u32[]{:S(2)}) copy-start(s32[128,2]{1,0:T(8,128)S(1)} %reshape.506) | copy-start | bytes 3076
  121.3 63.3 %all-to-all-start.1 = ((bf16[128,2,8,256]{3,2,1,0:T(8,128)(2,1)}), bf16[128,2,8,256]{3,2,1,0:T(8,128)(2,1)S(1)}, u32[]{:S(2)}, u32[]{:S(2)}) async-start(bf16[128,2,8,256]{3,2,1,0:T(8,128)(2,1)} %broadcast_select_fusion), calls=%async_computation.1 | async-start | bytes 2097152 | tf_op jit(solution)/shard_map/all_to_all | solution.py:168
  137.3 47.4 %copy-start.34 = (bf16[1024,768]{1,0:T(8,128)(2,1)}, bf16[1024,768]{1,0:T(8,128)(2,1)S(1)}, u32[]{:S(2)}) copy-start(bf16[1024,768]{1,0:T(8,128)(2,1)S(1)} %constant_dynamic-update-slice_fusion) | copy-start | bytes 4718596
  184.8 6.4 %copy-start.16 = (bf16[4,2,48,128]{3,2,1,0:T(8,128)(2,1)S(1)}, bf16[4,2,48,128]{3,2,1,0:T(8,128)(2,1)}, u32[]{:S(2)}) copy-start(bf16[4,2,48,128]{3,2,1,0:T(8,128)(2,1)} %copy.190) | copy-start | bytes 294916
  184.8 7.1 %copy-start.15 = (bf16[4,2,48,128]{3,2,0,1:T(8,128)(2,1)S(1)}, bf16[4,2,48,128]{3,2,0,1:T(8,128)(2,1)}, u32[]{:S(2)}) copy-start(bf16[4,2,48,128]{3,2,0,1:T(8,128)(2,1)} %get-tuple-element.7) | copy-start | bytes 294916
  187.2 13.0 %copy-start.10 = (bf16[2,256,768]{2,1,0:T(8,128)(2,1)}, bf16[2,256,768]{2,1,0:T(8,128)(2,1)S(1)}, u32[]{:S(2)}) copy-start(bf16[2,256,768]{2,1,0:T(8,128)(2,1)S(1)} %get-tuple-element.42) | copy-start | bytes 2359300
  187.2 19.7 %collective-permute-start = (bf16[2,256,768]{2,1,0:T(8,128)(2,1)S(1)}, bf16[2,256,768]{2,1,0:T(8,128)(2,1)S(1)}, u32[]{:S(2)}, u32[]{:S(2)}) collective-permute-start(bf16[2,256,768]{2,1,0:T(8,128)(2,1)S(1)} %get-tuple-element.42), channel_id=1, source_target_pairs={{0,1},{1,2},{2,3},{3,0},{4,5},{5,6},{6,7},{7,4},{8,9},{9,10},{10,1... | collective-permute-start | bytes 2359304 | tf_op jit(solution)/shard_map/ppermute | solution.py:111
  191.9 22.5 %collective-permute-start.1 = (bf16[2,256,768]{2,1,0:T(8,128)(2,1)S(1)}, bf16[2,256,768]{2,1,0:T(8,128)(2,1)S(1)}, u32[]{:S(2)}, u32[]{:S(2)}) collective-permute-start(bf16[2,256,768]{2,1,0:T(8,128)(2,1)S(1)} %get-tuple-element.42), channel_id=1, source_target_pairs={{0,3},{1,0},{2,1},{3,2},{4,7},{5,4},{6,5},{7,6},{8,11},{9,8},{10,9... | collective-permute-start | bytes 2359304 | tf_op jit(solution)/shard_map/ppermute | solution.py:112
  196.5 17.9 %copy-start.14 = (bf16[4,2,48,128]{3,2,0,1:T(8,128)(2,1)S(1)}, bf16[4,2,48,128]{3,2,0,1:T(8,128)(2,1)}, u32[]{:S(2)}) copy-start(bf16[4,2,48,128]{3,2,0,1:T(8,128)(2,1)} %get-tuple-element.5) | copy-start | bytes 294916
  208.6 56.1 %collective-permute-start.2 = (bf16[2,128,768]{2,1,0:T(8,128)(2,1)}, bf16[2,128,768]{2,1,0:T(8,128)(2,1)}, u32[]{:S(2)}, u32[]{:S(2)}) collective-permute-start(bf16[2,128,768]{2,1,0:T(8,128)(2,1)} %slice.186), channel_id=1, source_target_pairs={{0,1},{1,2},{2,3},{3,0},{4,5},{5,6},{6,7},{7,4},{8,9},{9,10},{10,1... | collective-permute-start | bytes 1179656 | tf_op jit(solution)/shard_map/ppermute | solution.py:113
  216.1 49.5 %collective-permute-start.3 = (bf16[2,128,768]{2,1,0:T(8,128)(2,1)}, bf16[2,128,768]{2,1,0:T(8,128)(2,1)}, u32[]{:S(2)}, u32[]{:S(2)}) collective-permute-start(bf16[2,128,768]{2,1,0:T(8,128)(2,1)} %slice.187), channel_id=1, source_target_pairs={{0,3},{1,0},{2,1},{3,2},{4,7},{5,4},{6,5},{7,6},{8,11},{9,8},{10,9... | collective-permute-start | bytes 1179656 | tf_op jit(solution)/shard_map/ppermute | solution.py:114
  255.1 6.5 %copy-start.9 = (bf16[4,2,96,128]{3,2,0,1:T(8,128)(2,1)S(1)}, bf16[4,2,96,128]{3,2,0,1:T(8,128)(2,1)}, u32[]{:S(2)}) copy-start(bf16[4,2,96,128]{3,2,0,1:T(8,128)(2,1)} %get-tuple-element.32) | copy-start | bytes 589828
  268.3 2.6 copy-start.31
  268.4 2.6 copy-start.32
  268.4 2.6 copy-start.33
  275.4 2.3 copy-start.4
  275.4 2.3 copy-start.27
  275.4 2.3 copy-start.29
  275.5 2.3 copy-start.30
  288.6 2.3 copy-start.5
  288.6 2.3 copy-start.17
  288.6 2.3 copy-start.19
  288.6 2.3 copy-start.21
  296.6 9.6 %copy-start.13 = (s32[128,2]{1,0:T(8,128)S(1)}, s32[128,2]{1,0:T(8,128)}, u32[]{:S(2)}) copy-start(s32[128,2]{1,0:T(8,128)} %copy-done.12) | copy-start | bytes 3076
  297.6 53.0 %all-to-all-start.7 = ((bf16[128,8,384]{2,1,0:T(8,128)(2,1)}), bf16[128,8,384]{2,1,0:T(8,128)(2,1)S(1)}, u32[]{:S(2)}, u32[]{:S(2)}) async-start(bf16[128,8,384]{2,1,0:T(8,128)(2,1)} %bitcast.155), calls=%async_computation.7 | async-start | bytes 1572864 | tf_op jit(solution)/shard_map/all_to_all | solution.py:195
  351.0 16.9 %copy-start.1 = (s32[128]{0:T(128)S(1)}, s32[128]{0:T(128)}, u32[]{:S(2)}) copy-start(s32[128]{0:T(128)} %param.12) | copy-start | bytes 1540
  (13 other events, 15.0 us)

commit v2 on v1

v2 whole, which is shorter than its diff:
```python
import functools

import jax
import jax.numpy as jnp
import numpy as np
from jax import lax
from jax.experimental import pallas as pl
from jax.experimental.pallas import tpu as pltpu
from jax.sharding import Mesh, PartitionSpec as P

HEADS = 6
HD = 64
LANES = 128
IMG = ("x", "z", "c")
VMEM_BYTES = 50 * 1024 * 1024

SECTIONS = (
    ("embed", 8, 6),
    ("project", 6, 9),
    ("self_out", 3, 6),
    ("query", 6, 3),
    ("keyval", 6, 6),
    ("cross_out", 3, 6),
)
PACKED = sum(rows * tiles for _, rows, tiles in SECTIONS)


def f32_dot(left, right):
    return jnp.dot(left, right, preferred_element_type=jnp.float32)


def normalize(values):
    mean_value = jnp.mean(values, axis=-1, keepdims=True)
    centred = values - mean_value
    variance = jnp.mean(centred * centred, axis=-1, keepdims=True)
    return centred * lax.rsqrt(variance + 1e-06)


def row_tables(toks, z_low, cores):
    quarter = PACKED // toks
    tiles = []
    at = 0
    for _, rows, count in SECTIONS:
        for _ in range(count):
            tiles.append((at, rows))
            at += rows
    table = np.zeros((3, toks, quarter * z_low * cores), np.int32)
    places = []
    for tok in range(toks):
        out = 0
        for start, rows in tiles:
            if start // quarter != tok:
                continue
            assert (start + rows - 1) // quarter == tok
            places.append((tok, out, rows * z_low * cores))
            for z in range(z_low):
                for core in range(cores):
                    for row in range(rows):
                        table[:, tok, out] = (start - tok * quarter + row, z, core)
                        out += 1
    return table, places


def pack(shards_in):
    pieces = []
    for shard in shards_in:
        rows, width = shard.shape
        pieces.append(
            jnp.transpose(shard.reshape(rows, width // LANES, LANES), (1, 0, 2)).reshape(-1, LANES)
        )
    return jnp.concatenate(pieces, axis=0)


def shifted(value, axis, pairs):
    return lax.ppermute(value, axis, pairs)


def cycle(count, shift):
    return [(i, (i + shift) % count) for i in range(count)]


def gather_weights(shards_in):
    toks, cores, depth = lax.axis_size("tok"), lax.axis_size("c"), lax.axis_size("z")
    groups = lax.axis_size("x")
    tok, core, z = lax.axis_index("tok"), lax.axis_index("c"), lax.axis_index("z")
    quarter = PACKED // toks
    z_low = depth // cores
    step = 4
    table, places = row_tables(toks, z_low, cores)
    mine = lax.dynamic_slice_in_dim(pack(shards_in), tok * quarter, quarter, axis=0)

    far = [mine] + [
        lax.ppermute(mine, "z", cycle(depth, step * s)) for s in range(1, depth // step)
    ]
    far = jnp.stack(far)
    near = [far] + [
        lax.ppermute(
            far, "z", [(i, i // step * step + (i + t) % step) for i in range(depth)]
        )
        for t in range(1, step)
    ]
    near = jnp.stack(near)
    both = jnp.stack([near, lax.ppermute(near, "c", cycle(cores, 1))])

    rows, low, from_core = lax.dynamic_index_in_dim(jnp.asarray(table), tok, axis=1, keepdims=False)
    from_z = core * z_low + low
    high_step = (z // step - from_z // step) % (depth // step)
    low_step = (z - from_z) % step
    order = (((from_core - core) % cores * step + low_step) * (depth // step) + high_step) * quarter + rows
    count = cores * depth * quarter
    mover = (order[:, None] == jnp.arange(count, dtype=jnp.int32)[None, :]).astype(jnp.bfloat16)
    ordered = f32_dot(mover, both.reshape(count, LANES)).astype(jnp.bfloat16)

    along_x = jnp.stack(
        [ordered] + [lax.ppermute(ordered, "x", cycle(groups, s)) for s in range(1, groups)]
    )
    own, left, right, far_low, far_high = round_ring(along_x, 0)
    along_y = jnp.stack([own, left, jnp.concatenate([far_low, far_high], axis=0), right])
    return along_y, lax.ppermute(along_y, "c", cycle(cores, 1)), places


def round_ring(own, axis):
    count = lax.axis_size("tok")
    half = own.shape[axis] // 2
    from_left = lax.ppermute(own, "tok", cycle(count, 1))
    from_right = lax.ppermute(own, "tok", cycle(count, -1))
    low = lax.slice_in_dim(from_left, 0, half, axis=axis)
    high = lax.slice_in_dim(from_right, half, 2 * half, axis=axis)
    far_low = lax.ppermute(low, "tok", cycle(count, 1))
    far_high = lax.ppermute(high, "tok", cycle(count, -1))
    return own, from_left, from_right, far_low, far_high


def assemble_kernel(places, at_ref, mine_ref, other_ref, *rest):
    outs, sems = rest[:-1], rest[-1]
    tok, x, core = at_ref[0], at_ref[1], at_ref[2]
    toks, groups = mine_ref.shape[0], mine_ref.shape[1]
    next_tile = 0
    for section, (_, _, tiles) in enumerate(SECTIONS):
        out = outs[section]
        for tile, (place_tok, start, rows) in enumerate(places[next_tile : next_tile + tiles]):
            tok_step = lax.rem(tok - place_tok + toks, toks)
            for x_step in range(groups):
                from_x = lax.rem(x - x_step + groups, groups)
                for source, half in ((mine_ref, core), (other_ref, 1 - core)):
                    pltpu.make_async_copy(
                        source.at[tok_step, x_step, pl.ds(start, rows)],
                        out.at[from_x, half, :, pl.ds(tile * LANES, LANES)],
                        sems.at[section],
                    ).start()
        next_tile += tiles
    for section in range(len(SECTIONS)):
        pltpu.make_async_copy(outs[section], outs[section], sems.at[section]).wait()


def assemble(mine, other, places):
    groups = mine.shape[1]
    cores = lax.axis_size("c")
    place = jnp.stack(
        [lax.axis_index("tok"), lax.axis_index("x"), lax.axis_index("c")]
    ).astype(jnp.int32)
    shapes = []
    next_tile = 0
    for _, _, tiles in SECTIONS:
        rows = places[next_tile][2]
        shapes.append(jax.ShapeDtypeStruct((groups, cores, rows, tiles * LANES), jnp.bfloat16))
        next_tile += tiles
    full = pl.pallas_call(
        functools.partial(assemble_kernel, places),
        out_shape=shapes,
        in_specs=[pl.BlockSpec(memory_space=pltpu.SMEM)] + [pl.BlockSpec(memory_space=pl.ANY)] * 2,
        out_specs=[pl.BlockSpec(memory_space=pl.ANY)] * len(shapes),
        scratch_shapes=[pltpu.SemaphoreType.DMA((len(SECTIONS),))],
        cost_estimate=pl.CostEstimate(
            flops=0, bytes_accessed=4 * mine.size * 2, transcendentals=0
        ),
        name="assemble",
    )(place, mine, other)
    return [matrix.reshape(-1, matrix.shape[-1]) for matrix in full]


def embed_kernel(arrived_ref, matrix_ref, out_ref):
    groups, blocks, images, block_rows, part = arrived_ref.shape
    for image in range(images):
        total = None
        for group in range(groups):
            rows = arrived_ref[group, :, image].astype(jnp.float32)
            rows = rows.reshape(blocks * block_rows, part).astype(jnp.bfloat16)
            product = f32_dot(rows, matrix_ref[group * part : (group + 1) * part, :])
            total = product if total is None else total + product
        out_ref[image] = total.astype(jnp.bfloat16)


def embed(arrived, matrix):
    groups, blocks, images, block_rows, part = arrived.shape
    rows, width = blocks * block_rows, matrix.shape[1]
    return pl.pallas_call(
        embed_kernel,
        out_shape=jax.ShapeDtypeStruct((images, rows, width), jnp.bfloat16),
        compiler_params=pltpu.CompilerParams(vmem_limit_bytes=VMEM_BYTES),
        cost_estimate=pl.CostEstimate(
            flops=2 * images * rows * matrix.size,
            bytes_accessed=2 * (arrived.size + matrix.size + images * rows * width),
            transcendentals=0,
        ),
        name="embed",
    )(arrived, matrix)


def attend(queries, key_ref, value_ref, first_key, first_value, chunk):
    rows = queries.shape[0]
    others = key_ref.shape[0]
    low_half = lax.broadcasted_iota(jnp.int32, (1, LANES), 1) < HD
    done = []
    for pair in range(HEADS * HD // LANES):
        query = queries[:, pair * LANES : (pair + 1) * LANES]
        blank = jnp.zeros_like(query)
        low_query = jnp.where(low_half, query, blank)
        high_query = jnp.where(low_half, blank, query)
        low_total = jnp.zeros((rows, LANES), jnp.float32)
        high_total = jnp.zeros((rows, LANES), jnp.float32)
        for start in range(0, others, chunk):
            at = slice(start, start + chunk)
            keys = key_ref[at, first_key + pair * LANES : first_key + (pair + 1) * LANES]
            values = value_ref[at, first_value + pair * LANES : first_value + (pair + 1) * LANES]
            ones = jnp.ones_like(values)
            across = (((1,), (1,)), ((), ()))
            scores = lax.dot_general(low_query, keys, across, preferred_element_type=jnp.float32)
            weights = jnp.exp(scores).astype(jnp.bfloat16)
            low_total += f32_dot(weights, jnp.where(low_half, values, ones))
            scores = lax.dot_general(high_query, keys, across, preferred_element_type=jnp.float32)
            weights = jnp.exp(scores).astype(jnp.bfloat16)
            high_total += f32_dot(weights, jnp.where(low_half, ones, values))
        numer = jnp.where(low_half, low_total, high_total)
        denom = pltpu.roll(jnp.where(low_half, high_total, low_total), HD, 1)
        done.append((numer / denom).astype(jnp.bfloat16))
    return jnp.concatenate(done, axis=1)


def scaled(queries):
    return (queries.astype(jnp.bfloat16).astype(jnp.float32) * HD**-0.5).astype(jnp.bfloat16)


def self_kernel(
    own_ref, left_ref, right_ref, low_ref, high_ref,
    project_ref, output_ref, query_ref, keyval_ref,
    after_ref, second_ref, cross_ref,
    keyval_scratch,
):
    width = output_ref.shape[0]
    own = own_ref[0].astype(jnp.float32)
    rows = own.shape[0]
    normed = normalize(own).astype(jnp.bfloat16)
    queries = scaled(f32_dot(normed, project_ref[:, :width]))
    at = 0
    for ref in (own_ref, left_ref, right_ref, low_ref, high_ref):
        if at > 0:
            normed = normalize(ref[0].astype(jnp.float32)).astype(jnp.bfloat16)
        here = slice(at, at + normed.shape[0])
        keyval_scratch[here] = f32_dot(normed, project_ref[:, width:]).astype(jnp.bfloat16)
        cross_ref[0, here] = f32_dot(normed, keyval_ref[...]).astype(jnp.bfloat16)
        at += normed.shape[0]
    attended = attend(queries, keyval_scratch, keyval_scratch, 0, width, 256)
    after = own + f32_dot(attended, output_ref[...])
    after_ref[0] = after
    second = normalize(after).astype(jnp.bfloat16)
    second_ref[0] = scaled(f32_dot(second, query_ref[...]))


def self_block(pieces, project, output, query, keyval):
    own = pieces[0]
    images, rows, model = own.shape
    width = output.shape[0]
    everyone = sum(piece.shape[1] for piece in pieces)

    def one(shape):
        return pl.BlockSpec((1,) + shape[1:], lambda i: (i, 0, 0))

    def whole(matrix):
        return pl.BlockSpec(matrix.shape, lambda i: (0, 0))

    matrices = (project, output, query, keyval)
    shapes = [
        jax.ShapeDtypeStruct((images, rows, model), jnp.float32),
        jax.ShapeDtypeStruct((images, rows, width), jnp.bfloat16),
        jax.ShapeDtypeStruct((images, everyone, 2 * width), jnp.bfloat16),
    ]
    flops = 2 * images * (
        everyone * model * 4 * width + rows * model * 3 * width + 2 * rows * everyone * width
    )
    return pl.pallas_call(
        self_kernel,
        grid=(images,),
        out_shape=shapes,
        in_specs=[one(piece.shape) for piece in pieces] + [whole(matrix) for matrix in matrices],
        out_specs=[one(shape.shape) for shape in shapes],
        scratch_shapes=[pltpu.VMEM((everyone, 2 * width), jnp.bfloat16)],
        compiler_params=pltpu.CompilerParams(vmem_limit_bytes=VMEM_BYTES),
        cost_estimate=pl.CostEstimate(
            flops=flops,
            bytes_accessed=2 * sum(matrix.size for matrix in matrices) + 8 * own.size,
            transcendentals=images * HEADS * rows * everyone,
        ),
        name="self_block",
    )(*pieces, *matrices)


def cross_kernel(after_ref, query_ref, keyval_ref, output_ref, out_ref):
    width, model = output_ref.shape
    halves, blocks, block_rows, part = out_ref.shape[1:]
    keyval = keyval_ref.at[0]
    attended = attend(query_ref[0], keyval, keyval, 0, width, 256)
    mixed = after_ref[0] + f32_dot(attended, output_ref[...])
    for half in range(halves):
        columns = mixed[:, half * part : (half + 1) * part]
        out_ref[0, half] = columns.reshape(blocks, block_rows, part).astype(jnp.bfloat16)


def cross_block(after, query, keyval, output, halves, block_rows):
    images, rows, model = after.shape
    width = output.shape[0]
    everyone = keyval.shape[1]
    shape = (images, halves, rows // block_rows, block_rows, model // halves)
    return pl.pallas_call(
        cross_kernel,
        grid=(images,),
        out_shape=jax.ShapeDtypeStruct(shape, jnp.bfloat16),
        in_specs=[
            pl.BlockSpec((1, rows, model), lambda i: (i, 0, 0)),
            pl.BlockSpec((1, rows, width), lambda i: (i, 0, 0)),
            pl.BlockSpec((1, everyone, 2 * width), lambda i: (images - 1 - i, 0, 0)),
            pl.BlockSpec(output.shape, lambda i: (0, 0)),
        ],
        out_specs=pl.BlockSpec((1,) + shape[1:], lambda i: (i, 0, 0, 0, 0)),
        compiler_params=pltpu.CompilerParams(vmem_limit_bytes=VMEM_BYTES),
        cost_estimate=pl.CostEstimate(
            flops=2 * images * (2 * rows * everyone * width + rows * model * width),
            bytes_accessed=4 * after.size + 2 * (query.size + keyval.size + output.size + after.size),
            transcendentals=images * HEADS * rows * everyone,
        ),
        name="cross_block",
    )(after, query, keyval, output)


def shards(tokens, pair_list, owner_base, *weight_shards):
    groups = lax.axis_size("x")
    row_devices = lax.axis_size("z") * lax.axis_size("c")
    devices = groups * row_devices
    column = lax.axis_index("z") * lax.axis_size("c") + lax.axis_index("c")
    spread, block_rows, encoder = tokens.shape[1], tokens.shape[3], tokens.shape[4]
    held = tokens.reshape(spread, block_rows, encoder)
    part = encoder // groups

    parted = jnp.stack([held[:, :, x * part : (x + 1) * part] for x in range(groups)])
    pieces = lax.all_to_all(parted, "x", 0, 0, tiled=True).reshape(devices, block_rows, part)

    bases = owner_base[pair_list]
    slot = (column - bases) % spread
    source = ((bases + slot - column) // row_devices) % groups
    place = source * spread + slot
    outgoing = jnp.take(pieces, place.reshape(-1), axis=0, mode="clip").reshape(
        devices, 2, block_rows, part
    )
    arrived = lax.all_to_all(outgoing, IMG, 0, 0, tiled=True)
    arrived = arrived.reshape(groups, row_devices, 2, block_rows, part)

    full = assemble(*gather_weights(weight_shards))
    embed_full, project_full, self_out_full, query_full, keyval_full, cross_out_full = full
    model_width = embed_full.shape[1]

    embedded = embed(arrived, embed_full)
    after_self, cross_queries, cross_keyval = self_block(
        round_ring(embedded, 1), project_full, self_out_full, query_full, keyval_full
    )

    halves = groups // 2
    backward = cross_block(
        after_self, cross_queries, cross_keyval, cross_out_full, halves, block_rows
    ).reshape(devices, block_rows, model_width // halves)
    returned = lax.all_to_all(backward, IMG, 0, 0, tiled=True)
    my_half = lax.axis_index("x") // halves
    my_place = lax.dynamic_index_in_dim(place, my_half, axis=1, keepdims=False)
    selector = (
        my_place[None, :] == jnp.arange(devices, dtype=jnp.int32)[:, None]
    ).astype(jnp.bfloat16)
    partial = jnp.einsum(
        "ge,ebd->gbd", selector, returned, preferred_element_type=jnp.float32
    ).astype(jnp.bfloat16)
    home = lax.all_to_all(
        partial.reshape(groups, spread, block_rows, model_width // halves), "x", 0, 0, tiled=True
    )
    home = home.reshape(2, halves, spread, block_rows, model_width // halves)
    total = home[0].astype(jnp.float32) + home[1].astype(jnp.float32)
    summed = jnp.concatenate([total[half] for half in range(halves)], axis=-1)
    return summed.astype(jnp.bfloat16).reshape(1, spread, 1, block_rows, model_width)


def solution(mesh):
    chips = Mesh(mesh.devices.reshape(4, 16, 2, 4), ("x", "z", "c", "tok"))
    rows = P(IMG, None)
    tokens = P(IMG, None, "tok", None, None)
    return jax.shard_map(
        shards,
        mesh=chips,
        in_specs=(tokens, P(), P()) + (rows,) * 6,
        out_specs=tokens,
        check_vma=False,
    )
```

time: 372 us -> 454 us (1.22)
  Pallas kernels: 0 us -> 217 us
  local copies, waits for them, and re-layouts: 91.6 us -> 12.3 us
  waiting for transfers between devices: 146 us -> 94.5 us
  starting transfers between devices: 53.7 us -> 105 us
  blocking collectives: 43.3 us -> 15.4 us
  matrix products: 26.5 us -> 1.27 us
    pallas_call x0 -> x4, Pallas kernels: none -> 217 us  [the longest x1 192 us: assemble(): pl.pallas_call(functools.partial(assemble_kernel, places), out_shape=shap...]
    ppermute x4 -> x19, starting transfers between devices: 13.2 us -> 74.3 us  [the longest x3 25.5 us: gather_weights(): lax.ppermute(mine, 'z', cycle(depth, step * s))]
    all_to_all x1, waiting for transfers between devices: 47.3 us -> 0.01 us  [shards(): arrived = lax.all_to_all(outgoing, IMG, 0, 0, tiled=True)]
    ppermute x4 -> x19, waiting for transfers between devices: 6.62 us -> 50.4 us  [the longest x2 16 us: round_ring(): from_left = lax.ppermute(own, 'tok', cycle(count, 1))]
    all_to_all x2 -> x0, waiting for transfers between devices: 39.9 us -> none  [spread_to(): lax.all_to_all(jnp.broadcast_to(value[None], (count,) + value.shape), axi...]
    unnamed x103 -> x18, local copies, waits for them, and re-layouts: 31.4 us -> 2.84 us
    all_to_all x3 -> x0, blocking collectives: 28 us -> none  [the longest x2 24.1 us: spread_to(): lax.all_to_all(jnp.broadcast_to(value[None], (count,) + value.shape), axi...]
    dot_general x14 -> x1, matrix products: 26.1 us -> 0.91 us  [f32_dot(): return jnp.dot(left, right, preferred_element_type=jnp.float32)]
  transfers between devices with their start and end apart: 9 -> 22, of which waited for: 6 -> 12; matrix products, arithmetic and copies ran while one was open for 21% -> 2% of each run, Pallas kernels for 0% -> 43%
where the time goes in v2:
time: 454 us; the launch traced here: 452 us
  Pallas kernels  217 us (48%)
  starting transfers between devices  105 us (23%)
  waiting for transfers between devices  94.5 us (21%)
  blocking collectives  15.4 us (3%)
  local copies, waits for them, and re-layouts  12.3 us (3%)
  other arithmetic  6.35 us (1%)
    pallas_call x1, Pallas kernels, assemble(): pl.pallas_call(functools.partial(assemble_kernel, places), out_shape=shap...  192 us
    all_to_all x1, waiting for transfers between devices, shards(): returned = lax.all_to_all(backward, IMG, 0, 0, tiled=True)  44.1 us
    ppermute x3, starting transfers between devices, gather_weights(): lax.ppermute(mine, 'z', cycle(depth, step * s))  25.5 us
    all_to_all x1, starting transfers between devices, shards(): returned = lax.all_to_all(backward, IMG, 0, 0, tiled=True)  16.7 us
    ppermute x2, waiting for transfers between devices, round_ring(): from_left = lax.ppermute(own, 'tok', cycle(count, 1))  16 us
    pallas_call x1, Pallas kernels, self_block(): pl.pallas_call(self_kernel, grid=(images,), out_shape=shapes, in_specs=[o...  15.8 us
    all_to_all x1, blocking collectives, shards(): lax.all_to_all(partial.reshape(groups, spread, block_rows, model_width //...  15.4 us
    ppermute x2, waiting for transfers between devices, round_ring(): far_low = lax.ppermute(low, 'tok', cycle(count, 1))  12.4 us
  transfers between devices with their start and end apart: 22, of which 12 were waited for; matrix products, arithmetic and copies ran while one was open for 2% of the time, Pallas kernels for 43%

profile of v2, /device:TPU:24, one launch (start us, length us, event | category | flops | bytes accessed | tf_op | source)
XLA Modules:
  0.0 452.3 jit_solution(12581441939730705389)
XLA Ops:
  4.8 9.1 %collective-permute-start = (bf16[48,128]{1,0:T(8,128)(2,1)S(1)}, bf16[48,128]{1,0:T(8,128)(2,1)S(1)}, u32[]{:S(2)}, u32[]{:S(2)}) collective-permute-start(bf16[48,128]{1,0:T(8,128)(2,1)S(1)} %constant_dynamic-slice_fusion), channel_id=1, source_target_pairs={{0,32},{8,40},{16,48},{24,56},{32,64},{40,72},{48,80},{56,88},{64,... | collective-permute-start | bytes 36872 | tf_op jit(solution)/shard_map/ppermute | solution.py:93
  13.9 10.9 %collective-permute-start.1 = (bf16[48,128]{1,0:T(8,128)(2,1)S(1)}, bf16[48,128]{1,0:T(8,128)(2,1)S(1)}, u32[]{:S(2)}, u32[]{:S(2)}) collective-permute-start(bf16[48,128]{1,0:T(8,128)(2,1)S(1)} %constant_dynamic-slice_fusion), channel_id=1, source_target_pairs={{0,64},{8,72},{16,80},{24,88},{32,96},{40,104},{48,112},{56,120},{... | collective-permute-start | bytes 36872 | tf_op jit(solution)/shard_map/ppermute | solution.py:93
  24.8 5.5 %collective-permute-start.2 = (bf16[48,128]{1,0:T(8,128)(2,1)S(1)}, bf16[48,128]{1,0:T(8,128)(2,1)S(1)}, u32[]{:S(2)}, u32[]{:S(2)}) collective-permute-start(bf16[48,128]{1,0:T(8,128)(2,1)S(1)} %constant_dynamic-slice_fusion), channel_id=1, source_target_pairs={{0,96},{8,104},{16,112},{24,120},{32,0},{40,8},{48,16},{56,24},{64... | collective-permute-start | bytes 36872 | tf_op jit(solution)/shard_map/ppermute | solution.py:93
  30.3 4.0 collective-permute-done.2
  34.3 2.9 collective-permute-start.3
  37.3 3.4 collective-permute-start.4
  40.7 3.8 collective-permute-start.5
  46.7 1.9 collective-permute-start.6
  51.0 3.4 collective-permute-start.7
  54.4 4.6 %collective-permute-start.8 = (bf16[768,128]{1,0:T(8,128)(2,1)S(1)}, bf16[768,128]{1,0:T(8,128)(2,1)S(1)}, u32[]{:S(2)}, u32[]{:S(2)}) collective-permute-start(bf16[768,128]{1,0:T(8,128)(2,1)S(1)} %fusion.2), channel_id=1, source_target_pairs={{0,256},{128,384},{256,0},{384,128},{1,257},{129,385},{257,1},{385... | collective-permute-start | bytes 589832 | tf_op jit(solution)/shard_map/ppermute | solution.py:115
  59.0 3.3 collective-permute-start.9
  63.3 3.5 all-to-all-start
  68.8 2.1 collective-permute-start.10
  70.9 3.7 collective-permute-start.12
  78.6 10.4 %all-to-all-start.1 = ((bf16[128,2,8,256]{3,2,1,0:T(8,128)(2,1)}), bf16[128,2,8,256]{3,2,1,0:T(8,128)(2,1)S(1)}, u32[]{:S(2)}, u32[]{:S(2)}) async-start(bf16[128,2,8,256]{3,2,1,0:T(8,128)(2,1)} %bitcast.10), calls=%async_computation.1 | async-start | bytes 2097152 | tf_op jit(solution)/shard_map/all_to_all | solution.py:364
  89.4 3.4 collective-permute-start.11
  92.9 2.4 collective-permute-start.13
  95.3 6.2 %collective-permute-done.11 = bf16[2,768,128]{2,1,0:T(8,128)(2,1)S(1)} collective-permute-done((bf16[2,768,128]{2,1,0:T(8,128)(2,1)S(1)}, bf16[2,768,128]{2,1,0:T(8,128)(2,1)S(1)}, u32[]{:S(2)}, u32[]{:S(2)}) %collective-permute-start.11) | collective-permute-done | bytes 393248 | tf_op jit(solution)/shard_map/ppermute | solution.py:129
  101.6 4.3 collective-permute-done.13
  110.4 5.3 %collective-permute-done.14.other_ref = bf16[4,4,768,128]{3,2,1,0:T(8,128)(2,1)} collective-permute-done((bf16[4,4,768,128]{3,2,1,0:T(8,128)(2,1)}, bf16[4,4,768,128]{3,2,1,0:T(8,128)(2,1)}, u32[]{:S(2)}, u32[]{:S(2)}) %collective-permute-start.14) | collective-permute-done | bytes 3145760 | tf_op jit(solution)/shard_map/ppermute | solution.py:119
  115.7 192.5 %assemble.1 = (bf16[4,2,128,768]{3,2,1,0:T(8,128)(2,1)}, bf16[4,2,96,1152]{3,2,1,0:T(8,128)(2,1)}, bf16[4,2,48,768]{3,2,1,0:T(8,128)(2,1)}, bf16[4,2,96,384]{3,2...) custom-call(s32[3]{0:T(128)} %pad_add_fusion.at_ref, ...), custom_call_target="tpu_custom_call" | custom-call | bytes 12582912 | tf_op jit(solution)/shard_map/assemble/pallas_call | solution.py:168
  312.5 3.9 collective-permute-start.16
  316.5 15.6 %collective-permute-done.15.left_ref = bf16[2,256,768]{2,1,0:T(8,128)(2,1)S(1)} collective-permute-done((bf16[2,256,768]{2,1,0:T(8,128)(2,1)S(1)}, bf16[2,256,768]{2,1,0:T(8,128)(2,1)S(1)}, u32[]{:S(2)}, u32[]{:S(2)}) %collective-permute-start.15) | collective-permute-done | bytes 786464 | tf_op jit(solution)/shard_map/ppermute | solution.py:125
  332.1 3.4 collective-permute-start.17
  335.6 2.6 collective-permute-start.18
  338.2 6.1 %collective-permute-done.17.low_ref = bf16[2,128,768]{2,1,0:T(8,128)(2,1)S(1)} collective-permute-done((bf16[2,128,768]{2,1,0:T(8,128)(2,1)S(1)}, bf16[2,128,768]{2,1,0:T(8,128)(2,1)S(1)}, u32[]{:S(2)}, u32[]{:S(2)}) %collective-permute-start.17) | collective-permute-done | bytes 393248 | tf_op jit(solution)/shard_map/ppermute | solution.py:129
  344.3 4.7 %collective-permute-done.18.high_ref = bf16[2,128,768]{2,1,0:T(8,128)(2,1)S(1)} collective-permute-done((bf16[2,128,768]{2,1,0:T(8,128)(2,1)S(1)}, bf16[2,128,768]{2,1,0:T(8,128)(2,1)S(1)}, u32[]{:S(2)}, u32[]{:S(2)}) %collective-permute-start.18) | collective-permute-done | bytes 393248 | tf_op jit(solution)/shard_map/ppermute | solution.py:130
  349.1 15.8 %self_block.1 = (f32[2,256,768]{2,1,0:T(8,128)}, bf16[2,256,384]{2,1,0:T(8,128)(2,1)S(1)}, bf16[2,1024,768]{2,1,0:T(8,128)(2,1)}) custom-call(bf16[2,256,768]{2,1,0:T(8,128)(2,1)S(1)} %embed.1.own_ref, bf16[2,256,768]{2,1,0:T(8,128)(2,1)S(1)} %collective-permute-done.15.left_ref, bf16[2,256,768]{2,1,0:T(8,128)(2,1)} %copy-done.7, ...), custom_call_target="tpu_custom_call" | custom-call | flops 6543114240 | bytes 7274496 | tf_op jit(solution)/shard_map/self_block/pallas_call | solution.py:291
  366.3 7.8 %cross_block.1 = bf16[2,2,32,8,384]{4,3,2,1,0:T(8,128)(2,1)} custom-call(f32[2,256,768]{2,1,0:T(8,128)S(1)} %copy-done.2, bf16[2,256,384]{2,1,0:T(8,128)(2,1)S(1)} %get-tuple-element.20.query_ref, bf16[2,1024,768]{2,1,0:T(8,128)(2,1)} %get-tuple-element.21.keyval_ref, bf16[384,768]{1,0:T(8,128)(2,1)S(1)} %bitcast.83), custom_call_target="tpu_custom_call" | custom-call | flops 1107296256 | bytes 6488064 | tf_op jit(solution)/shard_map/cross_block/pallas_call | solution.py:324
  374.1 16.7 %all-to-all-start.2 = ((bf16[128,8,384]{2,1,0:T(8,128)(2,1)}), bf16[128,8,384]{2,1,0:T(8,128)(2,1)S(1)}, u32[]{:S(2)}, u32[]{:S(2)}) async-start(bf16[128,8,384]{2,1,0:T(8,128)(2,1)} %bitcast.53), calls=%async_computation.2 | async-start | bytes 1572864 | tf_op jit(solution)/shard_map/all_to_all | solution.py:380
  391.1 44.1 %all-to-all-done.2 = bf16[128,8,384]{2,1,0:T(8,128)(2,1)S(1)} async-done(((bf16[128,8,384]{2,1,0:T(8,128)(2,1)}), bf16[128,8,384]{2,1,0:T(8,128)(2,1)S(1)}, u32[]{:S(2)}, u32[]{:S(2)}) %all-to-all-start.2) | async-done | bytes 786464 | tf_op jit(solution)/shard_map/all_to_all | solution.py:380
  436.0 15.4 %all_to_all.20 = bf16[4,32,8,384]{3,2,1,0:T(8,128)(2,1)S(1)} all-to-all(bf16[4,32,8,384]{3,2,1,0:T(8,128)(2,1)S(1)} %copy.58), channel_id=1, replica_groups=mesh['x'=4,'z'=16,'c'=2,'tok'=4] {'x'}, dimensions={0} | all-to-all | bytes 1572864 | tf_op jit(solution)/shard_map/all_to_all | solution.py:389
  (76 shorter events, 28.7 us)
Async XLA Ops:
  0.0 74.9 %copy-start = (s32[128]{0:T(128)S(1)}, s32[128]{0:T(128)}, u32[]{:S(2)}) copy-start(s32[128]{0:T(128)} %param.12) | copy-start | bytes 1540
  0.0 62.4 %copy-start.6 = (bf16[1,32,1,8,1024]{4,3,2,1,0:T(8,128)(2,1)S(1)}, bf16[1,32,1,8,1024]{4,3,2,1,0:T(8,128)(2,1)}, u32[]{:S(2)}) copy-start(bf16[1,32,1,8,1024]{4,3,2,1,0:T(8,128)(2,1)} %param.10) | copy-start | bytes 1572868
  4.8 25.5 %collective-permute-start = (bf16[48,128]{1,0:T(8,128)(2,1)S(1)}, bf16[48,128]{1,0:T(8,128)(2,1)S(1)}, u32[]{:S(2)}, u32[]{:S(2)}) collective-permute-start(bf16[48,128]{1,0:T(8,128)(2,1)S(1)} %constant_dynamic-slice_fusion), channel_id=1, source_target_pairs={{0,32},{8,40},{16,48},{24,56},{32,64},{40,72},{48,80},{56,88},{64,... | collective-permute-start | bytes 36872 | tf_op jit(solution)/shard_map/ppermute | solution.py:93
  13.9 16.4 %collective-permute-start.1 = (bf16[48,128]{1,0:T(8,128)(2,1)S(1)}, bf16[48,128]{1,0:T(8,128)(2,1)S(1)}, u32[]{:S(2)}, u32[]{:S(2)}) collective-permute-start(bf16[48,128]{1,0:T(8,128)(2,1)S(1)} %constant_dynamic-slice_fusion), channel_id=1, source_target_pairs={{0,64},{8,72},{16,80},{24,88},{32,96},{40,104},{48,112},{56,120},{... | collective-permute-start | bytes 36872 | tf_op jit(solution)/shard_map/ppermute | solution.py:93
  24.8 9.5 %collective-permute-start.2 = (bf16[48,128]{1,0:T(8,128)(2,1)S(1)}, bf16[48,128]{1,0:T(8,128)(2,1)S(1)}, u32[]{:S(2)}, u32[]{:S(2)}) collective-permute-start(bf16[48,128]{1,0:T(8,128)(2,1)S(1)} %constant_dynamic-slice_fusion), channel_id=1, source_target_pairs={{0,96},{8,104},{16,112},{24,120},{32,0},{40,8},{48,16},{56,24},{64... | collective-permute-start | bytes 36872 | tf_op jit(solution)/shard_map/ppermute | solution.py:93
  34.3 11.0 %collective-permute-start.3 = (bf16[4,48,128]{2,1,0:T(8,128)(2,1)S(1)}, bf16[4,48,128]{2,1,0:T(8,128)(2,1)S(1)}, u32[]{:S(2)}, u32[]{:S(2)}) collective-permute-start(bf16[4,48,128]{2,1,0:T(8,128)(2,1)S(1)} %get-tuple-element.37), channel_id=1, source_target_pairs={{0,8},{8,16},{16,24},{24,0},{32,40},{40,48},{48,56},{56,32},{64,72... | collective-permute-start | bytes 147464 | tf_op jit(solution)/shard_map/ppermute | solution.py:97
  37.3 8.0 %collective-permute-start.4 = (bf16[4,48,128]{2,1,0:T(8,128)(2,1)S(1)}, bf16[4,48,128]{2,1,0:T(8,128)(2,1)S(1)}, u32[]{:S(2)}, u32[]{:S(2)}) collective-permute-start(bf16[4,48,128]{2,1,0:T(8,128)(2,1)S(1)} %get-tuple-element.37), channel_id=1, source_target_pairs={{0,16},{8,24},{16,0},{24,8},{32,48},{40,56},{48,32},{56,40},{64,80... | collective-permute-start | bytes 147464 | tf_op jit(solution)/shard_map/ppermute | solution.py:97
  40.7 6.0 %collective-permute-start.5 = (bf16[4,48,128]{2,1,0:T(8,128)(2,1)S(1)}, bf16[4,48,128]{2,1,0:T(8,128)(2,1)S(1)}, u32[]{:S(2)}, u32[]{:S(2)}) collective-permute-start(bf16[4,48,128]{2,1,0:T(8,128)(2,1)S(1)} %get-tuple-element.37), channel_id=1, source_target_pairs={{0,24},{8,0},{16,8},{24,16},{32,56},{40,32},{48,40},{56,48},{64,88... | collective-permute-start | bytes 147464 | tf_op jit(solution)/shard_map/ppermute | solution.py:97
  46.7 3.3 collective-permute-start.6
  51.0 23.7 %copy-start.8 = (s32[128,2]{0,1:T(2,128)S(1)}, s32[128,2]{0,1:T(2,128)}, u32[]{:S(2)}) copy-start(s32[128,2]{0,1:T(2,128)} %param.11) | copy-start | bytes 3076
  51.0 15.8 %collective-permute-start.7 = (bf16[768,128]{1,0:T(8,128)(2,1)S(1)}, bf16[768,128]{1,0:T(8,128)(2,1)S(1)}, u32[]{:S(2)}, u32[]{:S(2)}) collective-permute-start(bf16[768,128]{1,0:T(8,128)(2,1)S(1)} %fusion.2), channel_id=1, source_target_pairs={{0,128},{128,256},{256,384},{384,0},{1,129},{129,257},{257,385},{3... | collective-permute-start | bytes 589832 | tf_op jit(solution)/shard_map/ppermute | solution.py:115
  54.4 12.4 %collective-permute-start.8 = (bf16[768,128]{1,0:T(8,128)(2,1)S(1)}, bf16[768,128]{1,0:T(8,128)(2,1)S(1)}, u32[]{:S(2)}, u32[]{:S(2)}) collective-permute-start(bf16[768,128]{1,0:T(8,128)(2,1)S(1)} %fusion.2), channel_id=1, source_target_pairs={{0,256},{128,384},{256,0},{384,128},{1,257},{129,385},{257,1},{385... | collective-permute-start | bytes 589832 | tf_op jit(solution)/shard_map/ppermute | solution.py:115
  59.0 8.7 %collective-permute-start.9 = (bf16[768,128]{1,0:T(8,128)(2,1)S(1)}, bf16[768,128]{1,0:T(8,128)(2,1)S(1)}, u32[]{:S(2)}, u32[]{:S(2)}) collective-permute-start(bf16[768,128]{1,0:T(8,128)(2,1)S(1)} %fusion.2), channel_id=1, source_target_pairs={{0,384},{128,0},{256,128},{384,256},{1,385},{129,1},{257,129},{385... | collective-permute-start | bytes 589832 | tf_op jit(solution)/shard_map/ppermute | solution.py:115
  63.3 13.5 %all-to-all-start = ((bf16[4,32,8,256]{3,2,1,0:T(8,128)(2,1)}), bf16[4,32,8,256]{3,2,1,0:T(8,128)(2,1)S(1)}, u32[]{:S(2)}, u32[]{:S(2)}) async-start(bf16[4,32,8,256]{3,2,1,0:T(8,128)(2,1)} %pad_maximum_fusion.2), calls=%async_computation | async-start | bytes 1048576 | tf_op jit(solution)/shard_map/all_to_all | solution.py:355
  68.8 20.6 %collective-permute-start.10 = (bf16[4,768,128]{2,1,0:T(8,128)(2,1)}, bf16[4,768,128]{2,1,0:T(8,128)(2,1)S(1)}, u32[]{:S(2)}, u32[]{:S(2)}) collective-permute-start(bf16[4,768,128]{2,1,0:T(8,128)(2,1)} %get-tuple-element.27), channel_id=1, source_target_pairs={{0,1},{1,2},{2,3},{3,0},{4,5},{5,6},{6,7},{7,4},{8,9},{9,10},{10,1... | collective-permute-start | bytes 2359304 | tf_op jit(solution)/shard_map/ppermute | solution.py:125
  70.9 22.0 %collective-permute-start.12 = (bf16[4,768,128]{2,1,0:T(8,128)(2,1)}, bf16[4,768,128]{2,1,0:T(8,128)(2,1)S(1)}, u32[]{:S(2)}, u32[]{:S(2)}) collective-permute-start(bf16[4,768,128]{2,1,0:T(8,128)(2,1)} %get-tuple-element.27), channel_id=1, source_target_pairs={{0,3},{1,0},{2,1},{3,2},{4,7},{5,4},{6,5},{7,6},{8,11},{9,8},{10,9... | collective-permute-start | bytes 2359304 | tf_op jit(solution)/shard_map/ppermute | solution.py:126
  78.6 229.7 %all-to-all-start.1 = ((bf16[128,2,8,256]{3,2,1,0:T(8,128)(2,1)}), bf16[128,2,8,256]{3,2,1,0:T(8,128)(2,1)S(1)}, u32[]{:S(2)}, u32[]{:S(2)}) async-start(bf16[128,2,8,256]{3,2,1,0:T(8,128)(2,1)} %bitcast.10), calls=%async_computation.1 | async-start | bytes 2097152 | tf_op jit(solution)/shard_map/all_to_all | solution.py:364
  89.4 12.2 %collective-permute-start.11 = (bf16[2,768,128]{2,1,0:T(8,128)(2,1)S(1)}, bf16[2,768,128]{2,1,0:T(8,128)(2,1)S(1)}, u32[]{:S(2)}, u32[]{:S(2)}) collective-permute-start(bf16[2,768,128]{2,1,0:T(8,128)(2,1)S(1)} %slice.63), channel_id=1, source_target_pairs={{0,1},{1,2},{2,3},{3,0},{4,5},{5,6},{6,7},{7,4},{8,9},{9,10},{10,1... | collective-permute-start | bytes 1179656 | tf_op jit(solution)/shard_map/ppermute | solution.py:129
  92.9 13.0 %collective-permute-start.13 = (bf16[2,768,128]{2,1,0:T(8,128)(2,1)S(1)}, bf16[2,768,128]{2,1,0:T(8,128)(2,1)S(1)}, u32[]{:S(2)}, u32[]{:S(2)}) collective-permute-start(bf16[2,768,128]{2,1,0:T(8,128)(2,1)S(1)} %slice.64), channel_id=1, source_target_pairs={{0,3},{1,0},{2,1},{3,2},{4,7},{5,4},{6,5},{7,6},{8,11},{9,8},{10,9... | collective-permute-start | bytes 1179656 | tf_op jit(solution)/shard_map/ppermute | solution.py:130
  107.8 7.9 %collective-permute-start.14 = (bf16[4,4,768,128]{3,2,1,0:T(8,128)(2,1)}, bf16[4,4,768,128]{3,2,1,0:T(8,128)(2,1)}, u32[]{:S(2)}, u32[]{:S(2)}) collective-permute-start(bf16[4,4,768,128]{3,2,1,0:T(8,128)(2,1)} %pad_maximum_fusion.mine_ref), channel_id=1, source_target_pairs={{0,4},{4,0},{1,5},{5,1},{2,6},{6,2},{3,7},{7,3},{8,12},{12,8},{9,1... | collective-permute-start | bytes 9437192 | tf_op jit(solution)/shard_map/ppermute | solution.py:119
  308.2 1.4 copy-start.1
  309.6 39.4 %copy-start.4 = (bf16[4,2,48,768]{3,2,1,0:T(8,128)(2,1)S(1)}, bf16[4,2,48,768]{3,2,1,0:T(8,128)(2,1)}, u32[]{:S(2)}) copy-start(bf16[4,2,48,768]{3,2,1,0:T(8,128)(2,1)} %get-tuple-element.16) | copy-start | bytes 1769476
  309.6 39.4 %copy-start.5 = (bf16[4,2,96,384]{3,2,1,0:T(8,128)(2,1)S(1)}, bf16[4,2,96,384]{3,2,1,0:T(8,128)(2,1)}, u32[]{:S(2)}) copy-start(bf16[4,2,96,384]{3,2,1,0:T(8,128)(2,1)} %get-tuple-element.17) | copy-start | bytes 1769476
  310.6 21.5 %collective-permute-start.15 = (bf16[2,256,768]{2,1,0:T(8,128)(2,1)S(1)}, bf16[2,256,768]{2,1,0:T(8,128)(2,1)S(1)}, u32[]{:S(2)}, u32[]{:S(2)}) collective-permute-start(bf16[2,256,768]{2,1,0:T(8,128)(2,1)S(1)} %embed.1.own_ref), channel_id=1, source_target_pairs={{0,1},{1,2},{2,3},{3,0},{4,5},{5,6},{6,7},{7,4},{8,9},{9,10},{10,1... | collective-permute-start | bytes 2359304 | tf_op jit(solution)/shard_map/ppermute | solution.py:125
  312.5 23.0 %collective-permute-start.16 = (bf16[2,256,768]{2,1,0:T(8,128)(2,1)S(1)}, bf16[2,256,768]{2,1,0:T(8,128)(2,1)S(1)}, u32[]{:S(2)}, u32[]{:S(2)}) collective-permute-start(bf16[2,256,768]{2,1,0:T(8,128)(2,1)S(1)} %embed.1.own_ref), channel_id=1, source_target_pairs={{0,3},{1,0},{2,1},{3,2},{4,7},{5,4},{6,5},{7,6},{8,11},{9,8},{10,9... | collective-permute-start | bytes 2359304 | tf_op jit(solution)/shard_map/ppermute | solution.py:126
  332.1 12.2 %collective-permute-start.17 = (bf16[2,128,768]{2,1,0:T(8,128)(2,1)S(1)}, bf16[2,128,768]{2,1,0:T(8,128)(2,1)S(1)}, u32[]{:S(2)}, u32[]{:S(2)}) collective-permute-start(bf16[2,128,768]{2,1,0:T(8,128)(2,1)S(1)} %slice.65), channel_id=1, source_target_pairs={{0,1},{1,2},{2,3},{3,0},{4,5},{5,6},{6,7},{7,4},{8,9},{9,10},{10,1... | collective-permute-start | bytes 1179656 | tf_op jit(solution)/shard_map/ppermute | solution.py:129
  335.6 13.5 %copy-start.7 = (bf16[2,256,768]{2,1,0:T(8,128)(2,1)}, bf16[2,256,768]{2,1,0:T(8,128)(2,1)S(1)}, u32[]{:S(2)}) copy-start(bf16[2,256,768]{2,1,0:T(8,128)(2,1)S(1)} %collective-permute-done.16.right_ref) | copy-start | bytes 2359300
  335.6 13.5 %collective-permute-start.18 = (bf16[2,128,768]{2,1,0:T(8,128)(2,1)S(1)}, bf16[2,128,768]{2,1,0:T(8,128)(2,1)S(1)}, u32[]{:S(2)}, u32[]{:S(2)}) collective-permute-start(bf16[2,128,768]{2,1,0:T(8,128)(2,1)S(1)} %slice.66), channel_id=1, source_target_pairs={{0,3},{1,0},{2,1},{3,2},{4,7},{5,4},{6,5},{7,6},{8,11},{9,8},{10,9... | collective-permute-start | bytes 1179656 | tf_op jit(solution)/shard_map/ppermute | solution.py:130
  349.1 15.8 %copy-start.3 = (bf16[4,2,48,768]{3,2,1,0:T(8,128)(2,1)S(1)}, bf16[4,2,48,768]{3,2,1,0:T(8,128)(2,1)}, u32[]{:S(2)}) copy-start(bf16[4,2,48,768]{3,2,1,0:T(8,128)(2,1)} %get-tuple-element.22) | copy-start | bytes 1769476
  364.9 1.4 copy-start.2
  374.1 61.1 %all-to-all-start.2 = ((bf16[128,8,384]{2,1,0:T(8,128)(2,1)}), bf16[128,8,384]{2,1,0:T(8,128)(2,1)S(1)}, u32[]{:S(2)}, u32[]{:S(2)}) async-start(bf16[128,8,384]{2,1,0:T(8,128)(2,1)} %bitcast.53), calls=%async_computation.2 | async-start | bytes 1572864 | tf_op jit(solution)/shard_map/all_to_all | solution.py:380

commit v3 on v2

v3 whole, which is shorter than its diff:
```python
import functools

import jax
import jax.numpy as jnp
import numpy as np
from jax import lax
from jax.experimental import pallas as pl
from jax.experimental.pallas import tpu as pltpu
from jax.sharding import Mesh, PartitionSpec as P

HEADS = 6
HD = 64
LANES = 128
IMG = ("x", "z", "c")
VMEM_BYTES = 50 * 1024 * 1024

SECTIONS = (
    ("embed", 8, 6),
    ("project", 6, 9),
    ("self_out", 3, 6),
    ("query", 6, 3),
    ("keyval", 6, 6),
    ("cross_out", 3, 6),
)
def f32_dot(left, right):
    return jnp.dot(left, right, preferred_element_type=jnp.float32)


def normalize(values):
    mean_value = jnp.mean(values, axis=-1, keepdims=True)
    centred = values - mean_value
    variance = jnp.mean(centred * centred, axis=-1, keepdims=True)
    return centred * lax.rsqrt(variance + 1e-06)


def row_tables(sections, toks, z_low, cores):
    total = sum(rows * tiles for _, rows, tiles in sections)
    quarter = total // toks
    table = np.zeros((3, toks, quarter * z_low * cores), np.int32)
    places = []
    at = 0
    for _, rows, tiles in sections:
        places.append([])
        for _ in range(tiles):
            tok, start = divmod(at, quarter)
            assert start + rows <= quarter
            out = start * z_low * cores
            places[-1].append((tok, out, rows * z_low * cores))
            for z in range(z_low):
                for core in range(cores):
                    for row in range(rows):
                        table[:, tok, out] = (start + row, z, core)
                        out += 1
            at += rows
    return table, places, quarter


def pack_kernel(sections, toks, tok_ref, *refs):
    shard_refs, out_ref = refs[:-1], refs[-1]
    pieces = []
    for ref, (_, _, tiles) in zip(shard_refs, sections):
        for tile in range(tiles):
            pieces.append((ref, slice(tile * LANES, (tile + 1) * LANES)))
    quarter = out_ref.shape[0]

    def taken(some):
        values = [ref[:, at].astype(jnp.float32) for ref, at in some]
        return jnp.concatenate(values, axis=0).astype(jnp.bfloat16)

    groups = [[] for _ in range(toks)]
    at = 0
    for ref, columns in pieces:
        groups[at // quarter].append((ref, columns))
        at += ref.shape[0]
    for tok in range(toks):
        @pl.when(tok_ref[0] == tok)
        def _(tok=tok):
            out_ref[...] = taken(groups[tok])


def pack(shards_in, sections, toks):
    quarter = sum(rows * tiles for _, rows, tiles in sections) // toks
    tok = jnp.zeros((1,), jnp.int32) if toks == 1 else lax.axis_index("tok").astype(jnp.int32)[None]
    return pl.pallas_call(
        functools.partial(pack_kernel, sections, toks),
        out_shape=jax.ShapeDtypeStruct((quarter, LANES), jnp.bfloat16),
        in_specs=[pl.BlockSpec(memory_space=pltpu.SMEM)]
        + [pl.BlockSpec(memory_space=pltpu.VMEM)] * len(shards_in),
        out_specs=pl.BlockSpec(memory_space=pltpu.VMEM),
        name="pack",
    )(tok, *shards_in)


def cycle(count, shift):
    return [(i, (i + shift) % count) for i in range(count)]


def swap_cores(value):
    return lax.ppermute(value, "c", cycle(lax.axis_size("c"), 1))


def start_weights(shards_in):
    packed = jnp.concatenate(
        [
            pack(shards_in[:1], SECTIONS[:1], 1),
            pack(shards_in[1:], SECTIONS[1:], lax.axis_size("tok")),
        ],
        axis=0,
    )
    return lax.all_gather(packed, "z", axis=0, tiled=False)


def order_weights(along_z):
    toks, cores = lax.axis_size("tok"), lax.axis_size("c")
    tok, core = lax.axis_index("tok"), lax.axis_index("c")
    depth, packed_rows, lanes = along_z.shape
    z_low = depth // cores
    first_table, _, first_rows = row_tables(SECTIONS[:1], 1, z_low, cores)
    rest_table, _, _ = row_tables(SECTIONS[1:], toks, z_low, cores)
    rest = lax.dynamic_index_in_dim(jnp.asarray(rest_table), tok, axis=1, keepdims=False)
    rest = rest + jnp.asarray([[first_rows], [0], [0]], jnp.int32)
    rows, low, from_core = jnp.concatenate([jnp.asarray(first_table[:, 0]), rest], axis=1)
    mine = lax.dynamic_slice_in_dim(along_z, core * z_low, z_low, axis=0)
    theirs = lax.dynamic_slice_in_dim(along_z, (1 - core) * z_low, z_low, axis=0)
    both = jnp.stack([mine, swap_cores(theirs)])
    order = ((from_core - core) % cores * z_low + low) * packed_rows + rows
    count = cores * z_low * packed_rows
    mover = (order[:, None] == jnp.arange(count, dtype=jnp.int32)[None, :]).astype(jnp.bfloat16)
    ordered = f32_dot(mover, both.reshape(count, lanes)).astype(jnp.bfloat16)
    return ordered, first_table.shape[2]


def spread_weights(ordered, first_rows):
    groups = lax.axis_size("x")
    along_x = [ordered] + [lax.ppermute(ordered, "x", cycle(groups, s)) for s in range(1, groups)]
    first = jnp.stack([piece[:first_rows] for piece in along_x])
    first_full = assemble(first[None], swap_cores(first)[None], SECTIONS[:1], 1)
    rest = jnp.stack([piece[first_rows:] for piece in along_x])
    own, left, right, far_low, far_high = round_ring(rest, 0)
    along_y = jnp.stack([own, left, jnp.concatenate([far_low, far_high], axis=0), right])
    return first_full + assemble(
        along_y, swap_cores(along_y), SECTIONS[1:], lax.axis_size("tok")
    )


def round_ring(own, axis):
    count = lax.axis_size("tok")
    half = own.shape[axis] // 2
    from_left = lax.ppermute(own, "tok", cycle(count, 1))
    from_right = lax.ppermute(own, "tok", cycle(count, -1))
    low = lax.slice_in_dim(from_left, 0, half, axis=axis)
    high = lax.slice_in_dim(from_right, half, 2 * half, axis=axis)
    far_low = lax.ppermute(low, "tok", cycle(count, 1))
    far_high = lax.ppermute(high, "tok", cycle(count, -1))
    return own, from_left, from_right, far_low, far_high


def assemble_kernel(places, at_ref, mine_ref, other_ref, *outs):
    toks, groups = mine_ref.shape[:2]
    tok, x, core = at_ref[0], at_ref[1], at_ref[2]
    for out, tiles in zip(outs, places):
        for tile, (place_tok, start, rows) in enumerate(tiles):
            tok_step = lax.rem(tok - place_tok + toks, toks) if toks > 1 else 0
            for x_step in range(groups):
                from_x = lax.rem(x - x_step + groups, groups)
                for source, half in ((mine_ref, core), (other_ref, 1 - core)):
                    out[from_x, half, :, tile * LANES : (tile + 1) * LANES] = source[
                        tok_step, x_step, start : start + rows, :
                    ]


def assemble(mine, other, sections, toks):
    groups = mine.shape[1]
    cores = lax.axis_size("c")
    _, places, _ = row_tables(sections, toks, lax.axis_size("z") // cores, cores)
    place = jnp.stack(
        [lax.axis_index("tok"), lax.axis_index("x"), lax.axis_index("c")]
    ).astype(jnp.int32)
    shapes = [
        jax.ShapeDtypeStruct((groups, cores, tiles[0][2], len(tiles) * LANES), jnp.bfloat16)
        for tiles in places
    ]
    full = pl.pallas_call(
        functools.partial(assemble_kernel, places),
        out_shape=shapes,
        in_specs=[pl.BlockSpec(memory_space=pltpu.SMEM)]
        + [pl.BlockSpec(memory_space=pltpu.VMEM)] * 2,
        out_specs=[pl.BlockSpec(memory_space=pltpu.VMEM)] * len(shapes),
        compiler_params=pltpu.CompilerParams(vmem_limit_bytes=VMEM_BYTES),
        cost_estimate=pl.CostEstimate(
            flops=0, bytes_accessed=4 * mine.size * 2, transcendentals=0
        ),
        name="assemble",
    )(place, mine, other)
    return [matrix.reshape(-1, matrix.shape[-1]) for matrix in full]


def embed_kernel(arrived_ref, matrix_ref, out_ref):
    groups, blocks, images, block_rows, part = arrived_ref.shape
    for image in range(images):
        total = None
        for group in range(groups):
            rows = arrived_ref[group, :, image].astype(jnp.float32)
            rows = rows.reshape(blocks * block_rows, part).astype(jnp.bfloat16)
            product = f32_dot(rows, matrix_ref[group * part : (group + 1) * part, :])
            total = product if total is None else total + product
        out_ref[image] = total.astype(jnp.bfloat16)


def embed(arrived, matrix):
    groups, blocks, images, block_rows, part = arrived.shape
    rows, width = blocks * block_rows, matrix.shape[1]
    return pl.pallas_call(
        embed_kernel,
        out_shape=jax.ShapeDtypeStruct((images, rows, width), jnp.bfloat16),
        compiler_params=pltpu.CompilerParams(vmem_limit_bytes=VMEM_BYTES),
        cost_estimate=pl.CostEstimate(
            flops=2 * images * rows * matrix.size,
            bytes_accessed=2 * (arrived.size + matrix.size + images * rows * width),
            transcendentals=0,
        ),
        name="embed",
    )(arrived, matrix)


def head_halves():
    return lax.broadcasted_iota(jnp.int32, (1, LANES), 1) < HD


def fold(queries, key_ref, value_ref, first_key, first_value, totals, chunk=256):
    others = key_ref.shape[0]
    low_half = head_halves()
    across = (((1,), (1,)), ((), ()))
    done = []
    for pair in range(HEADS // 2):
        query = queries[:, pair * LANES : (pair + 1) * LANES]
        blank = jnp.zeros_like(query)
        low_query = jnp.where(low_half, query, blank)
        high_query = jnp.where(low_half, blank, query)
        low_total, high_total = totals[2 * pair], totals[2 * pair + 1]
        for start in range(0, others, chunk):
            at = slice(start, start + chunk)
            keys = key_ref[at, first_key + pair * LANES : first_key + (pair + 1) * LANES]
            values = value_ref[at, first_value + pair * LANES : first_value + (pair + 1) * LANES]
            ones = jnp.ones_like(values)
            scores = lax.dot_general(low_query, keys, across, preferred_element_type=jnp.float32)
            weights = jnp.exp(scores).astype(jnp.bfloat16)
            low_total = low_total + f32_dot(weights, jnp.where(low_half, values, ones))
            scores = lax.dot_general(high_query, keys, across, preferred_element_type=jnp.float32)
            weights = jnp.exp(scores).astype(jnp.bfloat16)
            high_total = high_total + f32_dot(weights, jnp.where(low_half, ones, values))
        done += [low_total, high_total]
    return done


def finish(totals):
    low_half = head_halves()
    done = []
    for pair in range(HEADS // 2):
        low_total, high_total = totals[2 * pair], totals[2 * pair + 1]
        numer = jnp.where(low_half, low_total, high_total)
        denom = pltpu.roll(jnp.where(low_half, high_total, low_total), HD, 1)
        done.append((numer / denom).astype(jnp.bfloat16))
    return jnp.concatenate(done, axis=1)


def nothing(rows):
    return [jnp.zeros((rows, LANES), jnp.float32)] * HEADS


def scaled(queries):
    return (queries.astype(jnp.bfloat16).astype(jnp.float32) * HD**-0.5).astype(jnp.bfloat16)


def self_kernel(first, last, pieces, *refs):
    refs = list(refs)
    piece_refs = [refs.pop(0) for _ in range(pieces)]
    if not first:
        query_ref, totals_in = refs.pop(0), refs.pop(0)
    if last:
        own_ref = refs.pop(0)
    project_ref, keyval_ref = refs.pop(0), refs.pop(0)
    width = keyval_ref.shape[1] // 2
    if last:
        output_ref, second_ref = refs.pop(0), refs.pop(0)
    cross_ref = refs.pop(0)
    if first:
        query_out = refs.pop(0)
    if last:
        after_ref, next_ref = refs.pop(0), refs.pop(0)
    else:
        totals_out = refs.pop(0)
    scratch = refs.pop(0)
    at = 0
    for ref in piece_refs:
        normed = normalize(ref[0].astype(jnp.float32)).astype(jnp.bfloat16)
        here = slice(at, at + normed.shape[0])
        scratch[here] = f32_dot(normed, project_ref[:, width:]).astype(jnp.bfloat16)
        cross_ref[0, here] = f32_dot(normed, keyval_ref[...]).astype(jnp.bfloat16)
        at += normed.shape[0]
    if first:
        queries = scaled(f32_dot(normed, project_ref[:, :width]))
        query_out[0] = queries
        totals = nothing(queries.shape[0])
    else:
        queries = query_ref[0]
        totals = [totals_in[0, head] for head in range(HEADS)]
    totals = fold(queries, scratch, scratch, 0, width, totals)
    if last:
        after = own_ref[0].astype(jnp.float32) + f32_dot(finish(totals), output_ref[...])
        after_ref[0] = after
        second = normalize(after).astype(jnp.bfloat16)
        next_ref[0] = scaled(f32_dot(second, second_ref[...]))
    else:
        for head in range(HEADS):
            totals_out[0, head] = totals[head]


def per_image(shape):
    return pl.BlockSpec((1,) + shape[1:], lambda i: (i,) + (0,) * (len(shape) - 1))


def whole(matrix):
    return pl.BlockSpec(matrix.shape, lambda i: (0, 0))


def self_step(pieces, project, keyval, carry=None, ending=None):
    first, last = carry is None, ending is not None
    images, _, model = pieces[0].shape
    width = keyval.shape[1] // 2
    others = sum(piece.shape[1] for piece in pieces)
    arrays = list(pieces) + list(carry or ())
    matrices = [project, keyval]
    if last:
        arrays.append(ending[0])
        matrices += ending[1:]
    rows = pieces[0].shape[1] if first else carry[0].shape[1]
    shapes = [jax.ShapeDtypeStruct((images, others, 2 * width), jnp.bfloat16)]
    if first:
        shapes.append(jax.ShapeDtypeStruct((images, rows, width), jnp.bfloat16))
    if last:
        shapes.append(jax.ShapeDtypeStruct((images, rows, model), jnp.float32))
        shapes.append(jax.ShapeDtypeStruct((images, rows, width), jnp.bfloat16))
    else:
        shapes.append(jax.ShapeDtypeStruct((images, HEADS, rows, LANES), jnp.float32))
    return pl.pallas_call(
        functools.partial(self_kernel, first, last, len(pieces)),
        grid=(images,),
        out_shape=shapes,
        in_specs=[per_image(array.shape) for array in arrays] + [whole(matrix) for matrix in matrices],
        out_specs=[per_image(shape.shape) for shape in shapes],
        scratch_shapes=[pltpu.VMEM((others, 2 * width), jnp.bfloat16)],
        compiler_params=pltpu.CompilerParams(vmem_limit_bytes=VMEM_BYTES),
        cost_estimate=pl.CostEstimate(
            flops=2 * images * (others * model * 4 * width + 4 * rows * others * width),
            bytes_accessed=2 * sum(matrix.size for matrix in matrices)
            + sum(array.size * array.dtype.itemsize for array in arrays),
            transcendentals=images * HEADS * rows * others,
        ),
        name="self_step",
    )(*arrays, *matrices)


def cross_kernel(pieces, after_ref, query_ref, *refs):
    keyval_refs, output_ref, out_ref = refs[:pieces], refs[pieces], refs[pieces + 1]
    width = output_ref.shape[0]
    halves, blocks, block_rows, part = out_ref.shape[1:]
    queries = query_ref[0]
    totals = nothing(queries.shape[0])
    for ref in keyval_refs:
        keyval = ref.at[0]
        totals = fold(queries, keyval, keyval, 0, width, totals)
    mixed = after_ref[0] + f32_dot(finish(totals), output_ref[...])
    for half in range(halves):
        columns = mixed[:, half * part : (half + 1) * part]
        out_ref[0, half] = columns.reshape(blocks, block_rows, part).astype(jnp.bfloat16)


def cross_block(after, query, keyvals, output, halves, block_rows):
    images, rows, model = after.shape
    width = output.shape[0]
    everyone = sum(keyval.shape[1] for keyval in keyvals)
    shape = (images, halves, rows // block_rows, block_rows, model // halves)
    return pl.pallas_call(
        functools.partial(cross_kernel, len(keyvals)),
        grid=(images,),
        out_shape=jax.ShapeDtypeStruct(shape, jnp.bfloat16),
        in_specs=[per_image(after.shape), per_image(query.shape)]
        + [
            pl.BlockSpec((1,) + keyval.shape[1:], lambda i: (images - 1 - i, 0, 0))
            for keyval in keyvals
        ]
        + [whole(output)],
        out_specs=per_image(shape),
        compiler_params=pltpu.CompilerParams(vmem_limit_bytes=VMEM_BYTES),
        cost_estimate=pl.CostEstimate(
            flops=2 * images * (4 * rows * everyone * width + rows * model * width),
            bytes_accessed=4 * after.size + 2 * (query.size + output.size + after.size),
            transcendentals=images * HEADS * rows * everyone,
        ),
        name="cross_block",
    )(after, query, *keyvals, output)


def shards(tokens, pair_list, owner_base, *weight_shards):
    groups = lax.axis_size("x")
    row_devices = lax.axis_size("z") * lax.axis_size("c")
    devices = groups * row_devices
    column = lax.axis_index("z") * lax.axis_size("c") + lax.axis_index("c")
    spread, block_rows, encoder = tokens.shape[1], tokens.shape[3], tokens.shape[4]
    held = tokens.reshape(spread, block_rows, encoder)
    part = encoder // groups

    parted = jnp.stack([held[:, :, x * part : (x + 1) * part] for x in range(groups)])
    parted, weight_shards = lax.optimization_barrier((parted, weight_shards))
    pieces = lax.all_to_all(parted, "x", 0, 0, tiled=True).reshape(devices, block_rows, part)
    along_z = start_weights(weight_shards)
    pieces, along_z = lax.optimization_barrier((pieces, along_z))

    bases = owner_base[pair_list]
    slot = (column - bases) % spread
    source = ((bases + slot - column) // row_devices) % groups
    place = source * spread + slot
    outgoing = jnp.take(pieces, place.reshape(-1), axis=0, mode="clip").reshape(
        devices, 2, block_rows, part
    )
    ordered, first_rows = order_weights(along_z)
    outgoing, ordered = lax.optimization_barrier((outgoing, ordered))
    arrived = lax.all_to_all(outgoing, IMG, 0, 0, tiled=True)
    arrived = arrived.reshape(groups, row_devices, 2, block_rows, part)
    full = spread_weights(ordered, first_rows)
    embed_full, project_full, self_out_full, query_full, keyval_full, cross_out_full = full
    model_width = embed_full.shape[1]

    embedded = embed(arrived, embed_full)
    own, left, right, far_low, far_high = round_ring(embedded, 1)
    near_keyval, queries, totals = self_step([own], project_full, keyval_full)
    next_keyval, totals = self_step([left, right], project_full, keyval_full, (queries, totals))
    far_keyval, after_self, cross_queries = self_step(
        [far_low, far_high], project_full, keyval_full, (queries, totals),
        (own, self_out_full, query_full),
    )

    halves = groups // 2
    backward = cross_block(
        after_self, cross_queries, [near_keyval, next_keyval, far_keyval], cross_out_full,
        halves, block_rows,
    ).reshape(devices, block_rows, model_width // halves)
    returned = lax.all_to_all(backward, IMG, 0, 0, tiled=True)
    my_half = lax.axis_index("x") // halves
    my_place = lax.dynamic_index_in_dim(place, my_half, axis=1, keepdims=False)
    selector = (
        my_place[None, :] == jnp.arange(devices, dtype=jnp.int32)[:, None]
    ).astype(jnp.bfloat16)
    partial = jnp.einsum(
        "ge,ebd->gbd", selector, returned, preferred_element_type=jnp.float32
    ).astype(jnp.bfloat16)
    home = lax.all_to_all(
        partial.reshape(groups, spread, block_rows, model_width // halves), "x", 0, 0, tiled=True
    )
    home = home.reshape(2, halves, spread, block_rows, model_width // halves)
    total = home[0].astype(jnp.float32) + home[1].astype(jnp.float32)
    summed = jnp.concatenate([total[half] for half in range(halves)], axis=-1)
    return summed.astype(jnp.bfloat16).reshape(1, spread, 1, block_rows, model_width)


def solution(mesh):
    chips = Mesh(mesh.devices.reshape(4, 16, 2, 4), ("x", "z", "c", "tok"))
    rows = P(IMG, None)
    tokens = P(IMG, None, "tok", None, None)
    return jax.shard_map(
        shards,
        mesh=chips,
        in_specs=(tokens, P(), P()) + (rows,) * 6,
        out_specs=tokens,
        check_vma=False,
    )
```

time: 454 us -> 278 us (0.61)
  Pallas kernels: 217 us -> 38.3 us
  blocking collectives: 15.4 us -> 52.7 us
  starting transfers between devices: 105 us -> 70.4 us
    pallas_call x1 -> x2, Pallas kernels: 192 us -> 5.32 us  [assemble(): pl.pallas_call(functools.partial(assemble_kernel, places), out_shape=shap...]
    all_gather x0 -> x1, blocking collectives: none -> 37.4 us  [start_weights(): return lax.all_gather(packed, 'z', axis=0, tiled=False)]
    ppermute x11 -> x6, starting transfers between devices: 50.8 us -> 16.3 us  [the longest x3 10.1 us: spread_weights(): lax.ppermute(ordered, 'x', cycle(groups, s))]
    ppermute x11 -> x6, waiting for transfers between devices: 12.9 us -> 22.1 us  [the longest x3 19.8 us: spread_weights(): lax.ppermute(ordered, 'x', cycle(groups, s))]
    pallas_call x2 -> x6, Pallas kernels: 23.6 us -> 32 us  [the longest x3 21.7 us: self_step(): pl.pallas_call(functools.partial(self_kernel, first, last, len(pieces)),...]
    ppermute x2, waiting for transfers between devices: 12.4 us -> 4.03 us  [round_ring(): far_low = lax.ppermute(low, 'tok', cycle(count, 1))]
    ppermute x2, waiting for transfers between devices: 16 us -> 22.4 us  [round_ring(): from_left = lax.ppermute(own, 'tok', cycle(count, 1))]
    ppermute x2, waiting for transfers between devices: 9.05 us -> 4.47 us  [round_ring(): far_high = lax.ppermute(high, 'tok', cycle(count, -1))]
  transfers between devices with their start and end apart: 22 -> 17, of which waited for: 12 -> 8; matrix products, arithmetic and copies ran while one was open for 2% -> 3% of each run, Pallas kernels for 43% -> 8%
where the time goes in v3:
time: 278 us; the launch traced here: 275 us
  waiting for transfers between devices  97.1 us (35%)
  starting transfers between devices  70.4 us (25%)
  blocking collectives  52.7 us (19%)
  Pallas kernels  38.3 us (14%)
  local copies, waits for them, and re-layouts  8.11 us (3%)
  other arithmetic  6.42 us (2%)
    all_to_all x1, waiting for transfers between devices, shards(): returned = lax.all_to_all(backward, IMG, 0, 0, tiled=True)  44.1 us
    all_gather x1, blocking collectives, start_weights(): return lax.all_gather(packed, 'z', axis=0, tiled=False)  37.4 us
    ppermute x2, waiting for transfers between devices, round_ring(): from_left = lax.ppermute(own, 'tok', cycle(count, 1))  22.4 us
    pallas_call x3, Pallas kernels, self_step(): pl.pallas_call(functools.partial(self_kernel, first, last, len(pieces)),...  21.7 us
    ppermute x3, waiting for transfers between devices, spread_weights(): lax.ppermute(ordered, 'x', cycle(groups, s))  19.8 us
    all_to_all x1, blocking collectives, shards(): lax.all_to_all(partial.reshape(groups, spread, block_rows, model_width //...  15.4 us
    all_to_all x1, starting transfers between devices, shards(): returned = lax.all_to_all(backward, IMG, 0, 0, tiled=True)  14.2 us
    all_to_all x1, starting transfers between devices, shards(): arrived = lax.all_to_all(outgoing, IMG, 0, 0, tiled=True)  12.1 us
  transfers between devices with their start and end apart: 17, of which 8 were waited for; matrix products, arithmetic and copies ran while one was open for 3% of the time, Pallas kernels for 8%

profile of v3, /device:TPU:24, one launch (start us, length us, event | category | flops | bytes accessed | tf_op | source)
XLA Modules:
  0.0 275.4 jit_solution(6343231651446390664)
XLA Ops:
  2.0 4.3 %all-to-all-start = ((bf16[4,32,8,256]{3,2,1,0:T(8,128)(2,1)}), bf16[4,32,8,256]{3,2,1,0:T(8,128)(2,1)S(1)}, u32[]{:S(2)}, u32[]{:S(2)}) async-start(bf16[4,32,8,256]{3,2,1,0:T(8,128)(2,1)} %pad_maximum_fusion.3), calls=%async_computation | async-start | bytes 1048576 | tf_op jit(solution)/shard_map/all_to_all | solution.py:416
  12.8 37.4 %all-gather.1 = bf16[16,84,128]{2,1,0:T(8,128)(2,1)S(1)} all-gather(bf16[1,84,128]{2,1,0:T(8,128)(2,1)S(1)} %maximum_bitcast_fusion.1), channel_id=2, replica_groups=mesh['x'=4,'z'=16,'c'=2,'tok'=4] {'z'}, dimensions={0}, use_global_device_ids=true | all-gather | bytes 365568 | tf_op jit(solution)/shard_map/all_gather | solution.py:110
  50.2 1.9 collective-permute-start
  55.5 12.1 %all-to-all-start.1 = ((bf16[128,2,8,256]{3,2,1,0:T(8,128)(2,1)}), bf16[128,2,8,256]{3,2,1,0:T(8,128)(2,1)S(1)}, u32[]{:S(2)}, u32[]{:S(2)}) async-start(bf16[128,2,8,256]{3,2,1,0:T(8,128)(2,1)} %bitcast.12), calls=%async_computation.1 | async-start | bytes 2097152 | tf_op jit(solution)/shard_map/all_to_all | solution.py:429
  67.6 4.8 %collective-permute-start.3 = (bf16[1344,128]{1,0:T(8,128)(2,1)S(1)}, bf16[1344,128]{1,0:T(8,128)(2,1)S(1)}, u32[]{:S(2)}, u32[]{:S(2)}) collective-permute-start(bf16[1344,128]{1,0:T(8,128)(2,1)S(1)} %fusion.2), channel_id=1, source_target_pairs={{0,384},{128,0},{256,128},{384,256},{1,385},{129,1},{257,129},{385... | collective-permute-start | bytes 1032200 | tf_op jit(solution)/shard_map/ppermute | solution.py:135
  72.4 2.3 collective-permute-start.2
  74.8 3.0 %collective-permute-start.1 = (bf16[1344,128]{1,0:T(8,128)(2,1)S(1)}, bf16[1344,128]{1,0:T(8,128)(2,1)S(1)}, u32[]{:S(2)}, u32[]{:S(2)}) collective-permute-start(bf16[1344,128]{1,0:T(8,128)(2,1)S(1)} %fusion.2), channel_id=1, source_target_pairs={{0,128},{128,256},{256,384},{384,0},{1,129},{129,257},{257,385},{3... | collective-permute-start | bytes 1032200 | tf_op jit(solution)/shard_map/ppermute | solution.py:135
  77.8 14.1 %collective-permute-done.3 = bf16[1344,128]{1,0:T(8,128)(2,1)S(1)} collective-permute-done((bf16[1344,128]{1,0:T(8,128)(2,1)S(1)}, bf16[1344,128]{1,0:T(8,128)(2,1)S(1)}, u32[]{:S(2)}, u32[]{:S(2)}) %collective-permute-start.3) | collective-permute-done | bytes 344096 | tf_op jit(solution)/shard_map/ppermute | solution.py:135
  91.9 5.7 %collective-permute-done.1 = bf16[1344,128]{1,0:T(8,128)(2,1)S(1)} collective-permute-done((bf16[1344,128]{1,0:T(8,128)(2,1)S(1)}, bf16[1344,128]{1,0:T(8,128)(2,1)S(1)}, u32[]{:S(2)}, u32[]{:S(2)}) %collective-permute-start.1) | collective-permute-done | bytes 344096 | tf_op jit(solution)/shard_map/ppermute | solution.py:135
  97.8 2.1 collective-permute-start.9
  99.9 3.7 %collective-permute-start.11 = (bf16[4,576,128]{2,1,0:T(8,128)(2,1)S(1)}, bf16[4,576,128]{2,1,0:T(8,128)(2,1)S(1)}, u32[]{:S(2)}, u32[]{:S(2)}) collective-permute-start(bf16[4,576,128]{2,1,0:T(8,128)(2,1)S(1)} %get-tuple-element.59), channel_id=1, source_target_pairs={{0,3},{1,0},{2,1},{3,2},{4,7},{5,4},{6,5},{7,6},{8,11},{9,8},{10,9... | collective-permute-start | bytes 1769480 | tf_op jit(solution)/shard_map/ppermute | solution.py:150
  103.6 11.3 %collective-permute-done.9 = bf16[4,576,128]{2,1,0:T(8,128)(2,1)S(1)} collective-permute-done((bf16[4,576,128]{2,1,0:T(8,128)(2,1)S(1)}, bf16[4,576,128]{2,1,0:T(8,128)(2,1)S(1)}, u32[]{:S(2)}, u32[]{:S(2)}) %collective-permute-start.9) | collective-permute-done | bytes 589856 | tf_op jit(solution)/shard_map/ppermute | solution.py:149
  114.9 3.4 %collective-permute-start.10 = (bf16[2,576,128]{2,1,0:T(8,128)(2,1)S(1)}, bf16[2,576,128]{2,1,0:T(8,128)(2,1)S(1)}, u32[]{:S(2)}, u32[]{:S(2)}) collective-permute-start(bf16[2,576,128]{2,1,0:T(8,128)(2,1)S(1)} %slice.100), channel_id=1, source_target_pairs={{0,1},{1,2},{2,3},{3,0},{4,5},{5,6},{6,7},{7,4},{8,9},{9,10},{10,1... | collective-permute-start | bytes 884744 | tf_op jit(solution)/shard_map/ppermute | solution.py:153
  118.4 2.4 collective-permute-start.12
  120.8 4.0 %collective-permute-done.10 = bf16[2,576,128]{2,1,0:T(8,128)(2,1)S(1)} collective-permute-done((bf16[2,576,128]{2,1,0:T(8,128)(2,1)S(1)}, bf16[2,576,128]{2,1,0:T(8,128)(2,1)S(1)}, u32[]{:S(2)}, u32[]{:S(2)}) %collective-permute-start.10) | collective-permute-done | bytes 294944 | tf_op jit(solution)/shard_map/ppermute | solution.py:153
  124.9 4.5 %collective-permute-done.12 = bf16[2,576,128]{2,1,0:T(8,128)(2,1)S(1)} collective-permute-done((bf16[2,576,128]{2,1,0:T(8,128)(2,1)S(1)}, bf16[2,576,128]{2,1,0:T(8,128)(2,1)S(1)}, u32[]{:S(2)}, u32[]{:S(2)}) %collective-permute-start.12) | collective-permute-done | bytes 294944 | tf_op jit(solution)/shard_map/ppermute | solution.py:154
  131.1 1.9 collective-permute-start.13
  134.1 2.4 collective-permute-start.4
  136.6 2.3 collective-permute-done.4
  142.7 1.9 collective-permute-start.5
  144.6 3.9 %collective-permute-start.7 = (bf16[2,256,768]{2,1,0:T(8,128)(2,1)S(1)}, bf16[2,256,768]{2,1,0:T(8,128)(2,1)S(1)}, u32[]{:S(2)}, u32[]{:S(2)}) collective-permute-start(bf16[2,256,768]{2,1,0:T(8,128)(2,1)S(1)} %embed.1.refs_0_.refs_4_), channel_id=1, source_target_pairs={{0,3},{1,0},{2,1},{3,2},{4,7},{5,4},{6,5},{7,6},{8,11},{9,8},{10,9... | collective-permute-start | bytes 2359304 | tf_op jit(solution)/shard_map/ppermute | solution.py:150
  148.6 4.5 %assemble.3 = (bf16[4,2,96,1152]{3,2,1,0:T(8,128)(2,1)}, bf16[4,2,48,768]{3,2,1,0:T(8,128)(2,1)S(1)}, bf16[4,2,96,384]{3,2,1,0:T(8,128)(2,1)S(1)}, bf16[4,2,96,7...) custom-call(s32[3]{0:T(128)S(1)} %pad_add_fusion.1.at_ref, bf16[4,4,576,128]{3,2,1,0:T(8,128)(2,1)} %pad_maximum_fusion.mine_ref, ...), custom_call_target="tpu_custom_call" | custom-call | bytes 9437184 | tf_op jit(solution)/shard_map/assemble/pallas_call | solution.py:183
  153.1 11.1 %collective-permute-done.5.refs_0_ = bf16[2,256,768]{2,1,0:T(8,128)(2,1)S(1)} collective-permute-done((bf16[2,256,768]{2,1,0:T(8,128)(2,1)S(1)}, bf16[2,256,768]{2,1,0:T(8,128)(2,1)S(1)}, u32[]{:S(2)}, u32[]{:S(2)}) %collective-permute-start.5) | collective-permute-done | bytes 786464 | tf_op jit(solution)/shard_map/ppermute | solution.py:149
  164.2 3.4 %collective-permute-start.6 = (bf16[2,128,768]{2,1,0:T(8,128)(2,1)S(1)}, bf16[2,128,768]{2,1,0:T(8,128)(2,1)S(1)}, u32[]{:S(2)}, u32[]{:S(2)}) collective-permute-start(bf16[2,128,768]{2,1,0:T(8,128)(2,1)S(1)} %slice.95), channel_id=1, source_target_pairs={{0,1},{1,2},{2,3},{3,0},{4,5},{5,6},{6,7},{7,4},{8,9},{9,10},{10,1... | collective-permute-start | bytes 1179656 | tf_op jit(solution)/shard_map/ppermute | solution.py:153
  167.7 2.6 collective-permute-start.8
  170.3 6.1 %self_step.3 = (bf16[2,256,768]{2,1,0:T(8,128)(2,1)S(1)}, bf16[2,256,384]{2,1,0:T(8,128)(2,1)S(1)}, f32[2,6,256,128]{3,2,1,0:T(8,128)}) custom-call(bf16[2,256,768]{2,1,0:T(8,128)(2,1)S(1)} %embed.1.refs_0_.refs_4_, bf16[768,1152]{1,0:T(8,128)(2,1)} %bitcast.81, bf16[768,768]{1,0:T(8,128)(2,1)S(1)} %bitcast.71), custom_call_target="tpu_custom_call" | custom-call | flops 1610612736 | bytes 3735552 | tf_op jit(solution)/shard_map/self_step/pallas_call | solution.py:346
  176.4 8.0 %self_step.4 = (bf16[2,512,768]{2,1,0:T(8,128)(2,1)}, f32[2,6,256,128]{3,2,1,0:T(8,128)}) custom-call(bf16[2,256,768]{2,1,0:T(8,128)(2,1)S(1)} %collective-permute-done.5.refs_0_, bf16[2,256,768]{2,1,0:T(8,128)(2,1)S(1)} %collective-permute-done.7.refs_1_, bf16[2,256,384]{2,1,0:T(8,128)(2,1)S(1)} %get-tuple-element.42.refs_2_, ...), custom_call_target="tpu_custom_call" | custom-call | flops 3221225472 | bytes 6488064 | tf_op jit(solution)/shard_map/self_step/pallas_call | solution.py:346
  184.4 7.6 %self_step.5 = (bf16[2,256,768]{2,1,0:T(8,128)(2,1)S(1)}, f32[2,256,768]{2,1,0:T(8,128)}, bf16[2,256,384]{2,1,0:T(8,128)(2,1)S(1)}) custom-call(bf16[2,128,768]{2,1,0:T(8,128)(2,1)S(1)} %collective-permute-done.6.refs_0_, bf16[2,128,768]{2,1,0:T(8,128)(2,1)S(1)} %collective-permute-done.8.refs_1_, bf16[2,256,384]{2,1,0:T(8,128)(2,1)S(1)} %get-tuple-element.42.refs_2_, ...), custom_call_target="tpu_custom_call" | custom-call | flops 1610612736 | bytes 7667712 | tf_op jit(solution)/shard_map/self_step/pallas_call | solution.py:346
  192.0 7.7 %cross_block.1 = bf16[2,2,32,8,384]{4,3,2,1,0:T(8,128)(2,1)} custom-call(f32[2,256,768]{2,1,0:T(8,128)} %get-tuple-element.47.after_ref, bf16[2,256,384]{2,1,0:T(8,128)(2,1)S(1)} %get-tuple-element.48.query_ref, bf16[2,256,768]{2,1,0:T(8,128)(2,1)S(1)} %get-tuple-element.49.refs_0_, bf16[2,512,768]{2,1,0:T(8,128)(2,1)} %get-tuple-element.50.refs_1_, ...), custom_call_target="tpu_custom_call" | custom-call | flops 1912602624 | bytes 3342336 | tf_op jit(solution)/shard_map/cross_block/pallas_call | solution.py:384
  199.7 14.2 %all-to-all-start.2 = ((bf16[128,8,384]{2,1,0:T(8,128)(2,1)}), bf16[128,8,384]{2,1,0:T(8,128)(2,1)S(1)}, u32[]{:S(2)}, u32[]{:S(2)}) async-start(bf16[128,8,384]{2,1,0:T(8,128)(2,1)} %bitcast.39), calls=%async_computation.2 | async-start | bytes 1572864 | tf_op jit(solution)/shard_map/all_to_all | solution.py:449
  214.2 44.1 %all-to-all-done.2 = bf16[128,8,384]{2,1,0:T(8,128)(2,1)S(1)} async-done(((bf16[128,8,384]{2,1,0:T(8,128)(2,1)}), bf16[128,8,384]{2,1,0:T(8,128)(2,1)S(1)}, u32[]{:S(2)}, u32[]{:S(2)}) %all-to-all-start.2) | async-done | bytes 786464 | tf_op jit(solution)/shard_map/all_to_all | solution.py:449
  259.1 15.4 %all_to_all.20 = bf16[4,32,8,384]{3,2,1,0:T(8,128)(2,1)S(1)} all-to-all(bf16[4,32,8,384]{3,2,1,0:T(8,128)(2,1)S(1)} %copy.44), channel_id=1, replica_groups=mesh['x'=4,'z'=16,'c'=2,'tok'=4] {'x'}, dimensions={0} | all-to-all | bytes 1572864 | tf_op jit(solution)/shard_map/all_to_all | solution.py:458
  (77 shorter events, 20.9 us)
Async XLA Ops:
  0.0 6.6 %copy-start = (s32[128]{0:T(128)S(1)}, s32[128]{0:T(128)}, u32[]{:S(2)}) copy-start(s32[128]{0:T(128)} %param.14) | copy-start | bytes 1540
  0.0 6.3 %copy-start.8 = (s32[128,2]{0,1:T(2,128)S(1)}, s32[128,2]{0,1:T(2,128)}, u32[]{:S(2)}) copy-start(s32[128,2]{0,1:T(2,128)} %param.13) | copy-start | bytes 3076
  2.0 48.1 %all-to-all-start = ((bf16[4,32,8,256]{3,2,1,0:T(8,128)(2,1)}), bf16[4,32,8,256]{3,2,1,0:T(8,128)(2,1)S(1)}, u32[]{:S(2)}, u32[]{:S(2)}) async-start(bf16[4,32,8,256]{3,2,1,0:T(8,128)(2,1)} %pad_maximum_fusion.3), calls=%async_computation | async-start | bytes 1048576 | tf_op jit(solution)/shard_map/all_to_all | solution.py:416
  6.6 1.9 copy-start.9
  6.6 5.4 %copy-start.7 = (s32[3,768]{1,0:T(4,128)S(1)}, s32[3,768]{1,0:T(4,128)}, u32[]{:S(2)}) copy-start(s32[3,768]{1,0:T(4,128)} %constant.115.clone) | copy-start | bytes 27652
  50.2 3.7 %collective-permute-start = (bf16[8,84,128]{2,1,0:T(8,128)(2,1)S(1)}, bf16[8,84,128]{2,1,0:T(8,128)(2,1)S(1)}, u32[]{:S(2)}, u32[]{:S(2)}) collective-permute-start(bf16[8,84,128]{2,1,0:T(8,128)(2,1)S(1)} %get-tuple-element.67), channel_id=1, source_target_pairs={{0,4},{4,0},{1,5},{5,1},{2,6},{6,2},{3,7},{7,3},{8,12},{12,8},{9,1... | collective-permute-start | bytes 516104 | tf_op jit(solution)/shard_map/ppermute | solution.py:99
  55.5 42.1 %copy-start.5 = (bf16[1344,128]{1,0:T(8,128)(2,1)}, bf16[1344,128]{1,0:T(8,128)(2,1)S(1)}, u32[]{:S(2)}) copy-start(bf16[1344,128]{1,0:T(8,128)(2,1)S(1)} %fusion.2) | copy-start | bytes 1032196
  55.5 86.2 %all-to-all-start.1 = ((bf16[128,2,8,256]{3,2,1,0:T(8,128)(2,1)}), bf16[128,2,8,256]{3,2,1,0:T(8,128)(2,1)S(1)}, u32[]{:S(2)}, u32[]{:S(2)}) async-start(bf16[128,2,8,256]{3,2,1,0:T(8,128)(2,1)} %bitcast.12), calls=%async_computation.1 | async-start | bytes 2097152 | tf_op jit(solution)/shard_map/all_to_all | solution.py:429
  67.6 24.2 %collective-permute-start.3 = (bf16[1344,128]{1,0:T(8,128)(2,1)S(1)}, bf16[1344,128]{1,0:T(8,128)(2,1)S(1)}, u32[]{:S(2)}, u32[]{:S(2)}) collective-permute-start(bf16[1344,128]{1,0:T(8,128)(2,1)S(1)} %fusion.2), channel_id=1, source_target_pairs={{0,384},{128,0},{256,128},{384,256},{1,385},{129,1},{257,129},{385... | collective-permute-start | bytes 1032200 | tf_op jit(solution)/shard_map/ppermute | solution.py:135
  72.4 19.5 %collective-permute-start.2 = (bf16[1344,128]{1,0:T(8,128)(2,1)S(1)}, bf16[1344,128]{1,0:T(8,128)(2,1)S(1)}, u32[]{:S(2)}, u32[]{:S(2)}) collective-permute-start(bf16[1344,128]{1,0:T(8,128)(2,1)S(1)} %fusion.2), channel_id=1, source_target_pairs={{0,256},{128,384},{256,0},{384,128},{1,257},{129,385},{257,1},{385... | collective-permute-start | bytes 1032200 | tf_op jit(solution)/shard_map/ppermute | solution.py:135
  74.8 22.9 %collective-permute-start.1 = (bf16[1344,128]{1,0:T(8,128)(2,1)S(1)}, bf16[1344,128]{1,0:T(8,128)(2,1)S(1)}, u32[]{:S(2)}, u32[]{:S(2)}) collective-permute-start(bf16[1344,128]{1,0:T(8,128)(2,1)S(1)} %fusion.2), channel_id=1, source_target_pairs={{0,128},{128,256},{256,384},{384,0},{1,129},{129,257},{257,385},{3... | collective-permute-start | bytes 1032200 | tf_op jit(solution)/shard_map/ppermute | solution.py:135
  97.6 23.2 %copy-start.6 = (bf16[1344,128]{1,0:T(8,128)(2,1)S(1)}, bf16[1344,128]{1,0:T(8,128)(2,1)}, u32[]{:S(2)}) copy-start(bf16[1344,128]{1,0:T(8,128)(2,1)} %copy-done.5) | copy-start | bytes 1032196
  97.8 17.1 %collective-permute-start.9 = (bf16[4,576,128]{2,1,0:T(8,128)(2,1)S(1)}, bf16[4,576,128]{2,1,0:T(8,128)(2,1)S(1)}, u32[]{:S(2)}, u32[]{:S(2)}) collective-permute-start(bf16[4,576,128]{2,1,0:T(8,128)(2,1)S(1)} %get-tuple-element.59), channel_id=1, source_target_pairs={{0,1},{1,2},{2,3},{3,0},{4,5},{5,6},{6,7},{7,4},{8,9},{9,10},{10,1... | collective-permute-start | bytes 1769480 | tf_op jit(solution)/shard_map/ppermute | solution.py:149
  99.9 18.4 %collective-permute-start.11 = (bf16[4,576,128]{2,1,0:T(8,128)(2,1)S(1)}, bf16[4,576,128]{2,1,0:T(8,128)(2,1)S(1)}, u32[]{:S(2)}, u32[]{:S(2)}) collective-permute-start(bf16[4,576,128]{2,1,0:T(8,128)(2,1)S(1)} %get-tuple-element.59), channel_id=1, source_target_pairs={{0,3},{1,0},{2,1},{3,2},{4,7},{5,4},{6,5},{7,6},{8,11},{9,8},{10,9... | collective-permute-start | bytes 1769480 | tf_op jit(solution)/shard_map/ppermute | solution.py:150
  114.9 10.0 %collective-permute-start.10 = (bf16[2,576,128]{2,1,0:T(8,128)(2,1)S(1)}, bf16[2,576,128]{2,1,0:T(8,128)(2,1)S(1)}, u32[]{:S(2)}, u32[]{:S(2)}) collective-permute-start(bf16[2,576,128]{2,1,0:T(8,128)(2,1)S(1)} %slice.100), channel_id=1, source_target_pairs={{0,1},{1,2},{2,3},{3,0},{4,5},{5,6},{6,7},{7,4},{8,9},{9,10},{10,1... | collective-permute-start | bytes 884744 | tf_op jit(solution)/shard_map/ppermute | solution.py:153
  118.4 11.0 %collective-permute-start.12 = (bf16[2,576,128]{2,1,0:T(8,128)(2,1)S(1)}, bf16[2,576,128]{2,1,0:T(8,128)(2,1)S(1)}, u32[]{:S(2)}, u32[]{:S(2)}) collective-permute-start(bf16[2,576,128]{2,1,0:T(8,128)(2,1)S(1)} %slice.101), channel_id=1, source_target_pairs={{0,3},{1,0},{2,1},{3,2},{4,7},{5,4},{6,5},{7,6},{8,11},{9,8},{10,9... | collective-permute-start | bytes 884744 | tf_op jit(solution)/shard_map/ppermute | solution.py:154
  131.1 17.5 %collective-permute-start.13 = (bf16[4,4,576,128]{3,2,1,0:T(8,128)(2,1)}, bf16[4,4,576,128]{3,2,1,0:T(8,128)(2,1)}, u32[]{:S(2)}, u32[]{:S(2)}) collective-permute-start(bf16[4,4,576,128]{3,2,1,0:T(8,128)(2,1)} %pad_maximum_fusion.mine_ref), channel_id=1, source_target_pairs={{0,4},{4,0},{1,5},{5,1},{2,6},{6,2},{3,7},{7,3},{8,12},{12,8},{9,1... | collective-permute-start | bytes 7077896 | tf_op jit(solution)/shard_map/ppermute | solution.py:99
  134.1 4.7 %collective-permute-start.4 = (bf16[4,768,128]{2,1,0:T(8,128)(2,1)}, bf16[4,768,128]{2,1,0:T(8,128)(2,1)S(1)}, u32[]{:S(2)}, u32[]{:S(2)}) collective-permute-start(bf16[4,768,128]{2,1,0:T(8,128)(2,1)} %get-tuple-element.56), channel_id=1, source_target_pairs={{0,4},{4,0},{1,5},{5,1},{2,6},{6,2},{3,7},{7,3},{8,12},{12,8},{9,1... | collective-permute-start | bytes 2359304 | tf_op jit(solution)/shard_map/ppermute | solution.py:99
  138.9 0.9 copy-start.3
  139.8 1.1 copy-start.4
  142.7 27.6 %copy-start.1 = (bf16[2,256,768]{2,1,0:T(8,128)(2,1)}, bf16[2,256,768]{2,1,0:T(8,128)(2,1)S(1)}, u32[]{:S(2)}) copy-start(bf16[2,256,768]{2,1,0:T(8,128)(2,1)S(1)} %embed.1.refs_0_.refs_4_) | copy-start | bytes 2359300
  142.7 21.5 %collective-permute-start.5 = (bf16[2,256,768]{2,1,0:T(8,128)(2,1)S(1)}, bf16[2,256,768]{2,1,0:T(8,128)(2,1)S(1)}, u32[]{:S(2)}, u32[]{:S(2)}) collective-permute-start(bf16[2,256,768]{2,1,0:T(8,128)(2,1)S(1)} %embed.1.refs_0_.refs_4_), channel_id=1, source_target_pairs={{0,1},{1,2},{2,3},{3,0},{4,5},{5,6},{6,7},{7,4},{8,9},{9,10},{10,1... | collective-permute-start | bytes 2359304 | tf_op jit(solution)/shard_map/ppermute | solution.py:149
  144.6 23.0 %collective-permute-start.7 = (bf16[2,256,768]{2,1,0:T(8,128)(2,1)S(1)}, bf16[2,256,768]{2,1,0:T(8,128)(2,1)S(1)}, u32[]{:S(2)}, u32[]{:S(2)}) collective-permute-start(bf16[2,256,768]{2,1,0:T(8,128)(2,1)S(1)} %embed.1.refs_0_.refs_4_), channel_id=1, source_target_pairs={{0,3},{1,0},{2,1},{3,2},{4,7},{5,4},{6,5},{7,6},{8,11},{9,8},{10,9... | collective-permute-start | bytes 2359304 | tf_op jit(solution)/shard_map/ppermute | solution.py:150
  153.1 23.3 %copy-start.2 = (bf16[4,2,96,768]{3,2,1,0:T(8,128)(2,1)}, bf16[4,2,96,768]{3,2,1,0:T(8,128)(2,1)S(1)}, u32[]{:S(2)}) copy-start(bf16[4,2,96,768]{3,2,1,0:T(8,128)(2,1)S(1)} %get-tuple-element.41) | copy-start | bytes 3538948
  164.2 20.1 %collective-permute-start.6 = (bf16[2,128,768]{2,1,0:T(8,128)(2,1)S(1)}, bf16[2,128,768]{2,1,0:T(8,128)(2,1)S(1)}, u32[]{:S(2)}, u32[]{:S(2)}) collective-permute-start(bf16[2,128,768]{2,1,0:T(8,128)(2,1)S(1)} %slice.95), channel_id=1, source_target_pairs={{0,1},{1,2},{2,3},{3,0},{4,5},{5,6},{6,7},{7,4},{8,9},{9,10},{10,1... | collective-permute-start | bytes 1179656 | tf_op jit(solution)/shard_map/ppermute | solution.py:153
  167.7 16.7 %collective-permute-start.8 = (bf16[2,128,768]{2,1,0:T(8,128)(2,1)S(1)}, bf16[2,128,768]{2,1,0:T(8,128)(2,1)S(1)}, u32[]{:S(2)}, u32[]{:S(2)}) collective-permute-start(bf16[2,128,768]{2,1,0:T(8,128)(2,1)S(1)} %slice.96), channel_id=1, source_target_pairs={{0,3},{1,0},{2,1},{3,2},{4,7},{5,4},{6,5},{7,6},{8,11},{9,8},{10,9... | collective-permute-start | bytes 1179656 | tf_op jit(solution)/shard_map/ppermute | solution.py:154
  199.7 58.6 %all-to-all-start.2 = ((bf16[128,8,384]{2,1,0:T(8,128)(2,1)}), bf16[128,8,384]{2,1,0:T(8,128)(2,1)S(1)}, u32[]{:S(2)}, u32[]{:S(2)}) async-start(bf16[128,8,384]{2,1,0:T(8,128)(2,1)} %bitcast.39), calls=%async_computation.2 | async-start | bytes 1572864 | tf_op jit(solution)/shard_map/all_to_all | solution.py:449

commit v4 on v3

--- a/solution.py
+++ b/solution.py
@@ -12,6 +12,7 @@
 HD = 64
 LANES = 128
 IMG = ("x", "z", "c")
+NEAR = 4
 VMEM_BYTES = 50 * 1024 * 1024
 
 SECTIONS = (
@@ -107,52 +108,76 @@
         ],
         axis=0,
     )
-    return lax.all_gather(packed, "z", axis=0, tiled=False)
-
-
-def order_weights(along_z):
-    toks, cores = lax.axis_size("tok"), lax.axis_size("c")
-    tok, core = lax.axis_index("tok"), lax.axis_index("c")
-    depth, packed_rows, lanes = along_z.shape
-    z_low = depth // cores
+    depth = lax.axis_size("z")
+    return jnp.stack(
+        [packed]
+        + [lax.ppermute(packed, "z", cycle(depth, NEAR * s)) for s in range(1, depth // NEAR)]
+    )
+
+
+def order_weights(far):
+    toks, cores, depth = lax.axis_size("tok"), lax.axis_size("c"), lax.axis_size("z")
+    tok, core, z = lax.axis_index("tok"), lax.axis_index("c"), lax.axis_index("z")
+    steps, packed_rows, lanes = far.shape
+    z_low, highs = depth // cores, steps // cores
+    twice = jnp.concatenate([far, far])
+
+    def half_for(other):
+        first = (z // NEAR - highs * other - (highs - 1)) % steps
+        return lax.dynamic_slice_in_dim(twice, first, highs, axis=0)
+
+    both = jnp.stack([half_for(core), swap_cores(half_for(1 - core))])
+    near = [both] + [
+        lax.ppermute(both, "z", [(i, i // NEAR * NEAR + (i + t) % NEAR) for i in range(depth)])
+        for t in range(1, NEAR)
+    ]
+    count = cores * z_low * packed_rows
+    near = jnp.stack(near).reshape(count, lanes)
+
+    def ordered(table, first_row):
+        rows, low, from_core = table
+        order = ((z - low) % NEAR * cores + (from_core - core) % cores) * highs
+        order = (order + highs - 1 - low // NEAR) * packed_rows + first_row + rows
+        mover = order[:, None] == jnp.arange(count, dtype=jnp.int32)[None, :]
+        return f32_dot(mover.astype(jnp.bfloat16), near).astype(jnp.bfloat16)
+
     first_table, _, first_rows = row_tables(SECTIONS[:1], 1, z_low, cores)
     rest_table, _, _ = row_tables(SECTIONS[1:], toks, z_low, cores)
     rest = lax.dynamic_index_in_dim(jnp.asarray(rest_table), tok, axis=1, keepdims=False)
-    rest = rest + jnp.asarray([[first_rows], [0], [0]], jnp.int32)
-    rows, low, from_core = jnp.concatenate([jnp.asarray(first_table[:, 0]), rest], axis=1)
-    mine = lax.dynamic_slice_in_dim(along_z, core * z_low, z_low, axis=0)
-    theirs = lax.dynamic_slice_in_dim(along_z, (1 - core) * z_low, z_low, axis=0)
-    both = jnp.stack([mine, swap_cores(theirs)])
-    order = ((from_core - core) % cores * z_low + low) * packed_rows + rows
-    count = cores * z_low * packed_rows
-    mover = (order[:, None] == jnp.arange(count, dtype=jnp.int32)[None, :]).astype(jnp.bfloat16)
-    ordered = f32_dot(mover, both.reshape(count, lanes)).astype(jnp.bfloat16)
-    return ordered, first_table.shape[2]
-
-
-def spread_weights(ordered, first_rows):
+    return ordered(jnp.asarray(first_table[:, 0]), 0), ordered(rest, first_rows)
+
+
+def spread_weights(first, rest):
     groups = lax.axis_size("x")
-    along_x = [ordered] + [lax.ppermute(ordered, "x", cycle(groups, s)) for s in range(1, groups)]
-    first = jnp.stack([piece[:first_rows] for piece in along_x])
-    first_full = assemble(first[None], swap_cores(first)[None], SECTIONS[:1], 1)
-    rest = jnp.stack([piece[first_rows:] for piece in along_x])
-    own, left, right, far_low, far_high = round_ring(rest, 0)
-    along_y = jnp.stack([own, left, jnp.concatenate([far_low, far_high], axis=0), right])
-    return first_full + assemble(
+
+    def along_x(value):
+        return jnp.stack(
+            [value] + [lax.ppermute(value, "x", cycle(groups, s)) for s in range(1, groups)]
+        )
+
+    rest = along_x(rest)
+    first = along_x(first)
+    first_other = swap_cores(first)
+    left, right = ring_near(rest)
+    left, right, first_other = lax.optimization_barrier((left, right, first_other))
+    far_low, far_high = ring_far(left, right, 0)
+    along_y = jnp.stack([rest, left, jnp.concatenate([far_low, far_high], axis=0), right])
+    return assemble(first[None], first_other[None], SECTIONS[:1], 1) + assemble(
         along_y, swap_cores(along_y), SECTIONS[1:], lax.axis_size("tok")
     )
 
 
-def round_ring(own, axis):
+def ring_near(own):
     count = lax.axis_size("tok")
-    half = own.shape[axis] // 2
-    from_left = lax.ppermute(own, "tok", cycle(count, 1))
-    from_right = lax.ppermute(own, "tok", cycle(count, -1))
-    low = lax.slice_in_dim(from_left, 0, half, axis=axis)
-    high = lax.slice_in_dim(from_right, half, 2 * half, axis=axis)
-    far_low = lax.ppermute(low, "tok", cycle(count, 1))
-    far_high = lax.ppermute(high, "tok", cycle(count, -1))
-    return own, from_left, from_right, far_low, far_high
+    return lax.ppermute(own, "tok", cycle(count, 1)), lax.ppermute(own, "tok", cycle(count, -1))
+
+
+def ring_far(left, right, axis):
+    count = lax.axis_size("tok")
+    half = left.shape[axis] // 2
+    low = lax.slice_in_dim(left, 0, half, axis=axis)
+    high = lax.slice_in_dim(right, half, 2 * half, axis=axis)
+    return lax.ppermute(low, "tok", cycle(count, 1)), lax.ppermute(high, "tok", cycle(count, -1))
 
 
 def assemble_kernel(places, at_ref, mine_ref, other_ref, *outs):
@@ -414,8 +439,7 @@
     parted = jnp.stack([held[:, :, x * part : (x + 1) * part] for x in range(groups)])
     parted, weight_shards = lax.optimization_barrier((parted, weight_shards))
     pieces = lax.all_to_all(parted, "x", 0, 0, tiled=True).reshape(devices, block_rows, part)
-    along_z = start_weights(weight_shards)
-    pieces, along_z = lax.optimization_barrier((pieces, along_z))
+    far = start_weights(weight_shards)
 
     bases = owner_base[pair_list]
     slot = (column - bases) % spread
@@ -424,21 +448,22 @@
     outgoing = jnp.take(pieces, place.reshape(-1), axis=0, mode="clip").reshape(
         devices, 2, block_rows, part
     )
-    ordered, first_rows = order_weights(along_z)
-    outgoing, ordered = lax.optimization_barrier((outgoing, ordered))
+    outgoing, far = lax.optimization_barrier((outgoing, far))
     arrived = lax.all_to_all(outgoing, IMG, 0, 0, tiled=True)
     arrived = arrived.reshape(groups, row_devices, 2, block_rows, part)
-    full = spread_weights(ordered, first_rows)
+    full = spread_weights(*order_weights(far))
     embed_full, project_full, self_out_full, query_full, keyval_full, cross_out_full = full
     model_width = embed_full.shape[1]
 
     embedded = embed(arrived, embed_full)
-    own, left, right, far_low, far_high = round_ring(embedded, 1)
-    near_keyval, queries, totals = self_step([own], project_full, keyval_full)
+    left, right = ring_near(embedded)
+    near_keyval, queries, totals = self_step([embedded], project_full, keyval_full)
+    left, right, totals = lax.optimization_barrier((left, right, totals))
+    far_low, far_high = ring_far(left, right, 1)
     next_keyval, totals = self_step([left, right], project_full, keyval_full, (queries, totals))
     far_keyval, after_self, cross_queries = self_step(
         [far_low, far_high], project_full, keyval_full, (queries, totals),
-        (own, self_out_full, query_full),
+        (embedded, self_out_full, query_full),
     )
 
     halves = groups // 2

time: 278 us -> 308 us (1.11)
  starting transfers between devices: 70.4 us -> 114 us
  blocking collectives: 52.7 us -> 15.4 us
  waiting for transfers between devices: 97.1 us -> 123 us
    ppermute x11 -> x20, starting transfers between devices: 33.7 us -> 80.5 us  [the longest x3 25.5 us: start_weights(): lax.ppermute(packed, 'z', cycle(depth, NEAR * s))]
    all_gather x1 -> x0, blocking collectives: 37.4 us -> none  [start_weights(): return lax.all_gather(packed, 'z', axis=0, tiled=False)]
    ppermute x11 -> x20, waiting for transfers between devices: 50.7 us -> 72.5 us  [the longest x3 41.8 us: order_weights(): lax.ppermute(both, 'z', [(i, i // NEAR * NEAR + (i + t) % NEAR) for i in...]
    all_to_all x1, waiting for transfers between devices: 0.01 us -> 6.26 us  [shards(): lax.all_to_all(parted, 'x', 0, 0, tiled=True)]
    all_to_all x1, starting transfers between devices: 12.1 us -> 7.97 us  [shards(): arrived = lax.all_to_all(outgoing, IMG, 0, 0, tiled=True)]
  transfers between devices with their start and end apart: 17 -> 26, of which waited for: 8 -> 13; matrix products, arithmetic and copies ran while one was open for 3% -> 2% of each run, Pallas kernels for 8% -> 7%
where the time goes in v4:
time: 308 us; the launch traced here: 307 us
  waiting for transfers between devices  123 us (40%)
  starting transfers between devices  114 us (37%)
  Pallas kernels  38.8 us (13%)
  blocking collectives  15.4 us (5%)
  local copies, waits for them, and re-layouts  7.13 us (2%)
  other arithmetic  5.54 us (2%)
    all_to_all x1, waiting for transfers between devices, shards(): returned = lax.all_to_all(backward, IMG, 0, 0, tiled=True)  44.1 us
    ppermute x3, waiting for transfers between devices, order_weights(): lax.ppermute(both, 'z', [(i, i // NEAR * NEAR + (i + t) % NEAR) for i in...  41.8 us
    ppermute x3, starting transfers between devices, start_weights(): lax.ppermute(packed, 'z', cycle(depth, NEAR * s))  25.5 us
    pallas_call x3, Pallas kernels, self_step(): pl.pallas_call(functools.partial(self_kernel, first, last, len(pieces)),...  22.1 us
    ppermute x6, starting transfers between devices, along_x(): lax.ppermute(value, 'x', cycle(groups, s))  20.8 us
    all_to_all x1, starting transfers between devices, shards(): returned = lax.all_to_all(backward, IMG, 0, 0, tiled=True)  15.8 us
    all_to_all x1, blocking collectives, shards(): lax.all_to_all(partial.reshape(groups, spread, block_rows, model_width //...  15.4 us
    ppermute x2, waiting for transfers between devices, ring_near(): lax.ppermute(own, 'tok', cycle(count, 1))  15 us
  transfers between devices with their start and end apart: 26, of which 13 were waited for; matrix products, arithmetic and copies ran while one was open for 2% of the time, Pallas kernels for 7%

profile of v4, /device:TPU:24, one launch (start us, length us, event | category | flops | bytes accessed | tf_op | source)
XLA Modules:
  0.0 306.6 jit_solution(1286716883992206524)
XLA Ops:
  5.4 9.1 %collective-permute-start = (bf16[84,128]{1,0:T(8,128)(2,1)S(1)}, bf16[84,128]{1,0:T(8,128)(2,1)S(1)}, u32[]{:S(2)}, u32[]{:S(2)}) collective-permute-start(bf16[84,128]{1,0:T(8,128)(2,1)S(1)} %get-tuple-element.79), channel_id=1, source_target_pairs={{0,32},{8,40},{16,48},{24,56},{32,64},{40,72},{48,80},{56,88},{64,... | collective-permute-start | bytes 64520 | tf_op jit(solution)/shard_map/ppermute | solution.py:114
  14.5 10.9 %collective-permute-start.1 = (bf16[84,128]{1,0:T(8,128)(2,1)S(1)}, bf16[84,128]{1,0:T(8,128)(2,1)S(1)}, u32[]{:S(2)}, u32[]{:S(2)}) collective-permute-start(bf16[84,128]{1,0:T(8,128)(2,1)S(1)} %get-tuple-element.79), channel_id=1, source_target_pairs={{0,64},{8,72},{16,80},{24,88},{32,96},{40,104},{48,112},{56,120},{... | collective-permute-start | bytes 64520 | tf_op jit(solution)/shard_map/ppermute | solution.py:114
  25.5 5.5 %collective-permute-start.2 = (bf16[84,128]{1,0:T(8,128)(2,1)S(1)}, bf16[84,128]{1,0:T(8,128)(2,1)S(1)}, u32[]{:S(2)}, u32[]{:S(2)}) collective-permute-start(bf16[84,128]{1,0:T(8,128)(2,1)S(1)} %get-tuple-element.79), channel_id=1, source_target_pairs={{0,96},{8,104},{16,112},{24,120},{32,0},{40,8},{48,16},{56,24},{64... | collective-permute-start | bytes 64520 | tf_op jit(solution)/shard_map/ppermute | solution.py:114
  30.9 4.3 %all-to-all-start = ((bf16[4,32,8,256]{3,2,1,0:T(8,128)(2,1)}), bf16[4,32,8,256]{3,2,1,0:T(8,128)(2,1)S(1)}, u32[]{:S(2)}, u32[]{:S(2)}) async-start(bf16[4,32,8,256]{3,2,1,0:T(8,128)(2,1)} %pad_maximum_fusion.3), calls=%async_computation | async-start | bytes 1048576 | tf_op jit(solution)/shard_map/all_to_all | solution.py:441
  37.6 6.3 %all-to-all-done = bf16[4,32,8,256]{3,2,1,0:T(8,128)(2,1)S(1)} async-done(((bf16[4,32,8,256]{3,2,1,0:T(8,128)(2,1)}), bf16[4,32,8,256]{3,2,1,0:T(8,128)(2,1)S(1)}, u32[]{:S(2)}, u32[]{:S(2)}) %all-to-all-start) | async-done | bytes 524320 | tf_op jit(solution)/shard_map/all_to_all | solution.py:441
  47.6 8.0 %all-to-all-start.1 = ((bf16[128,2,8,256]{3,2,1,0:T(8,128)(2,1)}), bf16[128,2,8,256]{3,2,1,0:T(8,128)(2,1)S(1)}, u32[]{:S(2)}, u32[]{:S(2)}) async-start(bf16[128,2,8,256]{3,2,1,0:T(8,128)(2,1)} %bitcast.10), calls=%async_computation.1 | async-start | bytes 2097152 | tf_op jit(solution)/shard_map/all_to_all | solution.py:452
  56.5 3.0 collective-permute-start.4
  59.5 4.3 %collective-permute-start.5 = (bf16[2,2,84,128]{3,2,1,0:T(8,128)(2,1)S(1)}, bf16[2,2,84,128]{3,2,1,0:T(8,128)(2,1)S(1)}, u32[]{:S(2)}, u32[]{:S(2)}) collective-permute-start(bf16[2,2,84,128]{3,2,1,0:T(8,128)(2,1)S(1)} %get-tuple-element.77), channel_id=1, source_target_pairs={{0,16},{8,24},{16,0},{24,8},{32,48},{40,56},{48,32},{56,40},{64,80... | collective-permute-start | bytes 258056 | tf_op jit(solution)/shard_map/ppermute | solution.py:131
  63.8 3.4 %collective-permute-start.6 = (bf16[2,2,84,128]{3,2,1,0:T(8,128)(2,1)S(1)}, bf16[2,2,84,128]{3,2,1,0:T(8,128)(2,1)S(1)}, u32[]{:S(2)}, u32[]{:S(2)}) collective-permute-start(bf16[2,2,84,128]{3,2,1,0:T(8,128)(2,1)S(1)} %get-tuple-element.77), channel_id=1, source_target_pairs={{0,24},{8,0},{16,8},{24,16},{32,56},{40,32},{48,40},{56,48},{64,88... | collective-permute-start | bytes 258056 | tf_op jit(solution)/shard_map/ppermute | solution.py:131
  67.2 38.1 %collective-permute-done.4 = bf16[2,2,84,128]{3,2,1,0:T(8,128)(2,1)S(1)} collective-permute-done((bf16[2,2,84,128]{3,2,1,0:T(8,128)(2,1)S(1)}, bf16[2,2,84,128]{3,2,1,0:T(8,128)(2,1)S(1)}, u32[]{:S(2)}, u32[]{:S(2)}) %collective-permute-start.4) | collective-permute-done | bytes 86048 | tf_op jit(solution)/shard_map/ppermute | solution.py:131
  105.3 3.7 %collective-permute-done.5 = bf16[2,2,84,128]{3,2,1,0:T(8,128)(2,1)S(1)} collective-permute-done((bf16[2,2,84,128]{3,2,1,0:T(8,128)(2,1)S(1)}, bf16[2,2,84,128]{3,2,1,0:T(8,128)(2,1)S(1)}, u32[]{:S(2)}, u32[]{:S(2)}) %collective-permute-start.5) | collective-permute-done | bytes 86048 | tf_op jit(solution)/shard_map/ppermute | solution.py:131
  110.0 3.4 %collective-permute-start.7 = (bf16[768,128]{1,0:T(8,128)(2,1)S(1)}, bf16[768,128]{1,0:T(8,128)(2,1)S(1)}, u32[]{:S(2)}, u32[]{:S(2)}) collective-permute-start(bf16[768,128]{1,0:T(8,128)(2,1)S(1)} %fusion.4), channel_id=1, source_target_pairs={{0,128},{128,256},{256,384},{384,0},{1,129},{129,257},{257,385},{3... | collective-permute-start | bytes 589832 | tf_op jit(solution)/shard_map/ppermute | solution.py:155
  113.4 5.0 %collective-permute-start.8 = (bf16[768,128]{1,0:T(8,128)(2,1)S(1)}, bf16[768,128]{1,0:T(8,128)(2,1)S(1)}, u32[]{:S(2)}, u32[]{:S(2)}) collective-permute-start(bf16[768,128]{1,0:T(8,128)(2,1)S(1)} %fusion.4), channel_id=1, source_target_pairs={{0,256},{128,384},{256,0},{384,128},{1,257},{129,385},{257,1},{385... | collective-permute-start | bytes 589832 | tf_op jit(solution)/shard_map/ppermute | solution.py:155
  118.5 3.2 %collective-permute-start.9 = (bf16[768,128]{1,0:T(8,128)(2,1)S(1)}, bf16[768,128]{1,0:T(8,128)(2,1)S(1)}, u32[]{:S(2)}, u32[]{:S(2)}) collective-permute-start(bf16[768,128]{1,0:T(8,128)(2,1)S(1)} %fusion.4), channel_id=1, source_target_pairs={{0,384},{128,0},{256,128},{384,256},{1,385},{129,1},{257,129},{385... | collective-permute-start | bytes 589832 | tf_op jit(solution)/shard_map/ppermute | solution.py:155
  127.7 3.9 %collective-permute-start.12 = (bf16[576,128]{1,0:T(8,128)(2,1)S(1)}, bf16[576,128]{1,0:T(8,128)(2,1)S(1)}, u32[]{:S(2)}, u32[]{:S(2)}) collective-permute-start(bf16[576,128]{1,0:T(8,128)(2,1)S(1)} %fusion.5), channel_id=1, source_target_pairs={{0,384},{128,0},{256,128},{384,256},{1,385},{129,1},{257,129},{385... | collective-permute-start | bytes 442376 | tf_op jit(solution)/shard_map/ppermute | solution.py:155
  137.7 3.7 %collective-permute-start.14 = (bf16[4,576,128]{2,1,0:T(8,128)(2,1)S(1)}, bf16[4,576,128]{2,1,0:T(8,128)(2,1)S(1)}, u32[]{:S(2)}, u32[]{:S(2)}) collective-permute-start(bf16[4,576,128]{2,1,0:T(8,128)(2,1)S(1)} %get-tuple-element.67), channel_id=1, source_target_pairs={{0,3},{1,0},{2,1},{3,2},{4,7},{5,4},{6,5},{7,6},{8,11},{9,8},{10,9... | collective-permute-start | bytes 1769480 | tf_op jit(solution)/shard_map/ppermute | solution.py:172
  141.4 10.0 %collective-permute-done.13 = bf16[4,576,128]{2,1,0:T(8,128)(2,1)S(1)} collective-permute-done((bf16[4,576,128]{2,1,0:T(8,128)(2,1)S(1)}, bf16[4,576,128]{2,1,0:T(8,128)(2,1)S(1)}, u32[]{:S(2)}, u32[]{:S(2)}) %collective-permute-start.13) | collective-permute-done | bytes 589856 | tf_op jit(solution)/shard_map/ppermute | solution.py:172
  151.4 3.1 %collective-permute-done.14 = bf16[4,576,128]{2,1,0:T(8,128)(2,1)S(1)} collective-permute-done((bf16[4,576,128]{2,1,0:T(8,128)(2,1)S(1)}, bf16[4,576,128]{2,1,0:T(8,128)(2,1)S(1)}, u32[]{:S(2)}, u32[]{:S(2)}) %collective-permute-start.14) | collective-permute-done | bytes 589856 | tf_op jit(solution)/shard_map/ppermute | solution.py:172
  156.8 3.6 %collective-permute-start.19 = (bf16[2,576,128]{2,1,0:T(8,128)(2,1)S(1)}, bf16[2,576,128]{2,1,0:T(8,128)(2,1)S(1)}, u32[]{:S(2)}, u32[]{:S(2)}) collective-permute-start(bf16[2,576,128]{2,1,0:T(8,128)(2,1)S(1)} %slice.48), channel_id=1, source_target_pairs={{0,3},{1,0},{2,1},{3,2},{4,7},{5,4},{6,5},{7,6},{8,11},{9,8},{10,9... | collective-permute-start | bytes 884744 | tf_op jit(solution)/shard_map/ppermute | solution.py:180
  163.2 3.5 %collective-permute-done.19 = bf16[2,576,128]{2,1,0:T(8,128)(2,1)S(1)} collective-permute-done((bf16[2,576,128]{2,1,0:T(8,128)(2,1)S(1)}, bf16[2,576,128]{2,1,0:T(8,128)(2,1)S(1)}, u32[]{:S(2)}, u32[]{:S(2)}) %collective-permute-start.19) | collective-permute-done | bytes 294944 | tf_op jit(solution)/shard_map/ppermute | solution.py:180
  175.7 3.6 %collective-permute-start.17 = (bf16[2,256,768]{2,1,0:T(8,128)(2,1)S(1)}, bf16[2,256,768]{2,1,0:T(8,128)(2,1)S(1)}, u32[]{:S(2)}, u32[]{:S(2)}) collective-permute-start(bf16[2,256,768]{2,1,0:T(8,128)(2,1)S(1)} %embed.1.refs_0_.refs_4_), channel_id=1, source_target_pairs={{0,3},{1,0},{2,1},{3,2},{4,7},{5,4},{6,5},{7,6},{8,11},{9,8},{10,9... | collective-permute-start | bytes 2359304 | tf_op jit(solution)/shard_map/ppermute | solution.py:172
  179.3 4.5 %assemble.3 = (bf16[4,2,96,1152]{3,2,1,0:T(8,128)(2,1)}, bf16[4,2,48,768]{3,2,1,0:T(8,128)(2,1)S(1)}, bf16[4,2,96,384]{3,2,1,0:T(8,128)(2,1)S(1)}, bf16[4,2,96,7...) custom-call(s32[3]{0:T(128)S(1)} %pad_add_fusion.at_ref, bf16[4,4,576,128]{3,2,1,0:T(8,128)(2,1)} %pad_maximum_fusion.mine_ref, ...), custom_call_target="tpu_custom_call" | custom-call | bytes 9437184 | tf_op jit(solution)/shard_map/assemble/pallas_call | solution.py:208
  183.7 6.5 %self_step.3 = (bf16[2,256,768]{2,1,0:T(8,128)(2,1)S(1)}, bf16[2,256,384]{2,1,0:T(8,128)(2,1)S(1)}, f32[2,6,256,128]{3,2,1,0:T(8,128)}) custom-call(bf16[2,256,768]{2,1,0:T(8,128)(2,1)S(1)} %embed.1.refs_0_.refs_4_, bf16[768,1152]{1,0:T(8,128)(2,1)} %bitcast.80, bf16[768,768]{1,0:T(8,128)(2,1)S(1)} %bitcast.70), custom_call_target="tpu_custom_call" | custom-call | flops 1610612736 | bytes 3735552 | tf_op jit(solution)/shard_map/self_step/pallas_call | solution.py:371
  190.2 5.0 %collective-permute-done.16.refs_0_ = bf16[2,256,768]{2,1,0:T(8,128)(2,1)S(1)} collective-permute-done((bf16[2,256,768]{2,1,0:T(8,128)(2,1)S(1)}, bf16[2,256,768]{2,1,0:T(8,128)(2,1)S(1)}, u32[]{:S(2)}, u32[]{:S(2)}) %collective-permute-start.16) | collective-permute-done | bytes 786464 | tf_op jit(solution)/shard_map/ppermute | solution.py:172
  195.2 3.2 %collective-permute-done.17.refs_1_ = bf16[2,256,768]{2,1,0:T(8,128)(2,1)S(1)} collective-permute-done((bf16[2,256,768]{2,1,0:T(8,128)(2,1)S(1)}, bf16[2,256,768]{2,1,0:T(8,128)(2,1)S(1)}, u32[]{:S(2)}, u32[]{:S(2)}) %collective-permute-start.17) | collective-permute-done | bytes 786464 | tf_op jit(solution)/shard_map/ppermute | solution.py:172
  200.5 4.0 %collective-permute-start.22 = (bf16[2,128,768]{2,1,0:T(8,128)(2,1)S(1)}, bf16[2,128,768]{2,1,0:T(8,128)(2,1)S(1)}, u32[]{:S(2)}, u32[]{:S(2)}) collective-permute-start(bf16[2,128,768]{2,1,0:T(8,128)(2,1)S(1)} %slice.50), channel_id=1, source_target_pairs={{0,3},{1,0},{2,1},{3,2},{4,7},{5,4},{6,5},{7,6},{8,11},{9,8},{10,9... | collective-permute-start | bytes 1179656 | tf_op jit(solution)/shard_map/ppermute | solution.py:180
  204.5 8.0 %self_step.4 = (bf16[2,512,768]{2,1,0:T(8,128)(2,1)}, f32[2,6,256,128]{3,2,1,0:T(8,128)}) custom-call(bf16[2,256,768]{2,1,0:T(8,128)(2,1)S(1)} %collective-permute-done.16.refs_0_, bf16[2,256,768]{2,1,0:T(8,128)(2,1)S(1)} %collective-permute-done.17.refs_1_, bf16[2,256,384]{2,1,0:T(8,128)(2,1)S(1)} %get-tuple-element.50.refs_2_, ...), custom_call_target="tpu_custom_call" | custom-call | flops 3221225472 | bytes 6488064 | tf_op jit(solution)/shard_map/self_step/pallas_call | solution.py:371
  213.9 7.6 %self_step.5 = (bf16[2,256,768]{2,1,0:T(8,128)(2,1)S(1)}, f32[2,256,768]{2,1,0:T(8,128)}, bf16[2,256,384]{2,1,0:T(8,128)(2,1)S(1)}) custom-call(bf16[2,128,768]{2,1,0:T(8,128)(2,1)S(1)} %collective-permute-done.21.refs_0_, bf16[2,128,768]{2,1,0:T(8,128)(2,1)S(1)} %collective-permute-done.22.refs_1_, bf16[2,256,384]{2,1,0:T(8,128)(2,1)S(1)} %get-tuple-element.50.refs_2_, ...), custom_call_target="tpu_custom_call" | custom-call | flops 1610612736 | bytes 7667712 | tf_op jit(solution)/shard_map/self_step/pallas_call | solution.py:371
  221.6 7.8 %cross_block.1 = bf16[2,2,32,8,384]{4,3,2,1,0:T(8,128)(2,1)} custom-call(f32[2,256,768]{2,1,0:T(8,128)} %get-tuple-element.55.after_ref, bf16[2,256,384]{2,1,0:T(8,128)(2,1)S(1)} %get-tuple-element.56.query_ref, bf16[2,256,768]{2,1,0:T(8,128)(2,1)S(1)} %get-tuple-element.57.refs_0_, bf16[2,512,768]{2,1,0:T(8,128)(2,1)} %get-tuple-element.58.refs_1_, ...), custom_call_target="tpu_custom_call" | custom-call | flops 1912602624 | bytes 3342336 | tf_op jit(solution)/shard_map/cross_block/pallas_call | solution.py:409
  229.3 15.8 %all-to-all-start.2 = ((bf16[128,8,384]{2,1,0:T(8,128)(2,1)}), bf16[128,8,384]{2,1,0:T(8,128)(2,1)S(1)}, u32[]{:S(2)}, u32[]{:S(2)}) async-start(bf16[128,8,384]{2,1,0:T(8,128)(2,1)} %bitcast.45), calls=%async_computation.2 | async-start | bytes 1572864 | tf_op jit(solution)/shard_map/all_to_all | solution.py:474
  245.4 44.1 %all-to-all-done.2 = bf16[128,8,384]{2,1,0:T(8,128)(2,1)S(1)} async-done(((bf16[128,8,384]{2,1,0:T(8,128)(2,1)}), bf16[128,8,384]{2,1,0:T(8,128)(2,1)S(1)}, u32[]{:S(2)}, u32[]{:S(2)}) %all-to-all-start.2) | async-done | bytes 786464 | tf_op jit(solution)/shard_map/all_to_all | solution.py:474
  290.3 15.4 %all_to_all.20 = bf16[4,32,8,384]{3,2,1,0:T(8,128)(2,1)S(1)} all-to-all(bf16[4,32,8,384]{3,2,1,0:T(8,128)(2,1)S(1)} %copy.43), channel_id=1, replica_groups=mesh['x'=4,'z'=16,'c'=2,'tok'=4] {'x'}, dimensions={0} | all-to-all | bytes 1572864 | tf_op jit(solution)/shard_map/all_to_all | solution.py:483
  (92 shorter events, 44.7 us)
Async XLA Ops:
  0.0 35.5 %copy-start = (s32[128]{0:T(128)S(1)}, s32[128]{0:T(128)}, u32[]{:S(2)}) copy-start(s32[128]{0:T(128)} %param.13) | copy-start | bytes 1540
  0.0 35.2 %copy-start.9 = (s32[128,2]{0,1:T(2,128)S(1)}, s32[128,2]{0,1:T(2,128)}, u32[]{:S(2)}) copy-start(s32[128,2]{0,1:T(2,128)} %param.12) | copy-start | bytes 3076
  5.4 32.1 %collective-permute-start = (bf16[84,128]{1,0:T(8,128)(2,1)S(1)}, bf16[84,128]{1,0:T(8,128)(2,1)S(1)}, u32[]{:S(2)}, u32[]{:S(2)}) collective-permute-start(bf16[84,128]{1,0:T(8,128)(2,1)S(1)} %get-tuple-element.79), channel_id=1, source_target_pairs={{0,32},{8,40},{16,48},{24,56},{32,64},{40,72},{48,80},{56,88},{64,... | collective-permute-start | bytes 64520 | tf_op jit(solution)/shard_map/ppermute | solution.py:114
  14.5 23.0 %collective-permute-start.1 = (bf16[84,128]{1,0:T(8,128)(2,1)S(1)}, bf16[84,128]{1,0:T(8,128)(2,1)S(1)}, u32[]{:S(2)}, u32[]{:S(2)}) collective-permute-start(bf16[84,128]{1,0:T(8,128)(2,1)S(1)} %get-tuple-element.79), channel_id=1, source_target_pairs={{0,64},{8,72},{16,80},{24,88},{32,96},{40,104},{48,112},{56,120},{... | collective-permute-start | bytes 64520 | tf_op jit(solution)/shard_map/ppermute | solution.py:114
  25.5 12.1 %collective-permute-start.2 = (bf16[84,128]{1,0:T(8,128)(2,1)S(1)}, bf16[84,128]{1,0:T(8,128)(2,1)S(1)}, u32[]{:S(2)}, u32[]{:S(2)}) collective-permute-start(bf16[84,128]{1,0:T(8,128)(2,1)S(1)} %get-tuple-element.79), channel_id=1, source_target_pairs={{0,96},{8,104},{16,112},{24,120},{32,0},{40,8},{48,16},{56,24},{64... | collective-permute-start | bytes 64520 | tf_op jit(solution)/shard_map/ppermute | solution.py:114
  30.9 12.9 %all-to-all-start = ((bf16[4,32,8,256]{3,2,1,0:T(8,128)(2,1)}), bf16[4,32,8,256]{3,2,1,0:T(8,128)(2,1)S(1)}, u32[]{:S(2)}, u32[]{:S(2)}) async-start(bf16[4,32,8,256]{3,2,1,0:T(8,128)(2,1)} %pad_maximum_fusion.3), calls=%async_computation | async-start | bytes 1048576 | tf_op jit(solution)/shard_map/all_to_all | solution.py:441
  43.9 11.7 %copy-start.6 = (s32[768]{0:T(1024)S(1)}, s32[768]{0:T(1024)}, u32[]{:S(2)}) copy-start(s32[768]{0:T(1024)} %constant.206) | copy-start | bytes 9220
  43.9 11.8 %copy-start.7 = (s32[768]{0:T(1024)S(1)}, s32[768]{0:T(1024)}, u32[]{:S(2)}) copy-start(s32[768]{0:T(1024)} %constant.207) | copy-start | bytes 9220
  45.7 10.7 %collective-permute-start.3 = (bf16[2,84,128]{2,1,0:T(8,128)(2,1)S(1)}, bf16[2,84,128]{2,1,0:T(8,128)(2,1)S(1)}, u32[]{:S(2)}, u32[]{:S(2)}) collective-permute-start(bf16[2,84,128]{2,1,0:T(8,128)(2,1)S(1)} %get-tuple-element.75), channel_id=1, source_target_pairs={{0,4},{4,0},{1,5},{5,1},{2,6},{6,2},{3,7},{7,3},{8,12},{12,8},{9,1... | collective-permute-start | bytes 129032 | tf_op jit(solution)/shard_map/ppermute | solution.py:100
  47.6 124.8 %all-to-all-start.1 = ((bf16[128,2,8,256]{3,2,1,0:T(8,128)(2,1)}), bf16[128,2,8,256]{3,2,1,0:T(8,128)(2,1)S(1)}, u32[]{:S(2)}, u32[]{:S(2)}) async-start(bf16[128,2,8,256]{3,2,1,0:T(8,128)(2,1)} %bitcast.10), calls=%async_computation.1 | async-start | bytes 2097152 | tf_op jit(solution)/shard_map/all_to_all | solution.py:452
  56.5 48.9 %collective-permute-start.4 = (bf16[2,2,84,128]{3,2,1,0:T(8,128)(2,1)S(1)}, bf16[2,2,84,128]{3,2,1,0:T(8,128)(2,1)S(1)}, u32[]{:S(2)}, u32[]{:S(2)}) collective-permute-start(bf16[2,2,84,128]{3,2,1,0:T(8,128)(2,1)S(1)} %get-tuple-element.77), channel_id=1, source_target_pairs={{0,8},{8,16},{16,24},{24,0},{32,40},{40,48},{48,56},{56,32},{64,72... | collective-permute-start | bytes 258056 | tf_op jit(solution)/shard_map/ppermute | solution.py:131
  59.5 49.5 %collective-permute-start.5 = (bf16[2,2,84,128]{3,2,1,0:T(8,128)(2,1)S(1)}, bf16[2,2,84,128]{3,2,1,0:T(8,128)(2,1)S(1)}, u32[]{:S(2)}, u32[]{:S(2)}) collective-permute-start(bf16[2,2,84,128]{3,2,1,0:T(8,128)(2,1)S(1)} %get-tuple-element.77), channel_id=1, source_target_pairs={{0,16},{8,24},{16,0},{24,8},{32,48},{40,56},{48,32},{56,40},{64,80... | collective-permute-start | bytes 258056 | tf_op jit(solution)/shard_map/ppermute | solution.py:131
  63.8 45.2 %collective-permute-start.6 = (bf16[2,2,84,128]{3,2,1,0:T(8,128)(2,1)S(1)}, bf16[2,2,84,128]{3,2,1,0:T(8,128)(2,1)S(1)}, u32[]{:S(2)}, u32[]{:S(2)}) collective-permute-start(bf16[2,2,84,128]{3,2,1,0:T(8,128)(2,1)S(1)} %get-tuple-element.77), channel_id=1, source_target_pairs={{0,24},{8,0},{16,8},{24,16},{32,56},{40,32},{48,40},{56,48},{64,88... | collective-permute-start | bytes 258056 | tf_op jit(solution)/shard_map/ppermute | solution.py:131
  110.0 17.6 %collective-permute-start.7 = (bf16[768,128]{1,0:T(8,128)(2,1)S(1)}, bf16[768,128]{1,0:T(8,128)(2,1)S(1)}, u32[]{:S(2)}, u32[]{:S(2)}) collective-permute-start(bf16[768,128]{1,0:T(8,128)(2,1)S(1)} %fusion.4), channel_id=1, source_target_pairs={{0,128},{128,256},{256,384},{384,0},{1,129},{129,257},{257,385},{3... | collective-permute-start | bytes 589832 | tf_op jit(solution)/shard_map/ppermute | solution.py:155
  113.4 18.1 %collective-permute-start.8 = (bf16[768,128]{1,0:T(8,128)(2,1)S(1)}, bf16[768,128]{1,0:T(8,128)(2,1)S(1)}, u32[]{:S(2)}, u32[]{:S(2)}) collective-permute-start(bf16[768,128]{1,0:T(8,128)(2,1)S(1)} %fusion.4), channel_id=1, source_target_pairs={{0,256},{128,384},{256,0},{384,128},{1,257},{129,385},{257,1},{385... | collective-permute-start | bytes 589832 | tf_op jit(solution)/shard_map/ppermute | solution.py:155
  118.5 13.1 %collective-permute-start.9 = (bf16[768,128]{1,0:T(8,128)(2,1)S(1)}, bf16[768,128]{1,0:T(8,128)(2,1)S(1)}, u32[]{:S(2)}, u32[]{:S(2)}) collective-permute-start(bf16[768,128]{1,0:T(8,128)(2,1)S(1)} %fusion.4), channel_id=1, source_target_pairs={{0,384},{128,0},{256,128},{384,256},{1,385},{129,1},{257,129},{385... | collective-permute-start | bytes 589832 | tf_op jit(solution)/shard_map/ppermute | solution.py:155
  122.3 11.4 %collective-permute-start.10 = (bf16[576,128]{1,0:T(8,128)(2,1)S(1)}, bf16[576,128]{1,0:T(8,128)(2,1)S(1)}, u32[]{:S(2)}, u32[]{:S(2)}) collective-permute-start(bf16[576,128]{1,0:T(8,128)(2,1)S(1)} %fusion.5), channel_id=1, source_target_pairs={{0,128},{128,256},{256,384},{384,0},{1,129},{129,257},{257,385},{3... | collective-permute-start | bytes 442376 | tf_op jit(solution)/shard_map/ppermute | solution.py:155
  125.0 8.7 %collective-permute-start.11 = (bf16[576,128]{1,0:T(8,128)(2,1)S(1)}, bf16[576,128]{1,0:T(8,128)(2,1)S(1)}, u32[]{:S(2)}, u32[]{:S(2)}) collective-permute-start(bf16[576,128]{1,0:T(8,128)(2,1)S(1)} %fusion.5), channel_id=1, source_target_pairs={{0,256},{128,384},{256,0},{384,128},{1,257},{129,385},{257,1},{385... | collective-permute-start | bytes 442376 | tf_op jit(solution)/shard_map/ppermute | solution.py:155
  127.7 7.8 %collective-permute-start.12 = (bf16[576,128]{1,0:T(8,128)(2,1)S(1)}, bf16[576,128]{1,0:T(8,128)(2,1)S(1)}, u32[]{:S(2)}, u32[]{:S(2)}) collective-permute-start(bf16[576,128]{1,0:T(8,128)(2,1)S(1)} %fusion.5), channel_id=1, source_target_pairs={{0,384},{128,0},{256,128},{384,256},{1,385},{129,1},{257,129},{385... | collective-permute-start | bytes 442376 | tf_op jit(solution)/shard_map/ppermute | solution.py:155
  131.7 22.8 %collective-permute-start.15 = (bf16[4,768,128]{2,1,0:T(8,128)(2,1)S(1)}, bf16[4,768,128]{2,1,0:T(8,128)(2,1)S(1)}, u32[]{:S(2)}, u32[]{:S(2)}) collective-permute-start(bf16[4,768,128]{2,1,0:T(8,128)(2,1)S(1)} %get-tuple-element.64), channel_id=1, source_target_pairs={{0,4},{4,0},{1,5},{5,1},{2,6},{6,2},{3,7},{7,3},{8,12},{12,8},{9,1... | collective-permute-start | bytes 2359304 | tf_op jit(solution)/shard_map/ppermute | solution.py:100
  135.6 15.9 %collective-permute-start.13 = (bf16[4,576,128]{2,1,0:T(8,128)(2,1)S(1)}, bf16[4,576,128]{2,1,0:T(8,128)(2,1)S(1)}, u32[]{:S(2)}, u32[]{:S(2)}) collective-permute-start(bf16[4,576,128]{2,1,0:T(8,128)(2,1)S(1)} %get-tuple-element.67), channel_id=1, source_target_pairs={{0,1},{1,2},{2,3},{3,0},{4,5},{5,6},{6,7},{7,4},{8,9},{9,10},{10,1... | collective-permute-start | bytes 1769480 | tf_op jit(solution)/shard_map/ppermute | solution.py:172
  137.7 16.8 %collective-permute-start.14 = (bf16[4,576,128]{2,1,0:T(8,128)(2,1)S(1)}, bf16[4,576,128]{2,1,0:T(8,128)(2,1)S(1)}, u32[]{:S(2)}, u32[]{:S(2)}) collective-permute-start(bf16[4,576,128]{2,1,0:T(8,128)(2,1)S(1)} %get-tuple-element.67), channel_id=1, source_target_pairs={{0,3},{1,0},{2,1},{3,2},{4,7},{5,4},{6,5},{7,6},{8,11},{9,8},{10,9... | collective-permute-start | bytes 1769480 | tf_op jit(solution)/shard_map/ppermute | solution.py:172
  154.6 13.9 %copy-start.3 = (bf16[4,768,128]{2,1,0:T(8,128)(2,1)}, bf16[4,768,128]{2,1,0:T(8,128)(2,1)S(1)}, u32[]{:S(2)}) copy-start(bf16[4,768,128]{2,1,0:T(8,128)(2,1)S(1)} %collective-permute-done.15) | copy-start | bytes 2359300
  154.6 8.6 %collective-permute-start.18 = (bf16[2,576,128]{2,1,0:T(8,128)(2,1)S(1)}, bf16[2,576,128]{2,1,0:T(8,128)(2,1)S(1)}, u32[]{:S(2)}, u32[]{:S(2)}) collective-permute-start(bf16[2,576,128]{2,1,0:T(8,128)(2,1)S(1)} %slice.47), channel_id=1, source_target_pairs={{0,1},{1,2},{2,3},{3,0},{4,5},{5,6},{6,7},{7,4},{8,9},{9,10},{10,1... | collective-permute-start | bytes 884744 | tf_op jit(solution)/shard_map/ppermute | solution.py:180
  156.8 9.8 %collective-permute-start.19 = (bf16[2,576,128]{2,1,0:T(8,128)(2,1)S(1)}, bf16[2,576,128]{2,1,0:T(8,128)(2,1)S(1)}, u32[]{:S(2)}, u32[]{:S(2)}) collective-permute-start(bf16[2,576,128]{2,1,0:T(8,128)(2,1)S(1)} %slice.48), channel_id=1, source_target_pairs={{0,3},{1,0},{2,1},{3,2},{4,7},{5,4},{6,5},{7,6},{8,11},{9,8},{10,9... | collective-permute-start | bytes 884744 | tf_op jit(solution)/shard_map/ppermute | solution.py:180
  168.4 10.8 %collective-permute-start.20 = (bf16[4,4,576,128]{3,2,1,0:T(8,128)(2,1)}, bf16[4,4,576,128]{3,2,1,0:T(8,128)(2,1)}, u32[]{:S(2)}, u32[]{:S(2)}) collective-permute-start(bf16[4,4,576,128]{3,2,1,0:T(8,128)(2,1)} %pad_maximum_fusion.mine_ref), channel_id=1, source_target_pairs={{0,4},{4,0},{1,5},{5,1},{2,6},{6,2},{3,7},{7,3},{8,12},{12,8},{9,1... | collective-permute-start | bytes 7077896 | tf_op jit(solution)/shard_map/ppermute | solution.py:100
  173.4 21.8 %collective-permute-start.16 = (bf16[2,256,768]{2,1,0:T(8,128)(2,1)S(1)}, bf16[2,256,768]{2,1,0:T(8,128)(2,1)S(1)}, u32[]{:S(2)}, u32[]{:S(2)}) collective-permute-start(bf16[2,256,768]{2,1,0:T(8,128)(2,1)S(1)} %embed.1.refs_0_.refs_4_), channel_id=1, source_target_pairs={{0,1},{1,2},{2,3},{3,0},{4,5},{5,6},{6,7},{7,4},{8,9},{9,10},{10,1... | collective-permute-start | bytes 2359304 | tf_op jit(solution)/shard_map/ppermute | solution.py:172
  175.7 22.8 %collective-permute-start.17 = (bf16[2,256,768]{2,1,0:T(8,128)(2,1)S(1)}, bf16[2,256,768]{2,1,0:T(8,128)(2,1)S(1)}, u32[]{:S(2)}, u32[]{:S(2)}) collective-permute-start(bf16[2,256,768]{2,1,0:T(8,128)(2,1)S(1)} %embed.1.refs_0_.refs_4_), channel_id=1, source_target_pairs={{0,3},{1,0},{2,1},{3,2},{4,7},{5,4},{6,5},{7,6},{8,11},{9,8},{10,9... | collective-permute-start | bytes 2359304 | tf_op jit(solution)/shard_map/ppermute | solution.py:172
  183.7 20.8 %copy-start.2 = (bf16[4,2,96,768]{3,2,1,0:T(8,128)(2,1)}, bf16[4,2,96,768]{3,2,1,0:T(8,128)(2,1)S(1)}, u32[]{:S(2)}) copy-start(bf16[4,2,96,768]{3,2,1,0:T(8,128)(2,1)S(1)} %get-tuple-element.46) | copy-start | bytes 3538948
  198.5 14.1 %collective-permute-start.21 = (bf16[2,128,768]{2,1,0:T(8,128)(2,1)S(1)}, bf16[2,128,768]{2,1,0:T(8,128)(2,1)S(1)}, u32[]{:S(2)}, u32[]{:S(2)}) collective-permute-start(bf16[2,128,768]{2,1,0:T(8,128)(2,1)S(1)} %slice.49), channel_id=1, source_target_pairs={{0,1},{1,2},{2,3},{3,0},{4,5},{5,6},{6,7},{7,4},{8,9},{9,10},{10,1... | collective-permute-start | bytes 1179656 | tf_op jit(solution)/shard_map/ppermute | solution.py:180
  200.5 13.5 %collective-permute-start.22 = (bf16[2,128,768]{2,1,0:T(8,128)(2,1)S(1)}, bf16[2,128,768]{2,1,0:T(8,128)(2,1)S(1)}, u32[]{:S(2)}, u32[]{:S(2)}) collective-permute-start(bf16[2,128,768]{2,1,0:T(8,128)(2,1)S(1)} %slice.50), channel_id=1, source_target_pairs={{0,3},{1,0},{2,1},{3,2},{4,7},{5,4},{6,5},{7,6},{8,11},{9,8},{10,9... | collective-permute-start | bytes 1179656 | tf_op jit(solution)/shard_map/ppermute | solution.py:180
  229.3 60.2 %all-to-all-start.2 = ((bf16[128,8,384]{2,1,0:T(8,128)(2,1)}), bf16[128,8,384]{2,1,0:T(8,128)(2,1)S(1)}, u32[]{:S(2)}, u32[]{:S(2)}) async-start(bf16[128,8,384]{2,1,0:T(8,128)(2,1)} %bitcast.45), calls=%async_computation.2 | async-start | bytes 1572864 | tf_op jit(solution)/shard_map/all_to_all | solution.py:474
  (4 other events, 25.2 us)

commit v5 on v4

--- a/solution.py
+++ b/solution.py
@@ -115,11 +115,11 @@
     )
 
 
-def order_weights(far):
-    toks, cores, depth = lax.axis_size("tok"), lax.axis_size("c"), lax.axis_size("z")
-    tok, core, z = lax.axis_index("tok"), lax.axis_index("c"), lax.axis_index("z")
-    steps, packed_rows, lanes = far.shape
-    z_low, highs = depth // cores, steps // cores
+def near_weights(far):
+    cores, depth = lax.axis_size("c"), lax.axis_size("z")
+    core, z = lax.axis_index("c"), lax.axis_index("z")
+    steps = far.shape[0]
+    highs = steps // cores
     twice = jnp.concatenate([far, far])
 
     def half_for(other):
@@ -131,34 +131,37 @@
         lax.ppermute(both, "z", [(i, i // NEAR * NEAR + (i + t) % NEAR) for i in range(depth)])
         for t in range(1, NEAR)
     ]
+    return jnp.stack(near)
+
+
+def order_weights(near):
+    toks, cores, depth = lax.axis_size("tok"), lax.axis_size("c"), lax.axis_size("z")
+    tok, core, z = lax.axis_index("tok"), lax.axis_index("c"), lax.axis_index("z")
+    _, _, highs, packed_rows, lanes = near.shape
+    z_low = depth // cores
     count = cores * z_low * packed_rows
-    near = jnp.stack(near).reshape(count, lanes)
-
-    def ordered(table, first_row):
-        rows, low, from_core = table
-        order = ((z - low) % NEAR * cores + (from_core - core) % cores) * highs
-        order = (order + highs - 1 - low // NEAR) * packed_rows + first_row + rows
-        mover = order[:, None] == jnp.arange(count, dtype=jnp.int32)[None, :]
-        return f32_dot(mover.astype(jnp.bfloat16), near).astype(jnp.bfloat16)
+    near = near.reshape(count, lanes)
 
     first_table, _, first_rows = row_tables(SECTIONS[:1], 1, z_low, cores)
     rest_table, _, _ = row_tables(SECTIONS[1:], toks, z_low, cores)
     rest = lax.dynamic_index_in_dim(jnp.asarray(rest_table), tok, axis=1, keepdims=False)
-    return ordered(jnp.asarray(first_table[:, 0]), 0), ordered(rest, first_rows)
-
-
-def spread_weights(first, rest):
-    groups = lax.axis_size("x")
-
-    def along_x(value):
-        return jnp.stack(
-            [value] + [lax.ppermute(value, "x", cycle(groups, s)) for s in range(1, groups)]
-        )
-
-    rest = along_x(rest)
-    first = along_x(first)
+    rest = rest + jnp.asarray([[first_rows], [0], [0]], jnp.int32)
+    rows, low, from_core = jnp.concatenate([jnp.asarray(first_table[:, 0]), rest], axis=1)
+    order = ((z - low) % NEAR * cores + (from_core - core) % cores) * highs
+    order = (order + highs - 1 - low // NEAR) * packed_rows + rows
+    mover = order[:, None] == jnp.arange(count, dtype=jnp.int32)[None, :]
+    ordered = f32_dot(mover.astype(jnp.bfloat16), near).astype(jnp.bfloat16)
+    return ordered, first_table.shape[2]
+
+
+def spread_weights(ordered, first_rows):
+    left, right = near_on_ring(ordered, "x")
+    far_first = pass_on(left[:first_rows], "x", 1)
+    far_rest = pass_on(right[first_rows:], "x", -1)
+    first = jnp.stack([ordered[:first_rows], left[:first_rows], far_first, right[:first_rows]])
+    rest = jnp.stack([ordered[first_rows:], left[first_rows:], far_rest, right[first_rows:]])
     first_other = swap_cores(first)
-    left, right = ring_near(rest)
+    left, right = near_on_ring(rest, "tok")
     left, right, first_other = lax.optimization_barrier((left, right, first_other))
     far_low, far_high = ring_far(left, right, 0)
     along_y = jnp.stack([rest, left, jnp.concatenate([far_low, far_high], axis=0), right])
@@ -167,17 +170,19 @@
     )
 
 
-def ring_near(own):
-    count = lax.axis_size("tok")
-    return lax.ppermute(own, "tok", cycle(count, 1)), lax.ppermute(own, "tok", cycle(count, -1))
+def pass_on(value, axis, shift):
+    return lax.ppermute(value, axis, cycle(lax.axis_size(axis), shift))
+
+
+def near_on_ring(own, axis):
+    return pass_on(own, axis, 1), pass_on(own, axis, -1)
 
 
 def ring_far(left, right, axis):
-    count = lax.axis_size("tok")
     half = left.shape[axis] // 2
     low = lax.slice_in_dim(left, 0, half, axis=axis)
     high = lax.slice_in_dim(right, half, 2 * half, axis=axis)
-    return lax.ppermute(low, "tok", cycle(count, 1)), lax.ppermute(high, "tok", cycle(count, -1))
+    return pass_on(low, "tok", 1), pass_on(high, "tok", -1)
 
 
 def assemble_kernel(places, at_ref, mine_ref, other_ref, *outs):
@@ -448,15 +453,15 @@
     outgoing = jnp.take(pieces, place.reshape(-1), axis=0, mode="clip").reshape(
         devices, 2, block_rows, part
     )
-    outgoing, far = lax.optimization_barrier((outgoing, far))
+    outgoing, near = lax.optimization_barrier((outgoing, near_weights(far)))
     arrived = lax.all_to_all(outgoing, IMG, 0, 0, tiled=True)
     arrived = arrived.reshape(groups, row_devices, 2, block_rows, part)
-    full = spread_weights(*order_weights(far))
+    full = spread_weights(*order_weights(near))
     embed_full, project_full, self_out_full, query_full, keyval_full, cross_out_full = full
     model_width = embed_full.shape[1]
 
     embedded = embed(arrived, embed_full)
-    left, right = ring_near(embedded)
+    left, right = near_on_ring(embedded, "tok")
     near_keyval, queries, totals = self_step([embedded], project_full, keyval_full)
     left, right, totals = lax.optimization_barrier((left, right, totals))
     far_low, far_high = ring_far(left, right, 1)

time: 308 us -> 269 us (0.87)
  waiting for transfers between devices: 123 us -> 90.3 us
  starting transfers between devices: 114 us -> 107 us
    ppermute x17 -> x15, waiting for transfers between devices: 72.5 us -> 45 us  [the longest x12 41.2 us: pass_on(): return lax.ppermute(value, axis, cycle(lax.axis_size(axis), shift))]
    ppermute x17 -> x15, starting transfers between devices: 55 us -> 47.4 us  [the longest x12 37.3 us: pass_on(): return lax.ppermute(value, axis, cycle(lax.axis_size(axis), shift))]
    all_to_all x1, waiting for transfers between devices: 6.26 us -> 0.01 us  [shards(): lax.all_to_all(parted, 'x', 0, 0, tiled=True)]
  transfers between devices with their start and end apart: 26 -> 24, of which waited for: 13 -> 12; matrix products, arithmetic and copies ran while one was open for 2% -> 2% of each run, Pallas kernels for 7% -> 8%
where the time goes in v5:
time: 269 us; the launch traced here: 268 us
  starting transfers between devices  107 us (40%)
  waiting for transfers between devices  90.3 us (34%)
  Pallas kernels  38.9 us (14%)
  blocking collectives  15.4 us (6%)
  local copies, waits for them, and re-layouts  7.27 us (3%)
  other arithmetic  6.29 us (2%)
    all_to_all x1, waiting for transfers between devices, shards(): returned = lax.all_to_all(backward, IMG, 0, 0, tiled=True)  44.1 us
    ppermute x12, waiting for transfers between devices, pass_on(): return lax.ppermute(value, axis, cycle(lax.axis_size(axis), shift))  41.2 us
    ppermute x12, starting transfers between devices, pass_on(): return lax.ppermute(value, axis, cycle(lax.axis_size(axis), shift))  37.3 us
    ppermute x3, starting transfers between devices, start_weights(): lax.ppermute(packed, 'z', cycle(depth, NEAR * s))  25.5 us
    pallas_call x3, Pallas kernels, self_step(): pl.pallas_call(functools.partial(self_kernel, first, last, len(pieces)),...  22.2 us
    all_to_all x1, blocking collectives, shards(): lax.all_to_all(partial.reshape(groups, spread, block_rows, model_width //...  15.4 us
    all_to_all x1, starting transfers between devices, shards(): returned = lax.all_to_all(backward, IMG, 0, 0, tiled=True)  13.9 us
    all_to_all x1, starting transfers between devices, shards(): arrived = lax.all_to_all(outgoing, IMG, 0, 0, tiled=True)  10.4 us
  transfers between devices with their start and end apart: 24, of which 12 were waited for; matrix products, arithmetic and copies ran while one was open for 2% of the time, Pallas kernels for 8%

profile of v5, /device:TPU:24, one launch (start us, length us, event | category | flops | bytes accessed | tf_op | source)
XLA Modules:
  0.0 267.9 jit_solution(3633826677603737605)
XLA Ops:
  5.5 9.1 %collective-permute-start = (bf16[84,128]{1,0:T(8,128)(2,1)S(1)}, bf16[84,128]{1,0:T(8,128)(2,1)S(1)}, u32[]{:S(2)}, u32[]{:S(2)}) collective-permute-start(bf16[84,128]{1,0:T(8,128)(2,1)S(1)} %pad_maximum_fusion.7), channel_id=1, source_target_pairs={{0,32},{8,40},{16,48},{24,56},{32,64},{40,72},{48,80},{56,88},{64,... | collective-permute-start | bytes 64520 | tf_op jit(solution)/shard_map/ppermute | solution.py:114
  14.5 10.9 %collective-permute-start.1 = (bf16[84,128]{1,0:T(8,128)(2,1)S(1)}, bf16[84,128]{1,0:T(8,128)(2,1)S(1)}, u32[]{:S(2)}, u32[]{:S(2)}) collective-permute-start(bf16[84,128]{1,0:T(8,128)(2,1)S(1)} %pad_maximum_fusion.7), channel_id=1, source_target_pairs={{0,64},{8,72},{16,80},{24,88},{32,96},{40,104},{48,112},{56,120},{... | collective-permute-start | bytes 64520 | tf_op jit(solution)/shard_map/ppermute | solution.py:114
  25.5 5.5 %collective-permute-start.2 = (bf16[84,128]{1,0:T(8,128)(2,1)S(1)}, bf16[84,128]{1,0:T(8,128)(2,1)S(1)}, u32[]{:S(2)}, u32[]{:S(2)}) collective-permute-start(bf16[84,128]{1,0:T(8,128)(2,1)S(1)} %pad_maximum_fusion.7), channel_id=1, source_target_pairs={{0,96},{8,104},{16,112},{24,120},{32,0},{40,8},{48,16},{56,24},{64... | collective-permute-start | bytes 64520 | tf_op jit(solution)/shard_map/ppermute | solution.py:114
  30.9 4.3 %all-to-all-start = ((bf16[4,32,8,256]{3,2,1,0:T(8,128)(2,1)}), bf16[4,32,8,256]{3,2,1,0:T(8,128)(2,1)S(1)}, u32[]{:S(2)}, u32[]{:S(2)}) async-start(bf16[4,32,8,256]{3,2,1,0:T(8,128)(2,1)} %pad_maximum_fusion.3), calls=%async_computation | async-start | bytes 1048576 | tf_op jit(solution)/shard_map/all_to_all | solution.py:446
  42.4 2.9 %collective-permute-start.4 = (bf16[2,2,84,128]{3,2,1,0:T(8,128)(2,1)S(1)}, bf16[2,2,84,128]{3,2,1,0:T(8,128)(2,1)S(1)}, u32[]{:S(2)}, u32[]{:S(2)}) collective-permute-start(bf16[2,2,84,128]{3,2,1,0:T(8,128)(2,1)S(1)} %get-tuple-element.81), channel_id=1, source_target_pairs={{0,8},{8,16},{16,24},{24,0},{32,40},{40,48},{48,56},{56,32},{64,72... | collective-permute-start | bytes 258056 | tf_op jit(solution)/shard_map/ppermute | solution.py:131
  45.3 3.4 %collective-permute-start.5 = (bf16[2,2,84,128]{3,2,1,0:T(8,128)(2,1)S(1)}, bf16[2,2,84,128]{3,2,1,0:T(8,128)(2,1)S(1)}, u32[]{:S(2)}, u32[]{:S(2)}) collective-permute-start(bf16[2,2,84,128]{3,2,1,0:T(8,128)(2,1)S(1)} %get-tuple-element.81), channel_id=1, source_target_pairs={{0,16},{8,24},{16,0},{24,8},{32,48},{40,56},{48,32},{56,40},{64,80... | collective-permute-start | bytes 258056 | tf_op jit(solution)/shard_map/ppermute | solution.py:131
  48.7 3.8 %collective-permute-start.6 = (bf16[2,2,84,128]{3,2,1,0:T(8,128)(2,1)S(1)}, bf16[2,2,84,128]{3,2,1,0:T(8,128)(2,1)S(1)}, u32[]{:S(2)}, u32[]{:S(2)}) collective-permute-start(bf16[2,2,84,128]{3,2,1,0:T(8,128)(2,1)S(1)} %get-tuple-element.81), channel_id=1, source_target_pairs={{0,24},{8,0},{16,8},{24,16},{32,56},{40,32},{48,40},{56,48},{64,88... | collective-permute-start | bytes 258056 | tf_op jit(solution)/shard_map/ppermute | solution.py:131
  52.6 2.4 collective-permute-done.5
  59.8 5.1 %collective-permute-start.9 = (bf16[1344,128]{1,0:T(8,128)(2,1)S(1)}, bf16[1344,128]{1,0:T(8,128)(2,1)S(1)}, u32[]{:S(2)}, u32[]{:S(2)}) collective-permute-start(bf16[1344,128]{1,0:T(8,128)(2,1)S(1)} %fusion.2), channel_id=1, source_target_pairs={{0,384},{128,0},{256,128},{384,256},{1,385},{129,1},{257,129},{385... | collective-permute-start | bytes 1032200 | tf_op jit(solution)/shard_map/ppermute | solution.py:174
  66.9 10.4 %all-to-all-start.1 = ((bf16[128,2,8,256]{3,2,1,0:T(8,128)(2,1)}), bf16[128,2,8,256]{3,2,1,0:T(8,128)(2,1)S(1)}, u32[]{:S(2)}, u32[]{:S(2)}) async-start(bf16[128,2,8,256]{3,2,1,0:T(8,128)(2,1)} %bitcast.10), calls=%async_computation.1 | async-start | bytes 2097152 | tf_op jit(solution)/shard_map/all_to_all | solution.py:457
  77.4 4.8 %collective-permute-start.10 = (bf16[576,128]{1,0:T(8,128)(2,1)S(1)}, bf16[576,128]{1,0:T(8,128)(2,1)S(1)}, u32[]{:S(2)}, u32[]{:S(2)}) collective-permute-start(bf16[576,128]{1,0:T(8,128)(2,1)S(1)} %get-tuple-element.74), channel_id=1, source_target_pairs={{0,384},{128,0},{256,128},{384,256},{1,385},{129,1},{257,129},{385... | collective-permute-start | bytes 442376 | tf_op jit(solution)/shard_map/ppermute | solution.py:174
  84.2 9.2 %collective-permute-done.8 = bf16[768,128]{1,0:T(8,128)(2,1)S(1)} collective-permute-done((bf16[768,128]{1,0:T(8,128)(2,1)S(1)}, bf16[768,128]{1,0:T(8,128)(2,1)S(1)}, u32[]{:S(2)}, u32[]{:S(2)}) %collective-permute-start.8) | collective-permute-done | bytes 196640 | tf_op jit(solution)/shard_map/ppermute | solution.py:174
  97.7 3.7 %collective-permute-start.12 = (bf16[4,576,128]{2,1,0:T(8,128)(2,1)S(1)}, bf16[4,576,128]{2,1,0:T(8,128)(2,1)S(1)}, u32[]{:S(2)}, u32[]{:S(2)}) collective-permute-start(bf16[4,576,128]{2,1,0:T(8,128)(2,1)S(1)} %get-tuple-element.67), channel_id=1, source_target_pairs={{0,3},{1,0},{2,1},{3,2},{4,7},{5,4},{6,5},{7,6},{8,11},{9,8},{10,9... | collective-permute-start | bytes 1769480 | tf_op jit(solution)/shard_map/ppermute | solution.py:174
  101.5 11.8 %collective-permute-done.11 = bf16[4,576,128]{2,1,0:T(8,128)(2,1)S(1)} collective-permute-done((bf16[4,576,128]{2,1,0:T(8,128)(2,1)S(1)}, bf16[4,576,128]{2,1,0:T(8,128)(2,1)S(1)}, u32[]{:S(2)}, u32[]{:S(2)}) %collective-permute-start.11) | collective-permute-done | bytes 589856 | tf_op jit(solution)/shard_map/ppermute | solution.py:174
  113.2 3.1 %collective-permute-done.12 = bf16[4,576,128]{2,1,0:T(8,128)(2,1)S(1)} collective-permute-done((bf16[4,576,128]{2,1,0:T(8,128)(2,1)S(1)}, bf16[4,576,128]{2,1,0:T(8,128)(2,1)S(1)}, u32[]{:S(2)}, u32[]{:S(2)}) %collective-permute-start.12) | collective-permute-done | bytes 589856 | tf_op jit(solution)/shard_map/ppermute | solution.py:174
  116.4 2.2 collective-permute-start.16
  118.6 3.6 %collective-permute-start.17 = (bf16[2,576,128]{2,1,0:T(8,128)(2,1)S(1)}, bf16[2,576,128]{2,1,0:T(8,128)(2,1)S(1)}, u32[]{:S(2)}, u32[]{:S(2)}) collective-permute-start(bf16[2,576,128]{2,1,0:T(8,128)(2,1)S(1)} %slice.71), channel_id=1, source_target_pairs={{0,3},{1,0},{2,1},{3,2},{4,7},{5,4},{6,5},{7,6},{8,11},{9,8},{10,9... | collective-permute-start | bytes 884744 | tf_op jit(solution)/shard_map/ppermute | solution.py:174
  122.3 4.4 %collective-permute-done.16 = bf16[2,576,128]{2,1,0:T(8,128)(2,1)S(1)} collective-permute-done((bf16[2,576,128]{2,1,0:T(8,128)(2,1)S(1)}, bf16[2,576,128]{2,1,0:T(8,128)(2,1)S(1)}, u32[]{:S(2)}, u32[]{:S(2)}) %collective-permute-start.16) | collective-permute-done | bytes 294944 | tf_op jit(solution)/shard_map/ppermute | solution.py:174
  126.7 3.2 %collective-permute-done.17 = bf16[2,576,128]{2,1,0:T(8,128)(2,1)S(1)} collective-permute-done((bf16[2,576,128]{2,1,0:T(8,128)(2,1)S(1)}, bf16[2,576,128]{2,1,0:T(8,128)(2,1)S(1)}, u32[]{:S(2)}, u32[]{:S(2)}) %collective-permute-start.17) | collective-permute-done | bytes 294944 | tf_op jit(solution)/shard_map/ppermute | solution.py:174
  136.6 2.2 collective-permute-start.14
  138.8 3.6 %collective-permute-start.15 = (bf16[2,256,768]{2,1,0:T(8,128)(2,1)S(1)}, bf16[2,256,768]{2,1,0:T(8,128)(2,1)S(1)}, u32[]{:S(2)}, u32[]{:S(2)}) collective-permute-start(bf16[2,256,768]{2,1,0:T(8,128)(2,1)S(1)} %embed.1.refs_0_.refs_4_), channel_id=1, source_target_pairs={{0,3},{1,0},{2,1},{3,2},{4,7},{5,4},{6,5},{7,6},{8,11},{9,8},{10,9... | collective-permute-start | bytes 2359304 | tf_op jit(solution)/shard_map/ppermute | solution.py:174
  142.5 4.5 %assemble.3 = (bf16[4,2,96,1152]{3,2,1,0:T(8,128)(2,1)}, bf16[4,2,48,768]{3,2,1,0:T(8,128)(2,1)S(1)}, bf16[4,2,96,384]{3,2,1,0:T(8,128)(2,1)S(1)}, bf16[4,2,96,7...) custom-call(s32[3]{0:T(128)S(1)} %pad_add_fusion.1.at_ref, bf16[4,4,576,128]{3,2,1,0:T(8,128)(2,1)} %pad_maximum_fusion.mine_ref, ...), custom_call_target="tpu_custom_call" | custom-call | bytes 9437184 | tf_op jit(solution)/shard_map/assemble/pallas_call | solution.py:213
  146.9 6.5 %self_step.3 = (bf16[2,256,768]{2,1,0:T(8,128)(2,1)S(1)}, bf16[2,256,384]{2,1,0:T(8,128)(2,1)S(1)}, f32[2,6,256,128]{3,2,1,0:T(8,128)}) custom-call(bf16[2,256,768]{2,1,0:T(8,128)(2,1)S(1)} %embed.1.refs_0_.refs_4_, bf16[768,1152]{1,0:T(8,128)(2,1)} %bitcast.94, bf16[768,768]{1,0:T(8,128)(2,1)S(1)} %bitcast.84), custom_call_target="tpu_custom_call" | custom-call | flops 1610612736 | bytes 3735552 | tf_op jit(solution)/shard_map/self_step/pallas_call | solution.py:376
  153.4 5.0 %collective-permute-done.14.refs_0_ = bf16[2,256,768]{2,1,0:T(8,128)(2,1)S(1)} collective-permute-done((bf16[2,256,768]{2,1,0:T(8,128)(2,1)S(1)}, bf16[2,256,768]{2,1,0:T(8,128)(2,1)S(1)}, u32[]{:S(2)}, u32[]{:S(2)}) %collective-permute-start.14) | collective-permute-done | bytes 786464 | tf_op jit(solution)/shard_map/ppermute | solution.py:174
  158.4 3.1 %collective-permute-done.15.refs_1_ = bf16[2,256,768]{2,1,0:T(8,128)(2,1)S(1)} collective-permute-done((bf16[2,256,768]{2,1,0:T(8,128)(2,1)S(1)}, bf16[2,256,768]{2,1,0:T(8,128)(2,1)S(1)}, u32[]{:S(2)}, u32[]{:S(2)}) %collective-permute-start.15) | collective-permute-done | bytes 786464 | tf_op jit(solution)/shard_map/ppermute | solution.py:174
  163.6 4.0 %collective-permute-start.20 = (bf16[2,128,768]{2,1,0:T(8,128)(2,1)S(1)}, bf16[2,128,768]{2,1,0:T(8,128)(2,1)S(1)}, u32[]{:S(2)}, u32[]{:S(2)}) collective-permute-start(bf16[2,128,768]{2,1,0:T(8,128)(2,1)S(1)} %slice.73), channel_id=1, source_target_pairs={{0,3},{1,0},{2,1},{3,2},{4,7},{5,4},{6,5},{7,6},{8,11},{9,8},{10,9... | collective-permute-start | bytes 1179656 | tf_op jit(solution)/shard_map/ppermute | solution.py:174
  167.7 8.1 %self_step.4 = (bf16[2,512,768]{2,1,0:T(8,128)(2,1)}, f32[2,6,256,128]{3,2,1,0:T(8,128)}) custom-call(bf16[2,256,768]{2,1,0:T(8,128)(2,1)S(1)} %collective-permute-done.14.refs_0_, bf16[2,256,768]{2,1,0:T(8,128)(2,1)S(1)} %collective-permute-done.15.refs_1_, bf16[2,256,384]{2,1,0:T(8,128)(2,1)S(1)} %get-tuple-element.50.refs_2_, ...), custom_call_target="tpu_custom_call" | custom-call | flops 3221225472 | bytes 6488064 | tf_op jit(solution)/shard_map/self_step/pallas_call | solution.py:376
  177.1 7.6 %self_step.5 = (bf16[2,256,768]{2,1,0:T(8,128)(2,1)S(1)}, f32[2,256,768]{2,1,0:T(8,128)}, bf16[2,256,384]{2,1,0:T(8,128)(2,1)S(1)}) custom-call(bf16[2,128,768]{2,1,0:T(8,128)(2,1)S(1)} %collective-permute-done.19.refs_0_, bf16[2,128,768]{2,1,0:T(8,128)(2,1)S(1)} %collective-permute-done.20.refs_1_, bf16[2,256,384]{2,1,0:T(8,128)(2,1)S(1)} %get-tuple-element.50.refs_2_, ...), custom_call_target="tpu_custom_call" | custom-call | flops 1610612736 | bytes 7667712 | tf_op jit(solution)/shard_map/self_step/pallas_call | solution.py:376
  184.7 7.8 %cross_block.1 = bf16[2,2,32,8,384]{4,3,2,1,0:T(8,128)(2,1)} custom-call(f32[2,256,768]{2,1,0:T(8,128)} %get-tuple-element.55.after_ref, bf16[2,256,384]{2,1,0:T(8,128)(2,1)S(1)} %get-tuple-element.56.query_ref, bf16[2,256,768]{2,1,0:T(8,128)(2,1)S(1)} %get-tuple-element.57.refs_0_, bf16[2,512,768]{2,1,0:T(8,128)(2,1)} %get-tuple-element.58.refs_1_, ...), custom_call_target="tpu_custom_call" | custom-call | flops 1912602624 | bytes 3342336 | tf_op jit(solution)/shard_map/cross_block/pallas_call | solution.py:414
  192.5 13.9 %all-to-all-start.2 = ((bf16[128,8,384]{2,1,0:T(8,128)(2,1)}), bf16[128,8,384]{2,1,0:T(8,128)(2,1)S(1)}, u32[]{:S(2)}, u32[]{:S(2)}) async-start(bf16[128,8,384]{2,1,0:T(8,128)(2,1)} %bitcast.46), calls=%async_computation.2 | async-start | bytes 1572864 | tf_op jit(solution)/shard_map/all_to_all | solution.py:479
  206.6 44.1 %all-to-all-done.2 = bf16[128,8,384]{2,1,0:T(8,128)(2,1)S(1)} async-done(((bf16[128,8,384]{2,1,0:T(8,128)(2,1)}), bf16[128,8,384]{2,1,0:T(8,128)(2,1)S(1)}, u32[]{:S(2)}, u32[]{:S(2)}) %all-to-all-start.2) | async-done | bytes 786464 | tf_op jit(solution)/shard_map/all_to_all | solution.py:479
  251.6 15.4 %all_to_all.20 = bf16[4,32,8,384]{3,2,1,0:T(8,128)(2,1)S(1)} all-to-all(bf16[4,32,8,384]{3,2,1,0:T(8,128)(2,1)S(1)} %copy.44), channel_id=1, replica_groups=mesh['x'=4,'z'=16,'c'=2,'tok'=4] {'x'}, dimensions={0} | all-to-all | bytes 1572864 | tf_op jit(solution)/shard_map/all_to_all | solution.py:488
  (97 shorter events, 37.5 us)
Async XLA Ops:
  0.0 37.2 %copy-start = (s32[128]{0:T(128)S(1)}, s32[128]{0:T(128)}, u32[]{:S(2)}) copy-start(s32[128]{0:T(128)} %param.14) | copy-start | bytes 1540
  0.0 36.2 %copy-start.9 = (s32[3]{0:T(128)S(1)}, s32[3]{0:T(128)}, u32[]{:S(2)}) copy-start(s32[3]{0:T(128)} %constant.160) | copy-start | bytes 40
  0.0 37.0 %copy-start.7 = (s32[3,768]{1,0:T(4,128)S(1)}, s32[3,768]{1,0:T(4,128)}, u32[]{:S(2)}) copy-start(s32[3,768]{1,0:T(4,128)} %constant.152.clone) | copy-start | bytes 27652
  0.0 36.0 %copy-start.8 = (s32[128,2]{0,1:T(2,128)S(1)}, s32[128,2]{0,1:T(2,128)}, u32[]{:S(2)}) copy-start(s32[128,2]{0,1:T(2,128)} %param.13) | copy-start | bytes 3076
  5.5 33.6 %collective-permute-start = (bf16[84,128]{1,0:T(8,128)(2,1)S(1)}, bf16[84,128]{1,0:T(8,128)(2,1)S(1)}, u32[]{:S(2)}, u32[]{:S(2)}) collective-permute-start(bf16[84,128]{1,0:T(8,128)(2,1)S(1)} %pad_maximum_fusion.7), channel_id=1, source_target_pairs={{0,32},{8,40},{16,48},{24,56},{32,64},{40,72},{48,80},{56,88},{64,... | collective-permute-start | bytes 64520 | tf_op jit(solution)/shard_map/ppermute | solution.py:114
  14.5 24.6 %collective-permute-start.1 = (bf16[84,128]{1,0:T(8,128)(2,1)S(1)}, bf16[84,128]{1,0:T(8,128)(2,1)S(1)}, u32[]{:S(2)}, u32[]{:S(2)}) collective-permute-start(bf16[84,128]{1,0:T(8,128)(2,1)S(1)} %pad_maximum_fusion.7), channel_id=1, source_target_pairs={{0,64},{8,72},{16,80},{24,88},{32,96},{40,104},{48,112},{56,120},{... | collective-permute-start | bytes 64520 | tf_op jit(solution)/shard_map/ppermute | solution.py:114
  25.5 13.7 %collective-permute-start.2 = (bf16[84,128]{1,0:T(8,128)(2,1)S(1)}, bf16[84,128]{1,0:T(8,128)(2,1)S(1)}, u32[]{:S(2)}, u32[]{:S(2)}) collective-permute-start(bf16[84,128]{1,0:T(8,128)(2,1)S(1)} %pad_maximum_fusion.7), channel_id=1, source_target_pairs={{0,96},{8,104},{16,112},{24,120},{32,0},{40,8},{48,16},{56,24},{64... | collective-permute-start | bytes 64520 | tf_op jit(solution)/shard_map/ppermute | solution.py:114
  30.9 25.6 %all-to-all-start = ((bf16[4,32,8,256]{3,2,1,0:T(8,128)(2,1)}), bf16[4,32,8,256]{3,2,1,0:T(8,128)(2,1)S(1)}, u32[]{:S(2)}, u32[]{:S(2)}) async-start(bf16[4,32,8,256]{3,2,1,0:T(8,128)(2,1)} %pad_maximum_fusion.3), calls=%async_computation | async-start | bytes 1048576 | tf_op jit(solution)/shard_map/all_to_all | solution.py:446
  37.2 2.0 copy-start.5
  39.3 3.1 %collective-permute-start.3 = (bf16[2,84,128]{2,1,0:T(8,128)(2,1)S(1)}, bf16[2,84,128]{2,1,0:T(8,128)(2,1)S(1)}, u32[]{:S(2)}, u32[]{:S(2)}) collective-permute-start(bf16[2,84,128]{2,1,0:T(8,128)(2,1)S(1)} %get-tuple-element.79), channel_id=1, source_target_pairs={{0,4},{4,0},{1,5},{5,1},{2,6},{6,2},{3,7},{7,3},{8,12},{12,8},{9,1... | collective-permute-start | bytes 129032 | tf_op jit(solution)/shard_map/ppermute | solution.py:100
  42.4 10.2 %collective-permute-start.4 = (bf16[2,2,84,128]{3,2,1,0:T(8,128)(2,1)S(1)}, bf16[2,2,84,128]{3,2,1,0:T(8,128)(2,1)S(1)}, u32[]{:S(2)}, u32[]{:S(2)}) collective-permute-start(bf16[2,2,84,128]{3,2,1,0:T(8,128)(2,1)S(1)} %get-tuple-element.81), channel_id=1, source_target_pairs={{0,8},{8,16},{16,24},{24,0},{32,40},{40,48},{48,56},{56,32},{64,72... | collective-permute-start | bytes 258056 | tf_op jit(solution)/shard_map/ppermute | solution.py:131
  45.3 9.6 %collective-permute-start.5 = (bf16[2,2,84,128]{3,2,1,0:T(8,128)(2,1)S(1)}, bf16[2,2,84,128]{3,2,1,0:T(8,128)(2,1)S(1)}, u32[]{:S(2)}, u32[]{:S(2)}) collective-permute-start(bf16[2,2,84,128]{3,2,1,0:T(8,128)(2,1)S(1)} %get-tuple-element.81), channel_id=1, source_target_pairs={{0,16},{8,24},{16,0},{24,8},{32,48},{40,56},{48,32},{56,40},{64,80... | collective-permute-start | bytes 258056 | tf_op jit(solution)/shard_map/ppermute | solution.py:131
  48.7 7.7 %collective-permute-start.6 = (bf16[2,2,84,128]{3,2,1,0:T(8,128)(2,1)S(1)}, bf16[2,2,84,128]{3,2,1,0:T(8,128)(2,1)S(1)}, u32[]{:S(2)}, u32[]{:S(2)}) collective-permute-start(bf16[2,2,84,128]{3,2,1,0:T(8,128)(2,1)S(1)} %get-tuple-element.81), channel_id=1, source_target_pairs={{0,24},{8,0},{16,8},{24,16},{32,56},{40,32},{48,40},{56,48},{64,88... | collective-permute-start | bytes 258056 | tf_op jit(solution)/shard_map/ppermute | solution.py:131
  59.8 17.6 %collective-permute-start.9 = (bf16[1344,128]{1,0:T(8,128)(2,1)S(1)}, bf16[1344,128]{1,0:T(8,128)(2,1)S(1)}, u32[]{:S(2)}, u32[]{:S(2)}) collective-permute-start(bf16[1344,128]{1,0:T(8,128)(2,1)S(1)} %fusion.2), channel_id=1, source_target_pairs={{0,384},{128,0},{256,128},{384,256},{1,385},{129,1},{257,129},{385... | collective-permute-start | bytes 1032200 | tf_op jit(solution)/shard_map/ppermute | solution.py:174
  64.9 17.2 %collective-permute-start.7 = (bf16[1344,128]{1,0:T(8,128)(2,1)S(1)}, bf16[1344,128]{1,0:T(8,128)(2,1)S(1)}, u32[]{:S(2)}, u32[]{:S(2)}) collective-permute-start(bf16[1344,128]{1,0:T(8,128)(2,1)S(1)} %fusion.2), channel_id=1, source_target_pairs={{0,128},{128,256},{256,384},{384,0},{1,129},{129,257},{257,385},{3... | collective-permute-start | bytes 1032200 | tf_op jit(solution)/shard_map/ppermute | solution.py:174
  66.9 68.7 %all-to-all-start.1 = ((bf16[128,2,8,256]{3,2,1,0:T(8,128)(2,1)}), bf16[128,2,8,256]{3,2,1,0:T(8,128)(2,1)S(1)}, u32[]{:S(2)}, u32[]{:S(2)}) async-start(bf16[128,2,8,256]{3,2,1,0:T(8,128)(2,1)} %bitcast.10), calls=%async_computation.1 | async-start | bytes 2097152 | tf_op jit(solution)/shard_map/all_to_all | solution.py:457
  77.4 18.1 %collective-permute-start.10 = (bf16[576,128]{1,0:T(8,128)(2,1)S(1)}, bf16[576,128]{1,0:T(8,128)(2,1)S(1)}, u32[]{:S(2)}, u32[]{:S(2)}) collective-permute-start(bf16[576,128]{1,0:T(8,128)(2,1)S(1)} %get-tuple-element.74), channel_id=1, source_target_pairs={{0,384},{128,0},{256,128},{384,256},{1,385},{129,1},{257,129},{385... | collective-permute-start | bytes 442376 | tf_op jit(solution)/shard_map/ppermute | solution.py:174
  82.2 11.2 %collective-permute-start.8 = (bf16[768,128]{1,0:T(8,128)(2,1)S(1)}, bf16[768,128]{1,0:T(8,128)(2,1)S(1)}, u32[]{:S(2)}, u32[]{:S(2)}) collective-permute-start(bf16[768,128]{1,0:T(8,128)(2,1)S(1)} %get-tuple-element.77), channel_id=1, source_target_pairs={{0,128},{128,256},{256,384},{384,0},{1,129},{129,257},{257,385},{3... | collective-permute-start | bytes 589832 | tf_op jit(solution)/shard_map/ppermute | solution.py:174
  93.5 22.8 %collective-permute-start.13 = (bf16[4,768,128]{2,1,0:T(8,128)(2,1)S(1)}, bf16[4,768,128]{2,1,0:T(8,128)(2,1)S(1)}, u32[]{:S(2)}, u32[]{:S(2)}) collective-permute-start(bf16[4,768,128]{2,1,0:T(8,128)(2,1)S(1)} %get-tuple-element.64), channel_id=1, source_target_pairs={{0,4},{4,0},{1,5},{5,1},{2,6},{6,2},{3,7},{7,3},{8,12},{12,8},{9,1... | collective-permute-start | bytes 2359304 | tf_op jit(solution)/shard_map/ppermute | solution.py:100
  95.6 17.6 %collective-permute-start.11 = (bf16[4,576,128]{2,1,0:T(8,128)(2,1)S(1)}, bf16[4,576,128]{2,1,0:T(8,128)(2,1)S(1)}, u32[]{:S(2)}, u32[]{:S(2)}) collective-permute-start(bf16[4,576,128]{2,1,0:T(8,128)(2,1)S(1)} %get-tuple-element.67), channel_id=1, source_target_pairs={{0,1},{1,2},{2,3},{3,0},{4,5},{5,6},{6,7},{7,4},{8,9},{9,10},{10,1... | collective-permute-start | bytes 1769480 | tf_op jit(solution)/shard_map/ppermute | solution.py:174
  97.7 18.6 %collective-permute-start.12 = (bf16[4,576,128]{2,1,0:T(8,128)(2,1)S(1)}, bf16[4,576,128]{2,1,0:T(8,128)(2,1)S(1)}, u32[]{:S(2)}, u32[]{:S(2)}) collective-permute-start(bf16[4,576,128]{2,1,0:T(8,128)(2,1)S(1)} %get-tuple-element.67), channel_id=1, source_target_pairs={{0,3},{1,0},{2,1},{3,2},{4,7},{5,4},{6,5},{7,6},{8,11},{9,8},{10,9... | collective-permute-start | bytes 1769480 | tf_op jit(solution)/shard_map/ppermute | solution.py:174
  116.4 15.3 %copy-start.3 = (bf16[4,768,128]{2,1,0:T(8,128)(2,1)}, bf16[4,768,128]{2,1,0:T(8,128)(2,1)S(1)}, u32[]{:S(2)}) copy-start(bf16[4,768,128]{2,1,0:T(8,128)(2,1)S(1)} %collective-permute-done.13) | copy-start | bytes 2359300
  116.4 10.3 %collective-permute-start.16 = (bf16[2,576,128]{2,1,0:T(8,128)(2,1)S(1)}, bf16[2,576,128]{2,1,0:T(8,128)(2,1)S(1)}, u32[]{:S(2)}, u32[]{:S(2)}) collective-permute-start(bf16[2,576,128]{2,1,0:T(8,128)(2,1)S(1)} %slice.70), channel_id=1, source_target_pairs={{0,1},{1,2},{2,3},{3,0},{4,5},{5,6},{6,7},{7,4},{8,9},{9,10},{10,1... | collective-permute-start | bytes 884744 | tf_op jit(solution)/shard_map/ppermute | solution.py:174
  118.6 11.2 %collective-permute-start.17 = (bf16[2,576,128]{2,1,0:T(8,128)(2,1)S(1)}, bf16[2,576,128]{2,1,0:T(8,128)(2,1)S(1)}, u32[]{:S(2)}, u32[]{:S(2)}) collective-permute-start(bf16[2,576,128]{2,1,0:T(8,128)(2,1)S(1)} %slice.71), channel_id=1, source_target_pairs={{0,3},{1,0},{2,1},{3,2},{4,7},{5,4},{6,5},{7,6},{8,11},{9,8},{10,9... | collective-permute-start | bytes 884744 | tf_op jit(solution)/shard_map/ppermute | solution.py:174
  131.6 10.8 %collective-permute-start.18 = (bf16[4,4,576,128]{3,2,1,0:T(8,128)(2,1)}, bf16[4,4,576,128]{3,2,1,0:T(8,128)(2,1)}, u32[]{:S(2)}, u32[]{:S(2)}) collective-permute-start(bf16[4,4,576,128]{3,2,1,0:T(8,128)(2,1)} %pad_maximum_fusion.mine_ref), channel_id=1, source_target_pairs={{0,4},{4,0},{1,5},{5,1},{2,6},{6,2},{3,7},{7,3},{8,12},{12,8},{9,1... | collective-permute-start | bytes 7077896 | tf_op jit(solution)/shard_map/ppermute | solution.py:100
  136.6 10.4 %copy-start.1 = (bf16[2,256,768]{2,1,0:T(8,128)(2,1)}, bf16[2,256,768]{2,1,0:T(8,128)(2,1)S(1)}, u32[]{:S(2)}) copy-start(bf16[2,256,768]{2,1,0:T(8,128)(2,1)S(1)} %embed.1.refs_0_.refs_4_) | copy-start | bytes 2359300
  136.6 21.8 %collective-permute-start.14 = (bf16[2,256,768]{2,1,0:T(8,128)(2,1)S(1)}, bf16[2,256,768]{2,1,0:T(8,128)(2,1)S(1)}, u32[]{:S(2)}, u32[]{:S(2)}) collective-permute-start(bf16[2,256,768]{2,1,0:T(8,128)(2,1)S(1)} %embed.1.refs_0_.refs_4_), channel_id=1, source_target_pairs={{0,1},{1,2},{2,3},{3,0},{4,5},{5,6},{6,7},{7,4},{8,9},{9,10},{10,1... | collective-permute-start | bytes 2359304 | tf_op jit(solution)/shard_map/ppermute | solution.py:174
  138.8 22.8 %collective-permute-start.15 = (bf16[2,256,768]{2,1,0:T(8,128)(2,1)S(1)}, bf16[2,256,768]{2,1,0:T(8,128)(2,1)S(1)}, u32[]{:S(2)}, u32[]{:S(2)}) collective-permute-start(bf16[2,256,768]{2,1,0:T(8,128)(2,1)S(1)} %embed.1.refs_0_.refs_4_), channel_id=1, source_target_pairs={{0,3},{1,0},{2,1},{3,2},{4,7},{5,4},{6,5},{7,6},{8,11},{9,8},{10,9... | collective-permute-start | bytes 2359304 | tf_op jit(solution)/shard_map/ppermute | solution.py:174
  146.9 20.7 %copy-start.2 = (bf16[4,2,96,768]{3,2,1,0:T(8,128)(2,1)}, bf16[4,2,96,768]{3,2,1,0:T(8,128)(2,1)S(1)}, u32[]{:S(2)}) copy-start(bf16[4,2,96,768]{3,2,1,0:T(8,128)(2,1)S(1)} %get-tuple-element.46) | copy-start | bytes 3538948
  161.6 14.2 %collective-permute-start.19 = (bf16[2,128,768]{2,1,0:T(8,128)(2,1)S(1)}, bf16[2,128,768]{2,1,0:T(8,128)(2,1)S(1)}, u32[]{:S(2)}, u32[]{:S(2)}) collective-permute-start(bf16[2,128,768]{2,1,0:T(8,128)(2,1)S(1)} %slice.72), channel_id=1, source_target_pairs={{0,1},{1,2},{2,3},{3,0},{4,5},{5,6},{6,7},{7,4},{8,9},{9,10},{10,1... | collective-permute-start | bytes 1179656 | tf_op jit(solution)/shard_map/ppermute | solution.py:174
  163.6 13.5 %collective-permute-start.20 = (bf16[2,128,768]{2,1,0:T(8,128)(2,1)S(1)}, bf16[2,128,768]{2,1,0:T(8,128)(2,1)S(1)}, u32[]{:S(2)}, u32[]{:S(2)}) collective-permute-start(bf16[2,128,768]{2,1,0:T(8,128)(2,1)S(1)} %slice.73), channel_id=1, source_target_pairs={{0,3},{1,0},{2,1},{3,2},{4,7},{5,4},{6,5},{7,6},{8,11},{9,8},{10,9... | collective-permute-start | bytes 1179656 | tf_op jit(solution)/shard_map/ppermute | solution.py:174
  192.5 58.3 %all-to-all-start.2 = ((bf16[128,8,384]{2,1,0:T(8,128)(2,1)}), bf16[128,8,384]{2,1,0:T(8,128)(2,1)S(1)}, u32[]{:S(2)}, u32[]{:S(2)}) async-start(bf16[128,8,384]{2,1,0:T(8,128)(2,1)} %bitcast.46), calls=%async_computation.2 | async-start | bytes 1572864 | tf_op jit(solution)/shard_map/all_to_all | solution.py:479
  (2 other events, 3.1 us)

commit v6 on v5

--- a/solution.py
+++ b/solution.py
@@ -12,7 +12,6 @@
 HD = 64
 LANES = 128
 IMG = ("x", "z", "c")
-NEAR = 4
 VMEM_BYTES = 50 * 1024 * 1024
 
 SECTIONS = (
@@ -108,49 +107,28 @@
         ],
         axis=0,
     )
-    depth = lax.axis_size("z")
-    return jnp.stack(
-        [packed]
-        + [lax.ppermute(packed, "z", cycle(depth, NEAR * s)) for s in range(1, depth // NEAR)]
-    )
-
-
-def near_weights(far):
-    cores, depth = lax.axis_size("c"), lax.axis_size("z")
-    core, z = lax.axis_index("c"), lax.axis_index("z")
-    steps = far.shape[0]
-    highs = steps // cores
-    twice = jnp.concatenate([far, far])
-
-    def half_for(other):
-        first = (z // NEAR - highs * other - (highs - 1)) % steps
-        return lax.dynamic_slice_in_dim(twice, first, highs, axis=0)
-
-    both = jnp.stack([half_for(core), swap_cores(half_for(1 - core))])
-    near = [both] + [
-        lax.ppermute(both, "z", [(i, i // NEAR * NEAR + (i + t) % NEAR) for i in range(depth)])
-        for t in range(1, NEAR)
-    ]
-    return jnp.stack(near)
-
-
-def order_weights(near):
+    copies = jnp.broadcast_to(packed[None], (lax.axis_size("z"),) + packed.shape)
+    return lax.all_to_all(copies, "z", 0, 0, tiled=True)
+
+
+def order_weights(along_z):
     toks, cores, depth = lax.axis_size("tok"), lax.axis_size("c"), lax.axis_size("z")
-    tok, core, z = lax.axis_index("tok"), lax.axis_index("c"), lax.axis_index("z")
-    _, _, highs, packed_rows, lanes = near.shape
+    tok, core = lax.axis_index("tok"), lax.axis_index("c")
+    _, packed_rows, lanes = along_z.shape
     z_low = depth // cores
     count = cores * z_low * packed_rows
-    near = near.reshape(count, lanes)
+    mine = lax.dynamic_slice_in_dim(along_z, core * z_low, z_low, axis=0)
+    theirs = lax.dynamic_slice_in_dim(along_z, (1 - core) * z_low, z_low, axis=0)
+    both = jnp.stack([mine, swap_cores(theirs)]).reshape(count, lanes)
 
     first_table, _, first_rows = row_tables(SECTIONS[:1], 1, z_low, cores)
     rest_table, _, _ = row_tables(SECTIONS[1:], toks, z_low, cores)
     rest = lax.dynamic_index_in_dim(jnp.asarray(rest_table), tok, axis=1, keepdims=False)
     rest = rest + jnp.asarray([[first_rows], [0], [0]], jnp.int32)
     rows, low, from_core = jnp.concatenate([jnp.asarray(first_table[:, 0]), rest], axis=1)
-    order = ((z - low) % NEAR * cores + (from_core - core) % cores) * highs
-    order = (order + highs - 1 - low // NEAR) * packed_rows + rows
+    order = ((from_core - core) % cores * z_low + low) * packed_rows + rows
     mover = order[:, None] == jnp.arange(count, dtype=jnp.int32)[None, :]
-    ordered = f32_dot(mover.astype(jnp.bfloat16), near).astype(jnp.bfloat16)
+    ordered = f32_dot(mover.astype(jnp.bfloat16), both).astype(jnp.bfloat16)
     return ordered, first_table.shape[2]
 
 
@@ -441,31 +419,35 @@
     held = tokens.reshape(spread, block_rows, encoder)
     part = encoder // groups
 
-    parted = jnp.stack([held[:, :, x * part : (x + 1) * part] for x in range(groups)])
+    x = lax.axis_index("x")
+    parted = jnp.stack([held[:, :, i * part : (i + 1) * part] for i in range(groups)])
     parted, weight_shards = lax.optimization_barrier((parted, weight_shards))
-    pieces = lax.all_to_all(parted, "x", 0, 0, tiled=True).reshape(devices, block_rows, part)
-    far = start_weights(weight_shards)
+    along_z = start_weights(weight_shards)
+    pieces = []
+    for step in range(groups):
+        piece = lax.dynamic_index_in_dim(parted, (x + step) % groups, axis=0, keepdims=False)
+        pieces.append(piece if step == 0 else pass_on(piece, "x", step))
+    pieces = jnp.concatenate(pieces, axis=0)
 
     bases = owner_base[pair_list]
     slot = (column - bases) % spread
     source = ((bases + slot - column) // row_devices) % groups
     place = source * spread + slot
-    outgoing = jnp.take(pieces, place.reshape(-1), axis=0, mode="clip").reshape(
+    held_at = (x - source) % groups * spread + slot
+    outgoing = jnp.take(pieces, held_at.reshape(-1), axis=0, mode="clip").reshape(
         devices, 2, block_rows, part
     )
-    outgoing, near = lax.optimization_barrier((outgoing, near_weights(far)))
+    outgoing, along_z = lax.optimization_barrier((outgoing, along_z))
     arrived = lax.all_to_all(outgoing, IMG, 0, 0, tiled=True)
     arrived = arrived.reshape(groups, row_devices, 2, block_rows, part)
-    full = spread_weights(*order_weights(near))
+    full = spread_weights(*order_weights(along_z))
     embed_full, project_full, self_out_full, query_full, keyval_full, cross_out_full = full
     model_width = embed_full.shape[1]
 
     embedded = embed(arrived, embed_full)
     left, right = near_on_ring(embedded, "tok")
-    near_keyval, queries, totals = self_step([embedded], project_full, keyval_full)
-    left, right, totals = lax.optimization_barrier((left, right, totals))
     far_low, far_high = ring_far(left, right, 1)
-    next_keyval, totals = self_step([left, right], project_full, keyval_full, (queries, totals))
+    near_keyval, queries, totals = self_step([left, right, embedded], project_full, keyval_full)
     far_keyval, after_self, cross_queries = self_step(
         [far_low, far_high], project_full, keyval_full, (queries, totals),
         (embedded, self_out_full, query_full),
@@ -473,11 +455,11 @@
 
     halves = groups // 2
     backward = cross_block(
-        after_self, cross_queries, [near_keyval, next_keyval, far_keyval], cross_out_full,
+        after_self, cross_queries, [near_keyval, far_keyval], cross_out_full,
         halves, block_rows,
     ).reshape(devices, block_rows, model_width // halves)
     returned = lax.all_to_all(backward, IMG, 0, 0, tiled=True)
-    my_half = lax.axis_index("x") // halves
+    my_half = x // halves
     my_place = lax.dynamic_index_in_dim(place, my_half, axis=1, keepdims=False)
     selector = (
         my_place[None, :] == jnp.arange(devices, dtype=jnp.int32)[:, None]

time: 269 us -> 265 us (0.985)
  starting transfers between devices: 107 us -> 99.3 us
  waiting for transfers between devices: 90.3 us -> 98 us
  Pallas kernels: 38.9 us -> 35.8 us
    ppermute x6 -> x0, starting transfers between devices: 35.6 us -> none  [the longest x3 25.5 us: start_weights(): lax.ppermute(packed, 'z', cycle(depth, NEAR * s))]
    ppermute x12 -> x15, starting transfers between devices: 37.3 us -> 53.7 us  [pass_on(): return lax.ppermute(value, axis, cycle(lax.axis_size(axis), shift))]
    all_to_all x1, starting transfers between devices: 4.3 us -> 15.2 us  [start_weights(): return lax.all_to_all(copies, 'z', 0, 0, tiled=True)]
    ppermute x12 -> x15, waiting for transfers between devices: 41.2 us -> 49.6 us  [pass_on(): return lax.ppermute(value, axis, cycle(lax.axis_size(axis), shift))]
    all_to_all x1, waiting for transfers between devices: 0.01 us -> 4.3 us  [start_weights(): return lax.all_to_all(copies, 'z', 0, 0, tiled=True)]
    ppermute x6 -> x0, waiting for transfers between devices: 3.87 us -> none  [the longest x3 3.86 us: near_weights(): lax.ppermute(both, 'z', [(i, i // NEAR * NEAR + (i + t) % NEAR) for i in...]
    pallas_call x3 -> x2, Pallas kernels: 22.2 us -> 19.3 us  [self_step(): pl.pallas_call(functools.partial(self_kernel, first, last, len(pieces)),...]
  transfers between devices with their start and end apart: 24 -> 21, of which waited for: 12 -> 11; matrix products, arithmetic and copies ran while one was open for 2% -> 3% of each run, Pallas kernels for 8% -> 7%
where the time goes in v6:
time: 265 us; the launch traced here: 264 us
  starting transfers between devices  99.3 us (37%)
  waiting for transfers between devices  98 us (37%)
  Pallas kernels  35.8 us (14%)
  blocking collectives  15.4 us (6%)
  local copies, waits for them, and re-layouts  8.27 us (3%)
  other arithmetic  4.79 us (2%)
    ppermute x15, starting transfers between devices, pass_on(): return lax.ppermute(value, axis, cycle(lax.axis_size(axis), shift))  53.7 us
    ppermute x15, waiting for transfers between devices, pass_on(): return lax.ppermute(value, axis, cycle(lax.axis_size(axis), shift))  49.6 us
    all_to_all x1, waiting for transfers between devices, shards(): returned = lax.all_to_all(backward, IMG, 0, 0, tiled=True)  44.1 us
    pallas_call x2, Pallas kernels, self_step(): pl.pallas_call(functools.partial(self_kernel, first, last, len(pieces)),...  19.3 us
    all_to_all x1, blocking collectives, shards(): lax.all_to_all(partial.reshape(groups, spread, block_rows, model_width //...  15.4 us
    all_to_all x1, starting transfers between devices, start_weights(): return lax.all_to_all(copies, 'z', 0, 0, tiled=True)  15.2 us
    all_to_all x1, starting transfers between devices, shards(): returned = lax.all_to_all(backward, IMG, 0, 0, tiled=True)  13.7 us
    all_to_all x1, starting transfers between devices, shards(): arrived = lax.all_to_all(outgoing, IMG, 0, 0, tiled=True)  10.9 us
  transfers between devices with their start and end apart: 21, of which 11 were waited for; matrix products, arithmetic and copies ran while one was open for 3% of the time, Pallas kernels for 7%

profile of v6, /device:TPU:24, one launch (start us, length us, event | category | flops | bytes accessed | tf_op | source)
XLA Modules:
  0.0 264.0 jit_solution(13937560657200296514)
XLA Ops:
  5.4 15.2 %all-to-all-start = ((bf16[16,84,128]{2,1,0:T(8,128)(2,1)}), bf16[16,84,128]{2,1,0:T(8,128)(2,1)S(1)}, u32[]{:S(2)}, u32[]{:S(2)}) async-start(bf16[16,84,128]{2,1,0:T(8,128)(2,1)} %broadcast_in_dim.26), calls=%async_computation | async-start | bytes 720896 | tf_op jit(solution)/shard_map/all_to_all | solution.py:111
  20.7 4.7 %collective-permute-start.2 = (bf16[32,8,256]{2,1,0:T(8,128)(2,1)S(1)}, bf16[32,8,256]{2,1,0:T(8,128)(2,1)S(1)}, u32[]{:S(2)}, u32[]{:S(2)}) collective-permute-start(bf16[32,8,256]{2,1,0:T(8,128)(2,1)S(1)} %get-tuple-element.59), channel_id=1, source_target_pairs={{0,384},{128,0},{256,128},{384,256},{1,385},{129,1},{257,129},{385... | collective-permute-start | bytes 393224 | tf_op jit(solution)/shard_map/ppermute | solution.py:152
  25.4 2.7 %collective-permute-start.1 = (bf16[32,8,256]{2,1,0:T(8,128)(2,1)S(1)}, bf16[32,8,256]{2,1,0:T(8,128)(2,1)S(1)}, u32[]{:S(2)}, u32[]{:S(2)}) collective-permute-start(bf16[32,8,256]{2,1,0:T(8,128)(2,1)S(1)} %get-tuple-element.60), channel_id=1, source_target_pairs={{0,256},{128,384},{256,0},{384,128},{1,257},{129,385},{257,1},{385... | collective-permute-start | bytes 393224 | tf_op jit(solution)/shard_map/ppermute | solution.py:152
  28.1 2.8 %collective-permute-start = (bf16[32,8,256]{2,1,0:T(8,128)(2,1)S(1)}, bf16[32,8,256]{2,1,0:T(8,128)(2,1)S(1)}, u32[]{:S(2)}, u32[]{:S(2)}) collective-permute-start(bf16[32,8,256]{2,1,0:T(8,128)(2,1)S(1)} %get-tuple-element.61), channel_id=1, source_target_pairs={{0,128},{128,256},{256,384},{384,0},{1,129},{129,257},{257,385},{3... | collective-permute-start | bytes 393224 | tf_op jit(solution)/shard_map/ppermute | solution.py:152
  38.5 4.3 %all-to-all-done = bf16[16,84,128]{2,1,0:T(8,128)(2,1)S(1)} async-done(((bf16[16,84,128]{2,1,0:T(8,128)(2,1)}), bf16[16,84,128]{2,1,0:T(8,128)(2,1)S(1)}, u32[]{:S(2)}, u32[]{:S(2)}) %all-to-all-start) | async-done | bytes 344096 | tf_op jit(solution)/shard_map/all_to_all | solution.py:111
  42.8 1.9 collective-permute-start.3
  44.8 10.9 %all-to-all-start.1 = ((bf16[128,2,8,256]{3,2,1,0:T(8,128)(2,1)}), bf16[128,2,8,256]{3,2,1,0:T(8,128)(2,1)S(1)}, u32[]{:S(2)}, u32[]{:S(2)}) async-start(bf16[128,2,8,256]{3,2,1,0:T(8,128)(2,1)} %bitcast.13), calls=%async_computation.1 | async-start | bytes 2097152 | tf_op jit(solution)/shard_map/all_to_all | solution.py:441
  57.3 4.8 %collective-permute-start.6 = (bf16[1344,128]{1,0:T(8,128)(2,1)S(1)}, bf16[1344,128]{1,0:T(8,128)(2,1)S(1)}, u32[]{:S(2)}, u32[]{:S(2)}) collective-permute-start(bf16[1344,128]{1,0:T(8,128)(2,1)S(1)} %fusion.2), channel_id=1, source_target_pairs={{0,384},{128,0},{256,128},{384,256},{1,385},{129,1},{257,129},{385... | collective-permute-start | bytes 1032200 | tf_op jit(solution)/shard_map/ppermute | solution.py:152
  62.1 1.9 collective-permute-start.4
  64.1 8.0 %collective-permute-done.6 = bf16[1344,128]{1,0:T(8,128)(2,1)S(1)} collective-permute-done((bf16[1344,128]{1,0:T(8,128)(2,1)S(1)}, bf16[1344,128]{1,0:T(8,128)(2,1)S(1)}, u32[]{:S(2)}, u32[]{:S(2)}) %collective-permute-start.6) | collective-permute-done | bytes 344096 | tf_op jit(solution)/shard_map/ppermute | solution.py:152
  72.1 5.6 %collective-permute-start.7 = (bf16[576,128]{1,0:T(8,128)(2,1)S(1)}, bf16[576,128]{1,0:T(8,128)(2,1)S(1)}, u32[]{:S(2)}, u32[]{:S(2)}) collective-permute-start(bf16[576,128]{1,0:T(8,128)(2,1)S(1)} %get-tuple-element.70), channel_id=1, source_target_pairs={{0,384},{128,0},{256,128},{384,256},{1,385},{129,1},{257,129},{385... | collective-permute-start | bytes 442376 | tf_op jit(solution)/shard_map/ppermute | solution.py:152
  77.7 1.9 collective-permute-start.5
  79.7 8.4 %collective-permute-done.5 = bf16[768,128]{1,0:T(8,128)(2,1)S(1)} collective-permute-done((bf16[768,128]{1,0:T(8,128)(2,1)S(1)}, bf16[768,128]{1,0:T(8,128)(2,1)S(1)}, u32[]{:S(2)}, u32[]{:S(2)}) %collective-permute-start.5) | collective-permute-done | bytes 196640 | tf_op jit(solution)/shard_map/ppermute | solution.py:152
  88.2 1.9 collective-permute-start.10
  90.3 2.6 %collective-permute-start.9 = (bf16[4,576,128]{2,1,0:T(8,128)(2,1)S(1)}, bf16[4,576,128]{2,1,0:T(8,128)(2,1)S(1)}, u32[]{:S(2)}, u32[]{:S(2)}) collective-permute-start(bf16[4,576,128]{2,1,0:T(8,128)(2,1)S(1)} %get-tuple-element.57), channel_id=1, source_target_pairs={{0,3},{1,0},{2,1},{3,2},{4,7},{5,4},{6,5},{7,6},{8,11},{9,8},{10,9... | collective-permute-start | bytes 1769480 | tf_op jit(solution)/shard_map/ppermute | solution.py:152
  93.0 4.4 %collective-permute-start.8 = (bf16[4,576,128]{2,1,0:T(8,128)(2,1)S(1)}, bf16[4,576,128]{2,1,0:T(8,128)(2,1)S(1)}, u32[]{:S(2)}, u32[]{:S(2)}) collective-permute-start(bf16[4,576,128]{2,1,0:T(8,128)(2,1)S(1)} %get-tuple-element.57), channel_id=1, source_target_pairs={{0,1},{1,2},{2,3},{3,0},{4,5},{5,6},{6,7},{7,4},{8,9},{9,10},{10,1... | collective-permute-start | bytes 1769480 | tf_op jit(solution)/shard_map/ppermute | solution.py:152
  97.4 11.8 %collective-permute-done.9 = bf16[4,576,128]{2,1,0:T(8,128)(2,1)S(1)} collective-permute-done((bf16[4,576,128]{2,1,0:T(8,128)(2,1)S(1)}, bf16[4,576,128]{2,1,0:T(8,128)(2,1)S(1)}, u32[]{:S(2)}, u32[]{:S(2)}) %collective-permute-start.9) | collective-permute-done | bytes 589856 | tf_op jit(solution)/shard_map/ppermute | solution.py:152
  110.4 2.3 collective-permute-start.16
  112.7 5.2 %collective-permute-start.15 = (bf16[2,576,128]{2,1,0:T(8,128)(2,1)S(1)}, bf16[2,576,128]{2,1,0:T(8,128)(2,1)S(1)}, u32[]{:S(2)}, u32[]{:S(2)}) collective-permute-start(bf16[2,576,128]{2,1,0:T(8,128)(2,1)S(1)} %slice.72), channel_id=1, source_target_pairs={{0,1},{1,2},{2,3},{3,0},{4,5},{5,6},{6,7},{7,4},{8,9},{9,10},{10,1... | collective-permute-start | bytes 884744 | tf_op jit(solution)/shard_map/ppermute | solution.py:152
  117.9 4.6 %collective-permute-done.16 = bf16[2,576,128]{2,1,0:T(8,128)(2,1)S(1)} collective-permute-done((bf16[2,576,128]{2,1,0:T(8,128)(2,1)S(1)}, bf16[2,576,128]{2,1,0:T(8,128)(2,1)S(1)}, u32[]{:S(2)}, u32[]{:S(2)}) %collective-permute-start.16) | collective-permute-done | bytes 294944 | tf_op jit(solution)/shard_map/ppermute | solution.py:152
  129.3 3.8 %collective-permute-start.13 = (bf16[2,256,768]{2,1,0:T(8,128)(2,1)S(1)}, bf16[2,256,768]{2,1,0:T(8,128)(2,1)S(1)}, u32[]{:S(2)}, u32[]{:S(2)}) collective-permute-start(bf16[2,256,768]{2,1,0:T(8,128)(2,1)S(1)} %embed.1.refs_2_.refs_4_), channel_id=1, source_target_pairs={{0,3},{1,0},{2,1},{3,2},{4,7},{5,4},{6,5},{7,6},{8,11},{9,8},{10,9... | collective-permute-start | bytes 2359304 | tf_op jit(solution)/shard_map/ppermute | solution.py:152
  133.1 3.7 %collective-permute-start.11 = (bf16[2,256,768]{2,1,0:T(8,128)(2,1)S(1)}, bf16[2,256,768]{2,1,0:T(8,128)(2,1)S(1)}, u32[]{:S(2)}, u32[]{:S(2)}) collective-permute-start(bf16[2,256,768]{2,1,0:T(8,128)(2,1)S(1)} %embed.1.refs_2_.refs_4_), channel_id=1, source_target_pairs={{0,1},{1,2},{2,3},{3,0},{4,5},{5,6},{6,7},{7,4},{8,9},{9,10},{10,1... | collective-permute-start | bytes 2359304 | tf_op jit(solution)/shard_map/ppermute | solution.py:152
  136.9 4.4 %assemble.3 = (bf16[4,2,96,1152]{3,2,1,0:T(8,128)(2,1)}, bf16[4,2,48,768]{3,2,1,0:T(8,128)(2,1)S(1)}, bf16[4,2,96,384]{3,2,1,0:T(8,128)(2,1)S(1)}, bf16[4,2,96,7...) custom-call(s32[3]{0:T(128)S(1)} %pad_add_fusion.1.at_ref, bf16[4,4,576,128]{3,2,1,0:T(8,128)(2,1)} %pad_maximum_fusion.mine_ref, ...), custom_call_target="tpu_custom_call" | custom-call | bytes 9437184 | tf_op jit(solution)/shard_map/assemble/pallas_call | solution.py:191
  141.3 11.8 %collective-permute-done.13.refs_1_ = bf16[2,256,768]{2,1,0:T(8,128)(2,1)S(1)} collective-permute-done((bf16[2,256,768]{2,1,0:T(8,128)(2,1)S(1)}, bf16[2,256,768]{2,1,0:T(8,128)(2,1)S(1)}, u32[]{:S(2)}, u32[]{:S(2)}) %collective-permute-start.13) | collective-permute-done | bytes 786464 | tf_op jit(solution)/shard_map/ppermute | solution.py:152
  153.1 1.9 collective-permute-start.14
  155.1 5.3 %collective-permute-start.12 = (bf16[2,128,768]{2,1,0:T(8,128)(2,1)S(1)}, bf16[2,128,768]{2,1,0:T(8,128)(2,1)S(1)}, u32[]{:S(2)}, u32[]{:S(2)}) collective-permute-start(bf16[2,128,768]{2,1,0:T(8,128)(2,1)S(1)} %slice.92), channel_id=1, source_target_pairs={{0,1},{1,2},{2,3},{3,0},{4,5},{5,6},{6,7},{7,4},{8,9},{9,10},{10,1... | collective-permute-start | bytes 1179656 | tf_op jit(solution)/shard_map/ppermute | solution.py:152
  160.4 11.6 %self_step.2 = (bf16[2,768,768]{2,1,0:T(8,128)(2,1)}, bf16[2,256,384]{2,1,0:T(8,128)(2,1)S(1)}, f32[2,6,256,128]{3,2,1,0:T(8,128)}) custom-call(bf16[2,256,768]{2,1,0:T(8,128)(2,1)S(1)} %collective-permute-done.11.refs_0_, bf16[2,256,768]{2,1,0:T(8,128)(2,1)S(1)} %collective-permute-done.13.refs_1_, bf16[2,256,768]{2,1,0:T(8,128)(2,1)S(1)} %embed.1.refs_2_.refs_4_, ...), custom_call_target="tpu_custom_call" | custom-call | flops 4831838208 | bytes 5308416 | tf_op jit(solution)/shard_map/self_step/pallas_call | solution.py:354
  172.0 7.7 %self_step.3 = (bf16[2,256,768]{2,1,0:T(8,128)(2,1)S(1)}, f32[2,256,768]{2,1,0:T(8,128)}, bf16[2,256,384]{2,1,0:T(8,128)(2,1)S(1)}) custom-call(bf16[2,128,768]{2,1,0:T(8,128)(2,1)S(1)} %collective-permute-done.12.refs_0_, bf16[2,128,768]{2,1,0:T(8,128)(2,1)S(1)} %collective-permute-done.14.refs_1_, bf16[2,256,384]{2,1,0:T(8,128)(2,1)S(1)} %get-tuple-element.42.refs_2_, ...), custom_call_target="tpu_custom_call" | custom-call | flops 1610612736 | bytes 7667712 | tf_op jit(solution)/shard_map/self_step/pallas_call | solution.py:354
  181.1 7.6 %cross_block.1 = bf16[2,2,32,8,384]{4,3,2,1,0:T(8,128)(2,1)} custom-call(f32[2,256,768]{2,1,0:T(8,128)S(1)} %copy-done.3, bf16[2,256,384]{2,1,0:T(8,128)(2,1)S(1)} %get-tuple-element.47.query_ref, bf16[2,768,768]{2,1,0:T(8,128)(2,1)} %get-tuple-element.48.refs_0_, bf16[2,256,768]{2,1,0:T(8,128)(2,1)S(1)} %get-tuple-element.49.refs_1_, ...), custom_call_target="tpu_custom_call" | custom-call | flops 1912602624 | bytes 3342336 | tf_op jit(solution)/shard_map/cross_block/pallas_call | solution.py:392
  188.7 13.7 %all-to-all-start.2 = ((bf16[128,8,384]{2,1,0:T(8,128)(2,1)}), bf16[128,8,384]{2,1,0:T(8,128)(2,1)S(1)}, u32[]{:S(2)}, u32[]{:S(2)}) async-start(bf16[128,8,384]{2,1,0:T(8,128)(2,1)} %bitcast.41), calls=%async_computation.2 | async-start | bytes 1572864 | tf_op jit(solution)/shard_map/all_to_all | solution.py:461
  202.8 44.1 %all-to-all-done.2 = bf16[128,8,384]{2,1,0:T(8,128)(2,1)S(1)} async-done(((bf16[128,8,384]{2,1,0:T(8,128)(2,1)}), bf16[128,8,384]{2,1,0:T(8,128)(2,1)S(1)}, u32[]{:S(2)}, u32[]{:S(2)}) %all-to-all-start.2) | async-done | bytes 786464 | tf_op jit(solution)/shard_map/all_to_all | solution.py:461
  247.7 15.4 %all_to_all.20 = bf16[4,32,8,384]{3,2,1,0:T(8,128)(2,1)S(1)} all-to-all(bf16[4,32,8,384]{3,2,1,0:T(8,128)(2,1)S(1)} %copy.44), channel_id=1, replica_groups=mesh['x'=4,'z'=16,'c'=2,'tok'=4] {'x'}, dimensions={0} | all-to-all | bytes 1572864 | tf_op jit(solution)/shard_map/all_to_all | solution.py:470
  (78 shorter events, 26.3 us)
Async XLA Ops:
  0.0 31.2 %copy-start = (s32[128]{0:T(128)S(1)}, s32[128]{0:T(128)}, u32[]{:S(2)}) copy-start(s32[128]{0:T(128)} %param.14) | copy-start | bytes 1540
  0.0 30.9 %copy-start.5 = (s32[128,2]{0,1:T(2,128)S(1)}, s32[128,2]{0,1:T(2,128)}, u32[]{:S(2)}) copy-start(s32[128,2]{0,1:T(2,128)} %param.13) | copy-start | bytes 3076
  5.4 37.4 %all-to-all-start = ((bf16[16,84,128]{2,1,0:T(8,128)(2,1)}), bf16[16,84,128]{2,1,0:T(8,128)(2,1)S(1)}, u32[]{:S(2)}, u32[]{:S(2)}) async-start(bf16[16,84,128]{2,1,0:T(8,128)(2,1)} %broadcast_in_dim.26), calls=%async_computation | async-start | bytes 720896 | tf_op jit(solution)/shard_map/all_to_all | solution.py:111
  20.7 13.3 %collective-permute-start.2 = (bf16[32,8,256]{2,1,0:T(8,128)(2,1)S(1)}, bf16[32,8,256]{2,1,0:T(8,128)(2,1)S(1)}, u32[]{:S(2)}, u32[]{:S(2)}) collective-permute-start(bf16[32,8,256]{2,1,0:T(8,128)(2,1)S(1)} %get-tuple-element.59), channel_id=1, source_target_pairs={{0,384},{128,0},{256,128},{384,256},{1,385},{129,1},{257,129},{385... | collective-permute-start | bytes 393224 | tf_op jit(solution)/shard_map/ppermute | solution.py:152
  25.4 9.5 %collective-permute-start.1 = (bf16[32,8,256]{2,1,0:T(8,128)(2,1)S(1)}, bf16[32,8,256]{2,1,0:T(8,128)(2,1)S(1)}, u32[]{:S(2)}, u32[]{:S(2)}) collective-permute-start(bf16[32,8,256]{2,1,0:T(8,128)(2,1)S(1)} %get-tuple-element.60), channel_id=1, source_target_pairs={{0,256},{128,384},{256,0},{384,128},{1,257},{129,385},{257,1},{385... | collective-permute-start | bytes 393224 | tf_op jit(solution)/shard_map/ppermute | solution.py:152
  28.1 8.6 %collective-permute-start = (bf16[32,8,256]{2,1,0:T(8,128)(2,1)S(1)}, bf16[32,8,256]{2,1,0:T(8,128)(2,1)S(1)}, u32[]{:S(2)}, u32[]{:S(2)}) collective-permute-start(bf16[32,8,256]{2,1,0:T(8,128)(2,1)S(1)} %get-tuple-element.61), channel_id=1, source_target_pairs={{0,128},{128,256},{256,384},{384,0},{1,129},{129,257},{257,385},{3... | collective-permute-start | bytes 393224 | tf_op jit(solution)/shard_map/ppermute | solution.py:152
  31.2 1.9 copy-start.6
  31.3 2.7 %copy-start.4 = (s32[3,768]{1,0:T(4,128)S(1)}, s32[3,768]{1,0:T(4,128)}, u32[]{:S(2)}) copy-start(s32[3,768]{1,0:T(4,128)} %constant.149.clone) | copy-start | bytes 27652
  42.8 12.9 %collective-permute-start.3 = (bf16[8,84,128]{2,1,0:T(8,128)(2,1)S(1)}, bf16[8,84,128]{2,1,0:T(8,128)(2,1)S(1)}, u32[]{:S(2)}, u32[]{:S(2)}) collective-permute-start(bf16[8,84,128]{2,1,0:T(8,128)(2,1)S(1)} %get-tuple-element.69), channel_id=1, source_target_pairs={{0,4},{4,0},{1,5},{5,1},{2,6},{6,2},{3,7},{7,3},{8,12},{12,8},{9,1... | collective-permute-start | bytes 516104 | tf_op jit(solution)/shard_map/ppermute | solution.py:99
  44.8 83.5 %all-to-all-start.1 = ((bf16[128,2,8,256]{3,2,1,0:T(8,128)(2,1)}), bf16[128,2,8,256]{3,2,1,0:T(8,128)(2,1)S(1)}, u32[]{:S(2)}, u32[]{:S(2)}) async-start(bf16[128,2,8,256]{3,2,1,0:T(8,128)(2,1)} %bitcast.13), calls=%async_computation.1 | async-start | bytes 2097152 | tf_op jit(solution)/shard_map/all_to_all | solution.py:441
  57.3 14.8 %collective-permute-start.6 = (bf16[1344,128]{1,0:T(8,128)(2,1)S(1)}, bf16[1344,128]{1,0:T(8,128)(2,1)S(1)}, u32[]{:S(2)}, u32[]{:S(2)}) collective-permute-start(bf16[1344,128]{1,0:T(8,128)(2,1)S(1)} %fusion.2), channel_id=1, source_target_pairs={{0,384},{128,0},{256,128},{384,256},{1,385},{129,1},{257,129},{385... | collective-permute-start | bytes 1032200 | tf_op jit(solution)/shard_map/ppermute | solution.py:152
  62.1 15.6 %collective-permute-start.4 = (bf16[1344,128]{1,0:T(8,128)(2,1)S(1)}, bf16[1344,128]{1,0:T(8,128)(2,1)S(1)}, u32[]{:S(2)}, u32[]{:S(2)}) collective-permute-start(bf16[1344,128]{1,0:T(8,128)(2,1)S(1)} %fusion.2), channel_id=1, source_target_pairs={{0,128},{128,256},{256,384},{384,0},{1,129},{129,257},{257,385},{3... | collective-permute-start | bytes 1032200 | tf_op jit(solution)/shard_map/ppermute | solution.py:152
  72.1 18.1 %collective-permute-start.7 = (bf16[576,128]{1,0:T(8,128)(2,1)S(1)}, bf16[576,128]{1,0:T(8,128)(2,1)S(1)}, u32[]{:S(2)}, u32[]{:S(2)}) collective-permute-start(bf16[576,128]{1,0:T(8,128)(2,1)S(1)} %get-tuple-element.70), channel_id=1, source_target_pairs={{0,384},{128,0},{256,128},{384,256},{1,385},{129,1},{257,129},{385... | collective-permute-start | bytes 442376 | tf_op jit(solution)/shard_map/ppermute | solution.py:152
  77.7 10.4 %collective-permute-start.5 = (bf16[768,128]{1,0:T(8,128)(2,1)S(1)}, bf16[768,128]{1,0:T(8,128)(2,1)S(1)}, u32[]{:S(2)}, u32[]{:S(2)}) collective-permute-start(bf16[768,128]{1,0:T(8,128)(2,1)S(1)} %get-tuple-element.73), channel_id=1, source_target_pairs={{0,128},{128,256},{256,384},{384,0},{1,129},{129,257},{257,385},{3... | collective-permute-start | bytes 589832 | tf_op jit(solution)/shard_map/ppermute | solution.py:152
  88.2 22.1 %collective-permute-start.10 = (bf16[4,768,128]{2,1,0:T(8,128)(2,1)S(1)}, bf16[4,768,128]{2,1,0:T(8,128)(2,1)S(1)}, u32[]{:S(2)}, u32[]{:S(2)}) collective-permute-start(bf16[4,768,128]{2,1,0:T(8,128)(2,1)S(1)} %get-tuple-element.54), channel_id=1, source_target_pairs={{0,4},{4,0},{1,5},{5,1},{2,6},{6,2},{3,7},{7,3},{8,12},{12,8},{9,1... | collective-permute-start | bytes 2359304 | tf_op jit(solution)/shard_map/ppermute | solution.py:99
  90.3 18.8 %collective-permute-start.9 = (bf16[4,576,128]{2,1,0:T(8,128)(2,1)S(1)}, bf16[4,576,128]{2,1,0:T(8,128)(2,1)S(1)}, u32[]{:S(2)}, u32[]{:S(2)}) collective-permute-start(bf16[4,576,128]{2,1,0:T(8,128)(2,1)S(1)} %get-tuple-element.57), channel_id=1, source_target_pairs={{0,3},{1,0},{2,1},{3,2},{4,7},{5,4},{6,5},{7,6},{8,11},{9,8},{10,9... | collective-permute-start | bytes 1769480 | tf_op jit(solution)/shard_map/ppermute | solution.py:152
  93.0 17.4 %collective-permute-start.8 = (bf16[4,576,128]{2,1,0:T(8,128)(2,1)S(1)}, bf16[4,576,128]{2,1,0:T(8,128)(2,1)S(1)}, u32[]{:S(2)}, u32[]{:S(2)}) collective-permute-start(bf16[4,576,128]{2,1,0:T(8,128)(2,1)S(1)} %get-tuple-element.57), channel_id=1, source_target_pairs={{0,1},{1,2},{2,3},{3,0},{4,5},{5,6},{6,7},{7,4},{8,9},{9,10},{10,1... | collective-permute-start | bytes 1769480 | tf_op jit(solution)/shard_map/ppermute | solution.py:152
  110.4 12.2 %collective-permute-start.16 = (bf16[2,576,128]{2,1,0:T(8,128)(2,1)S(1)}, bf16[2,576,128]{2,1,0:T(8,128)(2,1)S(1)}, u32[]{:S(2)}, u32[]{:S(2)}) collective-permute-start(bf16[2,576,128]{2,1,0:T(8,128)(2,1)S(1)} %slice.73), channel_id=1, source_target_pairs={{0,3},{1,0},{2,1},{3,2},{4,7},{5,4},{6,5},{7,6},{8,11},{9,8},{10,9... | collective-permute-start | bytes 884744 | tf_op jit(solution)/shard_map/ppermute | solution.py:152
  112.7 11.0 %collective-permute-start.15 = (bf16[2,576,128]{2,1,0:T(8,128)(2,1)S(1)}, bf16[2,576,128]{2,1,0:T(8,128)(2,1)S(1)}, u32[]{:S(2)}, u32[]{:S(2)}) collective-permute-start(bf16[2,576,128]{2,1,0:T(8,128)(2,1)S(1)} %slice.72), channel_id=1, source_target_pairs={{0,1},{1,2},{2,3},{3,0},{4,5},{5,6},{6,7},{7,4},{8,9},{9,10},{10,1... | collective-permute-start | bytes 884744 | tf_op jit(solution)/shard_map/ppermute | solution.py:152
  125.5 11.4 %collective-permute-start.17 = (bf16[4,4,576,128]{3,2,1,0:T(8,128)(2,1)}, bf16[4,4,576,128]{3,2,1,0:T(8,128)(2,1)}, u32[]{:S(2)}, u32[]{:S(2)}) collective-permute-start(bf16[4,4,576,128]{3,2,1,0:T(8,128)(2,1)} %pad_maximum_fusion.mine_ref), channel_id=1, source_target_pairs={{0,4},{4,0},{1,5},{5,1},{2,6},{6,2},{3,7},{7,3},{8,12},{12,8},{9,1... | collective-permute-start | bytes 7077896 | tf_op jit(solution)/shard_map/ppermute | solution.py:99
  129.3 31.1 %copy-start.1 = (bf16[2,256,768]{2,1,0:T(8,128)(2,1)}, bf16[2,256,768]{2,1,0:T(8,128)(2,1)S(1)}, u32[]{:S(2)}) copy-start(bf16[2,256,768]{2,1,0:T(8,128)(2,1)S(1)} %embed.1.refs_2_.refs_4_) | copy-start | bytes 2359300
  129.3 23.8 %collective-permute-start.13 = (bf16[2,256,768]{2,1,0:T(8,128)(2,1)S(1)}, bf16[2,256,768]{2,1,0:T(8,128)(2,1)S(1)}, u32[]{:S(2)}, u32[]{:S(2)}) collective-permute-start(bf16[2,256,768]{2,1,0:T(8,128)(2,1)S(1)} %embed.1.refs_2_.refs_4_), channel_id=1, source_target_pairs={{0,3},{1,0},{2,1},{3,2},{4,7},{5,4},{6,5},{7,6},{8,11},{9,8},{10,9... | collective-permute-start | bytes 2359304 | tf_op jit(solution)/shard_map/ppermute | solution.py:152
  133.1 22.0 %collective-permute-start.11 = (bf16[2,256,768]{2,1,0:T(8,128)(2,1)S(1)}, bf16[2,256,768]{2,1,0:T(8,128)(2,1)S(1)}, u32[]{:S(2)}, u32[]{:S(2)}) collective-permute-start(bf16[2,256,768]{2,1,0:T(8,128)(2,1)S(1)} %embed.1.refs_2_.refs_4_), channel_id=1, source_target_pairs={{0,1},{1,2},{2,3},{3,0},{4,5},{5,6},{6,7},{7,4},{8,9},{9,10},{10,1... | collective-permute-start | bytes 2359304 | tf_op jit(solution)/shard_map/ppermute | solution.py:152
  141.3 30.7 %copy-start.2 = (bf16[4,2,96,768]{3,2,1,0:T(8,128)(2,1)}, bf16[4,2,96,768]{3,2,1,0:T(8,128)(2,1)S(1)}, u32[]{:S(2)}) copy-start(bf16[4,2,96,768]{3,2,1,0:T(8,128)(2,1)S(1)} %get-tuple-element.41) | copy-start | bytes 3538948
  153.1 18.9 %collective-permute-start.14 = (bf16[2,128,768]{2,1,0:T(8,128)(2,1)S(1)}, bf16[2,128,768]{2,1,0:T(8,128)(2,1)S(1)}, u32[]{:S(2)}, u32[]{:S(2)}) collective-permute-start(bf16[2,128,768]{2,1,0:T(8,128)(2,1)S(1)} %slice.93), channel_id=1, source_target_pairs={{0,3},{1,0},{2,1},{3,2},{4,7},{5,4},{6,5},{7,6},{8,11},{9,8},{10,9... | collective-permute-start | bytes 1179656 | tf_op jit(solution)/shard_map/ppermute | solution.py:152
  155.1 16.9 %collective-permute-start.12 = (bf16[2,128,768]{2,1,0:T(8,128)(2,1)S(1)}, bf16[2,128,768]{2,1,0:T(8,128)(2,1)S(1)}, u32[]{:S(2)}, u32[]{:S(2)}) collective-permute-start(bf16[2,128,768]{2,1,0:T(8,128)(2,1)S(1)} %slice.92), channel_id=1, source_target_pairs={{0,1},{1,2},{2,3},{3,0},{4,5},{5,6},{6,7},{7,4},{8,9},{9,10},{10,1... | collective-permute-start | bytes 1179656 | tf_op jit(solution)/shard_map/ppermute | solution.py:152
  179.7 1.4 copy-start.3
  188.7 58.1 %all-to-all-start.2 = ((bf16[128,8,384]{2,1,0:T(8,128)(2,1)}), bf16[128,8,384]{2,1,0:T(8,128)(2,1)S(1)}, u32[]{:S(2)}, u32[]{:S(2)}) async-start(bf16[128,8,384]{2,1,0:T(8,128)(2,1)} %bitcast.41), calls=%async_computation.2 | async-start | bytes 1572864 | tf_op jit(solution)/shard_map/all_to_all | solution.py:461

commit v7 on v6

--- a/solution.py
+++ b/solution.py
@@ -55,40 +55,37 @@
     return table, places, quarter
 
 
-def pack_kernel(sections, toks, tok_ref, *refs):
+def pack_kernel(toks, tok_ref, *refs):
     shard_refs, out_ref = refs[:-1], refs[-1]
-    pieces = []
-    for ref, (_, _, tiles) in zip(shard_refs, sections):
-        for tile in range(tiles):
-            pieces.append((ref, slice(tile * LANES, (tile + 1) * LANES)))
-    quarter = out_ref.shape[0]
-
-    def taken(some):
-        values = [ref[:, at].astype(jnp.float32) for ref, at in some]
-        return jnp.concatenate(values, axis=0).astype(jnp.bfloat16)
-
-    groups = [[] for _ in range(toks)]
+    tiles = [
+        [(ref, slice(tile * LANES, (tile + 1) * LANES)) for tile in range(count)]
+        for ref, (_, _, count) in zip(shard_refs, SECTIONS)
+    ]
+    rest = sum(tiles[1:], [])
+    quarter = sum(ref.shape[0] for ref, _ in rest) // toks
+    groups = [list(tiles[0]) for _ in range(toks)]
     at = 0
-    for ref, columns in pieces:
+    for ref, columns in rest:
         groups[at // quarter].append((ref, columns))
         at += ref.shape[0]
     for tok in range(toks):
         @pl.when(tok_ref[0] == tok)
         def _(tok=tok):
-            out_ref[...] = taken(groups[tok])
-
-
-def pack(shards_in, sections, toks):
-    quarter = sum(rows * tiles for _, rows, tiles in sections) // toks
-    tok = jnp.zeros((1,), jnp.int32) if toks == 1 else lax.axis_index("tok").astype(jnp.int32)[None]
+            values = [ref[:, columns].astype(jnp.float32) for ref, columns in groups[tok]]
+            out_ref[...] = jnp.concatenate(values, axis=0).astype(jnp.bfloat16)
+
+
+def pack(shards_in):
+    toks = lax.axis_size("tok")
+    sizes = [rows * tiles for _, rows, tiles in SECTIONS]
     return pl.pallas_call(
-        functools.partial(pack_kernel, sections, toks),
-        out_shape=jax.ShapeDtypeStruct((quarter, LANES), jnp.bfloat16),
+        functools.partial(pack_kernel, toks),
+        out_shape=jax.ShapeDtypeStruct((sizes[0] + sum(sizes[1:]) // toks, LANES), jnp.bfloat16),
         in_specs=[pl.BlockSpec(memory_space=pltpu.SMEM)]
         + [pl.BlockSpec(memory_space=pltpu.VMEM)] * len(shards_in),
         out_specs=pl.BlockSpec(memory_space=pltpu.VMEM),
         name="pack",
-    )(tok, *shards_in)
+    )(lax.axis_index("tok").astype(jnp.int32)[None], *shards_in)
 
 
 def cycle(count, shift):
@@ -100,13 +97,7 @@
 
 
 def start_weights(shards_in):
-    packed = jnp.concatenate(
-        [
-            pack(shards_in[:1], SECTIONS[:1], 1),
-            pack(shards_in[1:], SECTIONS[1:], lax.axis_size("tok")),
-        ],
-        axis=0,
-    )
+    packed = pack(shards_in)
     copies = jnp.broadcast_to(packed[None], (lax.axis_size("z"),) + packed.shape)
     return lax.all_to_all(copies, "z", 0, 0, tiled=True)
 
@@ -138,14 +129,13 @@
     far_rest = pass_on(right[first_rows:], "x", -1)
     first = jnp.stack([ordered[:first_rows], left[:first_rows], far_first, right[:first_rows]])
     rest = jnp.stack([ordered[first_rows:], left[first_rows:], far_rest, right[first_rows:]])
-    first_other = swap_cores(first)
-    left, right = near_on_ring(rest, "tok")
-    left, right, first_other = lax.optimization_barrier((left, right, first_other))
+    return assemble(first[None], swap_cores(first)[None], SECTIONS[:1], 1)[0], rest
+
+
+def finish_weights(rest, left, right):
     far_low, far_high = ring_far(left, right, 0)
     along_y = jnp.stack([rest, left, jnp.concatenate([far_low, far_high], axis=0), right])
-    return assemble(first[None], first_other[None], SECTIONS[:1], 1) + assemble(
-        along_y, swap_cores(along_y), SECTIONS[1:], lax.axis_size("tok")
-    )
+    return assemble(along_y, swap_cores(along_y), SECTIONS[1:], lax.axis_size("tok"))
 
 
 def pass_on(value, axis, shift):
@@ -440,11 +430,15 @@
     outgoing, along_z = lax.optimization_barrier((outgoing, along_z))
     arrived = lax.all_to_all(outgoing, IMG, 0, 0, tiled=True)
     arrived = arrived.reshape(groups, row_devices, 2, block_rows, part)
-    full = spread_weights(*order_weights(along_z))
-    embed_full, project_full, self_out_full, query_full, keyval_full, cross_out_full = full
+    embed_full, rest = spread_weights(*order_weights(along_z))
     model_width = embed_full.shape[1]
-
+    rest_left, rest_right = near_on_ring(rest, "tok")
     embedded = embed(arrived, embed_full)
+    rest_left, rest_right, embedded = lax.optimization_barrier((rest_left, rest_right, embedded))
+    project_full, self_out_full, query_full, keyval_full, cross_out_full = finish_weights(
+        rest, rest_left, rest_right
+    )
+
     left, right = near_on_ring(embedded, "tok")
     far_low, far_high = ring_far(left, right, 1)
     near_keyval, queries, totals = self_step([left, right, embedded], project_full, keyval_full)

time: 265 us -> 272 us (1.026)
  waiting for transfers between devices: 98 us -> 103 us
    all_to_all x1, waiting for transfers between devices: 0.01 us -> 8.36 us  [shards(): arrived = lax.all_to_all(outgoing, IMG, 0, 0, tiled=True)]
    ppermute x15, waiting for transfers between devices: 49.6 us -> 44.7 us  [pass_on(): return lax.ppermute(value, axis, cycle(lax.axis_size(axis), shift))]
  transfers between devices with their start and end apart: 21 -> 21, of which waited for: 11 -> 13; matrix products, arithmetic and copies ran while one was open for 3% -> 3% of each run, Pallas kernels for 7% -> 7%
where the time goes in v7:
time: 272 us; the launch traced here: 271 us
  waiting for transfers between devices  103 us (38%)
  starting transfers between devices  99.7 us (37%)
  Pallas kernels  34.8 us (13%)
  blocking collectives  15.4 us (6%)
  local copies, waits for them, and re-layouts  10.9 us (4%)
  other arithmetic  4.71 us (2%)
    ppermute x15, starting transfers between devices, pass_on(): return lax.ppermute(value, axis, cycle(lax.axis_size(axis), shift))  53.7 us
    ppermute x15, waiting for transfers between devices, pass_on(): return lax.ppermute(value, axis, cycle(lax.axis_size(axis), shift))  44.7 us
    all_to_all x1, waiting for transfers between devices, shards(): returned = lax.all_to_all(backward, IMG, 0, 0, tiled=True)  44.1 us
    pallas_call x2, Pallas kernels, self_step(): pl.pallas_call(functools.partial(self_kernel, first, last, len(pieces)),...  19.6 us
    all_to_all x1, blocking collectives, shards(): lax.all_to_all(partial.reshape(groups, spread, block_rows, model_width //...  15.4 us
    all_to_all x1, starting transfers between devices, start_weights(): return lax.all_to_all(copies, 'z', 0, 0, tiled=True)  15.2 us
    all_to_all x1, starting transfers between devices, shards(): returned = lax.all_to_all(backward, IMG, 0, 0, tiled=True)  14.2 us
    all_to_all x1, starting transfers between devices, shards(): arrived = lax.all_to_all(outgoing, IMG, 0, 0, tiled=True)  10.8 us
  transfers between devices with their start and end apart: 21, of which 13 were waited for; matrix products, arithmetic and copies ran while one was open for 3% of the time, Pallas kernels for 7%

profile of v7, /device:TPU:24, one launch (start us, length us, event | category | flops | bytes accessed | tf_op | source)
XLA Modules:
  0.0 270.8 jit_solution(11506996715815003219)
XLA Ops:
  4.2 15.2 %all-to-all-start = ((bf16[16,84,128]{2,1,0:T(8,128)(2,1)}), bf16[16,84,128]{2,1,0:T(8,128)(2,1)S(1)}, u32[]{:S(2)}, u32[]{:S(2)}) async-start(bf16[16,84,128]{2,1,0:T(8,128)(2,1)} %broadcast_in_dim.26), calls=%async_computation | async-start | bytes 720896 | tf_op jit(solution)/shard_map/all_to_all | solution.py:102
  19.5 4.7 %collective-permute-start.2 = (bf16[32,8,256]{2,1,0:T(8,128)(2,1)S(1)}, bf16[32,8,256]{2,1,0:T(8,128)(2,1)S(1)}, u32[]{:S(2)}, u32[]{:S(2)}) collective-permute-start(bf16[32,8,256]{2,1,0:T(8,128)(2,1)S(1)} %get-tuple-element.59), channel_id=1, source_target_pairs={{0,384},{128,0},{256,128},{384,256},{1,385},{129,1},{257,129},{385... | collective-permute-start | bytes 393224 | tf_op jit(solution)/shard_map/ppermute | solution.py:142
  24.1 2.7 %collective-permute-start.1 = (bf16[32,8,256]{2,1,0:T(8,128)(2,1)S(1)}, bf16[32,8,256]{2,1,0:T(8,128)(2,1)S(1)}, u32[]{:S(2)}, u32[]{:S(2)}) collective-permute-start(bf16[32,8,256]{2,1,0:T(8,128)(2,1)S(1)} %get-tuple-element.60), channel_id=1, source_target_pairs={{0,256},{128,384},{256,0},{384,128},{1,257},{129,385},{257,1},{385... | collective-permute-start | bytes 393224 | tf_op jit(solution)/shard_map/ppermute | solution.py:142
  26.9 2.8 %collective-permute-start = (bf16[32,8,256]{2,1,0:T(8,128)(2,1)S(1)}, bf16[32,8,256]{2,1,0:T(8,128)(2,1)S(1)}, u32[]{:S(2)}, u32[]{:S(2)}) collective-permute-start(bf16[32,8,256]{2,1,0:T(8,128)(2,1)S(1)} %get-tuple-element.61), channel_id=1, source_target_pairs={{0,128},{128,256},{256,384},{384,0},{1,129},{129,257},{257,385},{3... | collective-permute-start | bytes 393224 | tf_op jit(solution)/shard_map/ppermute | solution.py:142
  37.3 4.3 %all-to-all-done = bf16[16,84,128]{2,1,0:T(8,128)(2,1)S(1)} async-done(((bf16[16,84,128]{2,1,0:T(8,128)(2,1)}), bf16[16,84,128]{2,1,0:T(8,128)(2,1)S(1)}, u32[]{:S(2)}, u32[]{:S(2)}) %all-to-all-start) | async-done | bytes 344096 | tf_op jit(solution)/shard_map/all_to_all | solution.py:102
  41.5 10.8 %all-to-all-start.1 = ((bf16[128,2,8,256]{3,2,1,0:T(8,128)(2,1)}), bf16[128,2,8,256]{3,2,1,0:T(8,128)(2,1)S(1)}, u32[]{:S(2)}, u32[]{:S(2)}) async-start(bf16[128,2,8,256]{3,2,1,0:T(8,128)(2,1)} %bitcast.14), calls=%async_computation.1 | async-start | bytes 2097152 | tf_op jit(solution)/shard_map/all_to_all | solution.py:431
  53.2 1.9 collective-permute-start.3
  58.1 4.8 %collective-permute-start.5 = (bf16[1344,128]{1,0:T(8,128)(2,1)S(1)}, bf16[1344,128]{1,0:T(8,128)(2,1)S(1)}, u32[]{:S(2)}, u32[]{:S(2)}) collective-permute-start(bf16[1344,128]{1,0:T(8,128)(2,1)S(1)} %fusion.2), channel_id=1, source_target_pairs={{0,384},{128,0},{256,128},{384,256},{1,385},{129,1},{257,129},{385... | collective-permute-start | bytes 1032200 | tf_op jit(solution)/shard_map/ppermute | solution.py:142
  62.9 1.9 collective-permute-start.4
  64.9 7.5 %collective-permute-done.5 = bf16[1344,128]{1,0:T(8,128)(2,1)S(1)} collective-permute-done((bf16[1344,128]{1,0:T(8,128)(2,1)S(1)}, bf16[1344,128]{1,0:T(8,128)(2,1)S(1)}, u32[]{:S(2)}, u32[]{:S(2)}) %collective-permute-start.5) | collective-permute-done | bytes 344096 | tf_op jit(solution)/shard_map/ppermute | solution.py:142
  72.4 5.6 %collective-permute-start.6 = (bf16[576,128]{1,0:T(8,128)(2,1)S(1)}, bf16[576,128]{1,0:T(8,128)(2,1)S(1)}, u32[]{:S(2)}, u32[]{:S(2)}) collective-permute-start(bf16[576,128]{1,0:T(8,128)(2,1)S(1)} %get-tuple-element.72), channel_id=1, source_target_pairs={{0,384},{128,0},{256,128},{384,256},{1,385},{129,1},{257,129},{385... | collective-permute-start | bytes 442376 | tf_op jit(solution)/shard_map/ppermute | solution.py:142
  78.1 1.9 collective-permute-start.9
  80.0 8.6 %collective-permute-done.9 = bf16[768,128]{1,0:T(8,128)(2,1)S(1)} collective-permute-done((bf16[768,128]{1,0:T(8,128)(2,1)S(1)}, bf16[768,128]{1,0:T(8,128)(2,1)S(1)}, u32[]{:S(2)}, u32[]{:S(2)}) %collective-permute-start.9) | collective-permute-done | bytes 196640 | tf_op jit(solution)/shard_map/ppermute | solution.py:142
  88.8 1.9 collective-permute-start.10
  91.7 2.6 collective-permute-start.8
  94.3 4.4 %collective-permute-start.7 = (bf16[4,576,128]{2,1,0:T(8,128)(2,1)}, bf16[4,576,128]{2,1,0:T(8,128)(2,1)}, u32[]{:S(2)}, u32[]{:S(2)}) collective-permute-start(bf16[4,576,128]{2,1,0:T(8,128)(2,1)} %get-tuple-element.57), channel_id=1, source_target_pairs={{0,1},{1,2},{2,3},{3,0},{4,5},{5,6},{6,7},{7,4},{8,9},{9,10},{10,1... | collective-permute-start | bytes 1769480 | tf_op jit(solution)/shard_map/ppermute | solution.py:142
  99.6 8.4 %all-to-all-done.1 = bf16[128,2,8,256]{3,2,1,0:T(8,128)(2,1)S(1)} async-done(((bf16[128,2,8,256]{3,2,1,0:T(8,128)(2,1)}), bf16[128,2,8,256]{3,2,1,0:T(8,128)(2,1)S(1)}, u32[]{:S(2)}, u32[]{:S(2)}) %all-to-all-start.1) | async-done | bytes 1048608 | tf_op jit(solution)/shard_map/all_to_all | solution.py:431
  113.9 2.4 collective-permute-start.16
  116.3 5.2 %collective-permute-start.15 = (bf16[2,576,128]{2,1,0:T(8,128)(2,1)S(1)}, bf16[2,576,128]{2,1,0:T(8,128)(2,1)S(1)}, u32[]{:S(2)}, u32[]{:S(2)}) collective-permute-start(bf16[2,576,128]{2,1,0:T(8,128)(2,1)S(1)} %slice.72), channel_id=1, source_target_pairs={{0,1},{1,2},{2,3},{3,0},{4,5},{5,6},{6,7},{7,4},{8,9},{9,10},{10,1... | collective-permute-start | bytes 884744 | tf_op jit(solution)/shard_map/ppermute | solution.py:142
  121.5 4.6 %collective-permute-done.16 = bf16[2,576,128]{2,1,0:T(8,128)(2,1)S(1)} collective-permute-done((bf16[2,576,128]{2,1,0:T(8,128)(2,1)S(1)}, bf16[2,576,128]{2,1,0:T(8,128)(2,1)S(1)}, u32[]{:S(2)}, u32[]{:S(2)}) %collective-permute-start.16) | collective-permute-done | bytes 294944 | tf_op jit(solution)/shard_map/ppermute | solution.py:142
  128.9 1.9 collective-permute-start.17
  130.8 3.8 %collective-permute-start.13 = (bf16[2,256,768]{2,1,0:T(8,128)(2,1)S(1)}, bf16[2,256,768]{2,1,0:T(8,128)(2,1)S(1)}, u32[]{:S(2)}, u32[]{:S(2)}) collective-permute-start(bf16[2,256,768]{2,1,0:T(8,128)(2,1)S(1)} %embed.1.refs_2_.refs_4_), channel_id=1, source_target_pairs={{0,3},{1,0},{2,1},{3,2},{4,7},{5,4},{6,5},{7,6},{8,11},{9,8},{10,9... | collective-permute-start | bytes 2359304 | tf_op jit(solution)/shard_map/ppermute | solution.py:142
  134.6 3.7 %collective-permute-start.11 = (bf16[2,256,768]{2,1,0:T(8,128)(2,1)S(1)}, bf16[2,256,768]{2,1,0:T(8,128)(2,1)S(1)}, u32[]{:S(2)}, u32[]{:S(2)}) collective-permute-start(bf16[2,256,768]{2,1,0:T(8,128)(2,1)S(1)} %embed.1.refs_2_.refs_4_), channel_id=1, source_target_pairs={{0,1},{1,2},{2,3},{3,0},{4,5},{5,6},{6,7},{7,4},{8,9},{9,10},{10,1... | collective-permute-start | bytes 2359304 | tf_op jit(solution)/shard_map/ppermute | solution.py:142
  138.4 16.3 %collective-permute-done.13.refs_1_ = bf16[2,256,768]{2,1,0:T(8,128)(2,1)S(1)} collective-permute-done((bf16[2,256,768]{2,1,0:T(8,128)(2,1)S(1)}, bf16[2,256,768]{2,1,0:T(8,128)(2,1)S(1)}, u32[]{:S(2)}, u32[]{:S(2)}) %collective-permute-start.13) | collective-permute-done | bytes 786464 | tf_op jit(solution)/shard_map/ppermute | solution.py:142
  156.6 5.3 %collective-permute-start.12 = (bf16[2,128,768]{2,1,0:T(8,128)(2,1)S(1)}, bf16[2,128,768]{2,1,0:T(8,128)(2,1)S(1)}, u32[]{:S(2)}, u32[]{:S(2)}) collective-permute-start(bf16[2,128,768]{2,1,0:T(8,128)(2,1)S(1)} %slice.92), channel_id=1, source_target_pairs={{0,1},{1,2},{2,3},{3,0},{4,5},{5,6},{6,7},{7,4},{8,9},{9,10},{10,1... | collective-permute-start | bytes 1179656 | tf_op jit(solution)/shard_map/ppermute | solution.py:142
  162.0 4.4 %assemble.3 = (bf16[4,2,96,1152]{3,2,1,0:T(8,128)(2,1)}, bf16[4,2,48,768]{3,2,1,0:T(8,128)(2,1)S(1)}, bf16[4,2,96,384]{3,2,1,0:T(8,128)(2,1)S(1)}, bf16[4,2,96,7...) custom-call(s32[3]{0:T(128)S(1)} %pad_add_fusion.1.at_ref, bf16[4,4,576,128]{3,2,1,0:T(8,128)(2,1)} %copy-done.4, ...), custom_call_target="tpu_custom_call" | custom-call | bytes 9437184 | tf_op jit(solution)/shard_map/assemble/pallas_call | solution.py:181
  166.4 11.9 %self_step.2 = (bf16[2,768,768]{2,1,0:T(8,128)(2,1)}, bf16[2,256,384]{2,1,0:T(8,128)(2,1)S(1)}, f32[2,6,256,128]{3,2,1,0:T(8,128)}) custom-call(bf16[2,256,768]{2,1,0:T(8,128)(2,1)S(1)} %collective-permute-done.11.refs_0_, bf16[2,256,768]{2,1,0:T(8,128)(2,1)S(1)} %collective-permute-done.13.refs_1_, bf16[2,256,768]{2,1,0:T(8,128)(2,1)S(1)} %embed.1.refs_2_.refs_4_, ...), custom_call_target="tpu_custom_call" | custom-call | flops 4831838208 | bytes 5308416 | tf_op jit(solution)/shard_map/self_step/pallas_call | solution.py:344
  178.4 7.7 %self_step.3 = (bf16[2,256,768]{2,1,0:T(8,128)(2,1)S(1)}, f32[2,256,768]{2,1,0:T(8,128)}, bf16[2,256,384]{2,1,0:T(8,128)(2,1)S(1)}) custom-call(bf16[2,128,768]{2,1,0:T(8,128)(2,1)S(1)} %collective-permute-done.12.refs_0_, bf16[2,128,768]{2,1,0:T(8,128)(2,1)S(1)} %collective-permute-done.14.refs_1_, bf16[2,256,384]{2,1,0:T(8,128)(2,1)S(1)} %get-tuple-element.42.refs_2_, ...), custom_call_target="tpu_custom_call" | custom-call | flops 1610612736 | bytes 7667712 | tf_op jit(solution)/shard_map/self_step/pallas_call | solution.py:344
  187.4 7.6 %cross_block.1 = bf16[2,2,32,8,384]{4,3,2,1,0:T(8,128)(2,1)} custom-call(f32[2,256,768]{2,1,0:T(8,128)S(1)} %copy-done.3, bf16[2,256,384]{2,1,0:T(8,128)(2,1)S(1)} %get-tuple-element.47.query_ref, bf16[2,768,768]{2,1,0:T(8,128)(2,1)} %get-tuple-element.48.refs_0_, bf16[2,256,768]{2,1,0:T(8,128)(2,1)S(1)} %get-tuple-element.49.refs_1_, ...), custom_call_target="tpu_custom_call" | custom-call | flops 1912602624 | bytes 3342336 | tf_op jit(solution)/shard_map/cross_block/pallas_call | solution.py:382
  195.0 14.2 %all-to-all-start.2 = ((bf16[128,8,384]{2,1,0:T(8,128)(2,1)}), bf16[128,8,384]{2,1,0:T(8,128)(2,1)S(1)}, u32[]{:S(2)}, u32[]{:S(2)}) async-start(bf16[128,8,384]{2,1,0:T(8,128)(2,1)} %bitcast.41), calls=%async_computation.2 | async-start | bytes 1572864 | tf_op jit(solution)/shard_map/all_to_all | solution.py:455
  209.6 44.1 %all-to-all-done.2 = bf16[128,8,384]{2,1,0:T(8,128)(2,1)S(1)} async-done(((bf16[128,8,384]{2,1,0:T(8,128)(2,1)}), bf16[128,8,384]{2,1,0:T(8,128)(2,1)S(1)}, u32[]{:S(2)}, u32[]{:S(2)}) %all-to-all-start.2) | async-done | bytes 786464 | tf_op jit(solution)/shard_map/all_to_all | solution.py:455
  254.5 15.4 %all_to_all.20 = bf16[4,32,8,384]{3,2,1,0:T(8,128)(2,1)S(1)} all-to-all(bf16[4,32,8,384]{3,2,1,0:T(8,128)(2,1)S(1)} %copy.44), channel_id=1, replica_groups=mesh['x'=4,'z'=16,'c'=2,'tok'=4] {'x'}, dimensions={0} | all-to-all | bytes 1572864 | tf_op jit(solution)/shard_map/all_to_all | solution.py:464
  (78 shorter events, 31.7 us)
Async XLA Ops:
  0.0 30.0 %copy-start = (s32[128]{0:T(128)S(1)}, s32[128]{0:T(128)}, u32[]{:S(2)}) copy-start(s32[128]{0:T(128)} %param.14) | copy-start | bytes 1540
  0.0 29.7 %copy-start.6 = (s32[128,2]{0,1:T(2,128)S(1)}, s32[128,2]{0,1:T(2,128)}, u32[]{:S(2)}) copy-start(s32[128,2]{0,1:T(2,128)} %param.13) | copy-start | bytes 3076
  4.2 37.4 %all-to-all-start = ((bf16[16,84,128]{2,1,0:T(8,128)(2,1)}), bf16[16,84,128]{2,1,0:T(8,128)(2,1)S(1)}, u32[]{:S(2)}, u32[]{:S(2)}) async-start(bf16[16,84,128]{2,1,0:T(8,128)(2,1)} %broadcast_in_dim.26), calls=%async_computation | async-start | bytes 720896 | tf_op jit(solution)/shard_map/all_to_all | solution.py:102
  19.5 12.4 %collective-permute-start.2 = (bf16[32,8,256]{2,1,0:T(8,128)(2,1)S(1)}, bf16[32,8,256]{2,1,0:T(8,128)(2,1)S(1)}, u32[]{:S(2)}, u32[]{:S(2)}) collective-permute-start(bf16[32,8,256]{2,1,0:T(8,128)(2,1)S(1)} %get-tuple-element.59), channel_id=1, source_target_pairs={{0,384},{128,0},{256,128},{384,256},{1,385},{129,1},{257,129},{385... | collective-permute-start | bytes 393224 | tf_op jit(solution)/shard_map/ppermute | solution.py:142
  24.1 9.5 %collective-permute-start.1 = (bf16[32,8,256]{2,1,0:T(8,128)(2,1)S(1)}, bf16[32,8,256]{2,1,0:T(8,128)(2,1)S(1)}, u32[]{:S(2)}, u32[]{:S(2)}) collective-permute-start(bf16[32,8,256]{2,1,0:T(8,128)(2,1)S(1)} %get-tuple-element.60), channel_id=1, source_target_pairs={{0,256},{128,384},{256,0},{384,128},{1,257},{129,385},{257,1},{385... | collective-permute-start | bytes 393224 | tf_op jit(solution)/shard_map/ppermute | solution.py:142
  26.9 8.6 %collective-permute-start = (bf16[32,8,256]{2,1,0:T(8,128)(2,1)S(1)}, bf16[32,8,256]{2,1,0:T(8,128)(2,1)S(1)}, u32[]{:S(2)}, u32[]{:S(2)}) collective-permute-start(bf16[32,8,256]{2,1,0:T(8,128)(2,1)S(1)} %get-tuple-element.61), channel_id=1, source_target_pairs={{0,128},{128,256},{256,384},{384,0},{1,129},{129,257},{257,385},{3... | collective-permute-start | bytes 393224 | tf_op jit(solution)/shard_map/ppermute | solution.py:142
  35.5 16.8 %copy-start.7 = (s32[3]{0:T(128)S(1)}, s32[3]{0:T(128)}, u32[]{:S(2)}) copy-start(s32[3]{0:T(128)} %constant.155) | copy-start | bytes 40
  35.5 17.6 %copy-start.5 = (s32[3,768]{1,0:T(4,128)S(1)}, s32[3,768]{1,0:T(4,128)}, u32[]{:S(2)}) copy-start(s32[3,768]{1,0:T(4,128)} %constant.147.clone) | copy-start | bytes 27652
  41.5 66.4 %all-to-all-start.1 = ((bf16[128,2,8,256]{3,2,1,0:T(8,128)(2,1)}), bf16[128,2,8,256]{3,2,1,0:T(8,128)(2,1)S(1)}, u32[]{:S(2)}, u32[]{:S(2)}) async-start(bf16[128,2,8,256]{3,2,1,0:T(8,128)(2,1)} %bitcast.14), calls=%async_computation.1 | async-start | bytes 2097152 | tf_op jit(solution)/shard_map/all_to_all | solution.py:431
  53.2 3.3 %collective-permute-start.3 = (bf16[8,84,128]{2,1,0:T(8,128)(2,1)S(1)}, bf16[8,84,128]{2,1,0:T(8,128)(2,1)S(1)}, u32[]{:S(2)}, u32[]{:S(2)}) collective-permute-start(bf16[8,84,128]{2,1,0:T(8,128)(2,1)S(1)} %get-tuple-element.69), channel_id=1, source_target_pairs={{0,4},{4,0},{1,5},{5,1},{2,6},{6,2},{3,7},{7,3},{8,12},{12,8},{9,1... | collective-permute-start | bytes 516104 | tf_op jit(solution)/shard_map/ppermute | solution.py:96
  58.1 14.3 %collective-permute-start.5 = (bf16[1344,128]{1,0:T(8,128)(2,1)S(1)}, bf16[1344,128]{1,0:T(8,128)(2,1)S(1)}, u32[]{:S(2)}, u32[]{:S(2)}) collective-permute-start(bf16[1344,128]{1,0:T(8,128)(2,1)S(1)} %fusion.2), channel_id=1, source_target_pairs={{0,384},{128,0},{256,128},{384,256},{1,385},{129,1},{257,129},{385... | collective-permute-start | bytes 1032200 | tf_op jit(solution)/shard_map/ppermute | solution.py:142
  62.9 15.1 %collective-permute-start.4 = (bf16[1344,128]{1,0:T(8,128)(2,1)S(1)}, bf16[1344,128]{1,0:T(8,128)(2,1)S(1)}, u32[]{:S(2)}, u32[]{:S(2)}) collective-permute-start(bf16[1344,128]{1,0:T(8,128)(2,1)S(1)} %fusion.2), channel_id=1, source_target_pairs={{0,128},{128,256},{256,384},{384,0},{1,129},{129,257},{257,385},{3... | collective-permute-start | bytes 1032200 | tf_op jit(solution)/shard_map/ppermute | solution.py:142
  72.4 18.3 %collective-permute-start.6 = (bf16[576,128]{1,0:T(8,128)(2,1)S(1)}, bf16[576,128]{1,0:T(8,128)(2,1)S(1)}, u32[]{:S(2)}, u32[]{:S(2)}) collective-permute-start(bf16[576,128]{1,0:T(8,128)(2,1)S(1)} %get-tuple-element.72), channel_id=1, source_target_pairs={{0,384},{128,0},{256,128},{384,256},{1,385},{129,1},{257,129},{385... | collective-permute-start | bytes 442376 | tf_op jit(solution)/shard_map/ppermute | solution.py:142
  78.1 10.6 %collective-permute-start.9 = (bf16[768,128]{1,0:T(8,128)(2,1)S(1)}, bf16[768,128]{1,0:T(8,128)(2,1)S(1)}, u32[]{:S(2)}, u32[]{:S(2)}) collective-permute-start(bf16[768,128]{1,0:T(8,128)(2,1)S(1)} %get-tuple-element.71), channel_id=1, source_target_pairs={{0,128},{128,256},{256,384},{384,0},{1,129},{129,257},{257,385},{3... | collective-permute-start | bytes 589832 | tf_op jit(solution)/shard_map/ppermute | solution.py:142
  88.8 10.0 %collective-permute-start.10 = (bf16[4,768,128]{2,1,0:T(8,128)(2,1)S(1)}, bf16[4,768,128]{2,1,0:T(8,128)(2,1)S(1)}, u32[]{:S(2)}, u32[]{:S(2)}) collective-permute-start(bf16[4,768,128]{2,1,0:T(8,128)(2,1)S(1)} %get-tuple-element.54), channel_id=1, source_target_pairs={{0,4},{4,0},{1,5},{5,1},{2,6},{6,2},{3,7},{7,3},{8,12},{12,8},{9,1... | collective-permute-start | bytes 2359304 | tf_op jit(solution)/shard_map/ppermute | solution.py:96
  91.7 19.1 %collective-permute-start.8 = (bf16[4,576,128]{2,1,0:T(8,128)(2,1)}, bf16[4,576,128]{2,1,0:T(8,128)(2,1)}, u32[]{:S(2)}, u32[]{:S(2)}) collective-permute-start(bf16[4,576,128]{2,1,0:T(8,128)(2,1)} %get-tuple-element.57), channel_id=1, source_target_pairs={{0,3},{1,0},{2,1},{3,2},{4,7},{5,4},{6,5},{7,6},{8,11},{9,8},{10,9... | collective-permute-start | bytes 1769480 | tf_op jit(solution)/shard_map/ppermute | solution.py:142
  94.3 17.7 %collective-permute-start.7 = (bf16[4,576,128]{2,1,0:T(8,128)(2,1)}, bf16[4,576,128]{2,1,0:T(8,128)(2,1)}, u32[]{:S(2)}, u32[]{:S(2)}) collective-permute-start(bf16[4,576,128]{2,1,0:T(8,128)(2,1)} %get-tuple-element.57), channel_id=1, source_target_pairs={{0,1},{1,2},{2,3},{3,0},{4,5},{5,6},{6,7},{7,4},{8,9},{9,10},{10,1... | collective-permute-start | bytes 1769480 | tf_op jit(solution)/shard_map/ppermute | solution.py:142
  109.0 57.5 %copy-start.1 = (bf16[2,256,768]{2,1,0:T(8,128)(2,1)}, bf16[2,256,768]{2,1,0:T(8,128)(2,1)S(1)}, u32[]{:S(2)}) copy-start(bf16[2,256,768]{2,1,0:T(8,128)(2,1)S(1)} %embed.1.refs_2_.refs_4_) | copy-start | bytes 2359300
  113.9 12.2 %collective-permute-start.16 = (bf16[2,576,128]{2,1,0:T(8,128)(2,1)S(1)}, bf16[2,576,128]{2,1,0:T(8,128)(2,1)S(1)}, u32[]{:S(2)}, u32[]{:S(2)}) collective-permute-start(bf16[2,576,128]{2,1,0:T(8,128)(2,1)S(1)} %slice.73), channel_id=1, source_target_pairs={{0,3},{1,0},{2,1},{3,2},{4,7},{5,4},{6,5},{7,6},{8,11},{9,8},{10,9... | collective-permute-start | bytes 884744 | tf_op jit(solution)/shard_map/ppermute | solution.py:142
  116.3 11.0 %collective-permute-start.15 = (bf16[2,576,128]{2,1,0:T(8,128)(2,1)S(1)}, bf16[2,576,128]{2,1,0:T(8,128)(2,1)S(1)}, u32[]{:S(2)}, u32[]{:S(2)}) collective-permute-start(bf16[2,576,128]{2,1,0:T(8,128)(2,1)S(1)} %slice.72), channel_id=1, source_target_pairs={{0,1},{1,2},{2,3},{3,0},{4,5},{5,6},{6,7},{7,4},{8,9},{9,10},{10,1... | collective-permute-start | bytes 884744 | tf_op jit(solution)/shard_map/ppermute | solution.py:142
  128.9 33.1 %copy-start.4 = (bf16[4,4,576,128]{3,2,1,0:T(8,128)(2,1)}, bf16[4,4,576,128]{3,2,1,0:T(8,128)(2,1)S(1)}, u32[]{:S(2)}) copy-start(bf16[4,4,576,128]{3,2,1,0:T(8,128)(2,1)S(1)} %pad_maximum_fusion.mine_ref) | copy-start | bytes 7077892
  128.9 33.1 %collective-permute-start.17 = (bf16[4,4,576,128]{3,2,1,0:T(8,128)(2,1)S(1)}, bf16[4,4,576,128]{3,2,1,0:T(8,128)(2,1)}, u32[]{:S(2)}, u32[]{:S(2)}) collective-permute-start(bf16[4,4,576,128]{3,2,1,0:T(8,128)(2,1)S(1)} %pad_maximum_fusion.mine_ref), channel_id=1, source_target_pairs={{0,4},{4,0},{1,5},{5,1},{2,6},{6,2},{3,7},{7,3},{8,12},{12,8},{9,1... | collective-permute-start | bytes 7077896 | tf_op jit(solution)/shard_map/ppermute | solution.py:96
  130.8 23.8 %collective-permute-start.13 = (bf16[2,256,768]{2,1,0:T(8,128)(2,1)S(1)}, bf16[2,256,768]{2,1,0:T(8,128)(2,1)S(1)}, u32[]{:S(2)}, u32[]{:S(2)}) collective-permute-start(bf16[2,256,768]{2,1,0:T(8,128)(2,1)S(1)} %embed.1.refs_2_.refs_4_), channel_id=1, source_target_pairs={{0,3},{1,0},{2,1},{3,2},{4,7},{5,4},{6,5},{7,6},{8,11},{9,8},{10,9... | collective-permute-start | bytes 2359304 | tf_op jit(solution)/shard_map/ppermute | solution.py:142
  134.6 22.0 %collective-permute-start.11 = (bf16[2,256,768]{2,1,0:T(8,128)(2,1)S(1)}, bf16[2,256,768]{2,1,0:T(8,128)(2,1)S(1)}, u32[]{:S(2)}, u32[]{:S(2)}) collective-permute-start(bf16[2,256,768]{2,1,0:T(8,128)(2,1)S(1)} %embed.1.refs_2_.refs_4_), channel_id=1, source_target_pairs={{0,1},{1,2},{2,3},{3,0},{4,5},{5,6},{6,7},{7,4},{8,9},{9,10},{10,1... | collective-permute-start | bytes 2359304 | tf_op jit(solution)/shard_map/ppermute | solution.py:142
  154.7 23.7 %collective-permute-start.14 = (bf16[2,128,768]{2,1,0:T(8,128)(2,1)S(1)}, bf16[2,128,768]{2,1,0:T(8,128)(2,1)S(1)}, u32[]{:S(2)}, u32[]{:S(2)}) collective-permute-start(bf16[2,128,768]{2,1,0:T(8,128)(2,1)S(1)} %slice.93), channel_id=1, source_target_pairs={{0,3},{1,0},{2,1},{3,2},{4,7},{5,4},{6,5},{7,6},{8,11},{9,8},{10,9... | collective-permute-start | bytes 1179656 | tf_op jit(solution)/shard_map/ppermute | solution.py:142
  156.6 21.7 %collective-permute-start.12 = (bf16[2,128,768]{2,1,0:T(8,128)(2,1)S(1)}, bf16[2,128,768]{2,1,0:T(8,128)(2,1)S(1)}, u32[]{:S(2)}, u32[]{:S(2)}) collective-permute-start(bf16[2,128,768]{2,1,0:T(8,128)(2,1)S(1)} %slice.92), channel_id=1, source_target_pairs={{0,1},{1,2},{2,3},{3,0},{4,5},{5,6},{6,7},{7,4},{8,9},{9,10},{10,1... | collective-permute-start | bytes 1179656 | tf_op jit(solution)/shard_map/ppermute | solution.py:142
  166.4 11.9 %copy-start.2 = (bf16[4,2,96,768]{3,2,1,0:T(8,128)(2,1)}, bf16[4,2,96,768]{3,2,1,0:T(8,128)(2,1)S(1)}, u32[]{:S(2)}) copy-start(bf16[4,2,96,768]{3,2,1,0:T(8,128)(2,1)S(1)} %get-tuple-element.41) | copy-start | bytes 3538948
  186.0 1.4 copy-start.3
  195.0 58.6 %all-to-all-start.2 = ((bf16[128,8,384]{2,1,0:T(8,128)(2,1)}), bf16[128,8,384]{2,1,0:T(8,128)(2,1)S(1)}, u32[]{:S(2)}, u32[]{:S(2)}) async-start(bf16[128,8,384]{2,1,0:T(8,128)(2,1)} %bitcast.41), calls=%async_computation.2 | async-start | bytes 1572864 | tf_op jit(solution)/shard_map/all_to_all | solution.py:455

commit v8 on v7

--- a/solution.py
+++ b/solution.py
@@ -132,10 +132,14 @@
     return assemble(first[None], swap_cores(first)[None], SECTIONS[:1], 1)[0], rest
 
 
-def finish_weights(rest, left, right):
+def finish_weights(rest, left, right, before_swap):
     far_low, far_high = ring_far(left, right, 0)
     along_y = jnp.stack([rest, left, jnp.concatenate([far_low, far_high], axis=0), right])
-    return assemble(along_y, swap_cores(along_y), SECTIONS[1:], lax.axis_size("tok"))
+    along_y, before_swap = lax.optimization_barrier((along_y, before_swap))
+    return (
+        assemble(along_y, swap_cores(along_y), SECTIONS[1:], lax.axis_size("tok")),
+        before_swap,
+    )
 
 
 def pass_on(value, axis, shift):
@@ -435,11 +439,9 @@
     rest_left, rest_right = near_on_ring(rest, "tok")
     embedded = embed(arrived, embed_full)
     rest_left, rest_right, embedded = lax.optimization_barrier((rest_left, rest_right, embedded))
-    project_full, self_out_full, query_full, keyval_full, cross_out_full = finish_weights(
-        rest, rest_left, rest_right
-    )
-
-    left, right = near_on_ring(embedded, "tok")
+    near = near_on_ring(embedded, "tok")
+    full, (left, right) = finish_weights(rest, rest_left, rest_right, near)
+    project_full, self_out_full, query_full, keyval_full, cross_out_full = full
     far_low, far_high = ring_far(left, right, 1)
     near_keyval, queries, totals = self_step([left, right, embedded], project_full, keyval_full)
     far_keyval, after_self, cross_queries = self_step(

time: 272 us -> 265 us (0.974)
  waiting for transfers between devices: 103 us -> 96.1 us
    ppermute x15, waiting for transfers between devices: 44.7 us -> 36.8 us  [pass_on(): return lax.ppermute(value, axis, cycle(lax.axis_size(axis), shift))]
  transfers between devices with their start and end apart: 21 -> 21, of which waited for: 13 -> 12; matrix products, arithmetic and copies ran while one was open for 3% -> 4% of each run, Pallas kernels for 7% -> 7%
where the time goes in v8:
time: 265 us; the launch traced here: 262 us
  starting transfers between devices  98 us (37%)
  waiting for transfers between devices  96.1 us (36%)
  Pallas kernels  34.8 us (13%)
  blocking collectives  15.4 us (6%)
  local copies, waits for them, and re-layouts  10.9 us (4%)
  other arithmetic  4.71 us (2%)
    ppermute x15, starting transfers between devices, pass_on(): return lax.ppermute(value, axis, cycle(lax.axis_size(axis), shift))  52 us
    all_to_all x1, waiting for transfers between devices, shards(): returned = lax.all_to_all(backward, IMG, 0, 0, tiled=True)  44.1 us
    ppermute x15, waiting for transfers between devices, pass_on(): return lax.ppermute(value, axis, cycle(lax.axis_size(axis), shift))  36.8 us
    pallas_call x2, Pallas kernels, self_step(): pl.pallas_call(functools.partial(self_kernel, first, last, len(pieces)),...  19.6 us
    all_to_all x1, blocking collectives, shards(): lax.all_to_all(partial.reshape(groups, spread, block_rows, model_width //...  15.4 us
    all_to_all x1, starting transfers between devices, start_weights(): return lax.all_to_all(copies, 'z', 0, 0, tiled=True)  15.2 us
    all_to_all x1, starting transfers between devices, shards(): returned = lax.all_to_all(backward, IMG, 0, 0, tiled=True)  14.2 us
    all_to_all x1, starting transfers between devices, shards(): arrived = lax.all_to_all(outgoing, IMG, 0, 0, tiled=True)  10.8 us
  transfers between devices with their start and end apart: 21, of which 12 were waited for; matrix products, arithmetic and copies ran while one was open for 4% of the time, Pallas kernels for 7%

profile of v8, /device:TPU:24, one launch (start us, length us, event | category | flops | bytes accessed | tf_op | source)
XLA Modules:
  0.0 262.4 jit_solution(12534803943125525541)
XLA Ops:
  4.2 15.2 %all-to-all-start = ((bf16[16,84,128]{2,1,0:T(8,128)(2,1)}), bf16[16,84,128]{2,1,0:T(8,128)(2,1)S(1)}, u32[]{:S(2)}, u32[]{:S(2)}) async-start(bf16[16,84,128]{2,1,0:T(8,128)(2,1)} %broadcast_in_dim.26), calls=%async_computation | async-start | bytes 720896 | tf_op jit(solution)/shard_map/all_to_all | solution.py:102
  19.5 4.7 %collective-permute-start.2 = (bf16[32,8,256]{2,1,0:T(8,128)(2,1)S(1)}, bf16[32,8,256]{2,1,0:T(8,128)(2,1)S(1)}, u32[]{:S(2)}, u32[]{:S(2)}) collective-permute-start(bf16[32,8,256]{2,1,0:T(8,128)(2,1)S(1)} %get-tuple-element.65), channel_id=1, source_target_pairs={{0,384},{128,0},{256,128},{384,256},{1,385},{129,1},{257,129},{385... | collective-permute-start | bytes 393224 | tf_op jit(solution)/shard_map/ppermute | solution.py:146
  24.1 2.7 %collective-permute-start.1 = (bf16[32,8,256]{2,1,0:T(8,128)(2,1)S(1)}, bf16[32,8,256]{2,1,0:T(8,128)(2,1)S(1)}, u32[]{:S(2)}, u32[]{:S(2)}) collective-permute-start(bf16[32,8,256]{2,1,0:T(8,128)(2,1)S(1)} %get-tuple-element.66), channel_id=1, source_target_pairs={{0,256},{128,384},{256,0},{384,128},{1,257},{129,385},{257,1},{385... | collective-permute-start | bytes 393224 | tf_op jit(solution)/shard_map/ppermute | solution.py:146
  26.9 2.8 %collective-permute-start = (bf16[32,8,256]{2,1,0:T(8,128)(2,1)S(1)}, bf16[32,8,256]{2,1,0:T(8,128)(2,1)S(1)}, u32[]{:S(2)}, u32[]{:S(2)}) collective-permute-start(bf16[32,8,256]{2,1,0:T(8,128)(2,1)S(1)} %get-tuple-element.67), channel_id=1, source_target_pairs={{0,128},{128,256},{256,384},{384,0},{1,129},{129,257},{257,385},{3... | collective-permute-start | bytes 393224 | tf_op jit(solution)/shard_map/ppermute | solution.py:146
  37.3 4.3 %all-to-all-done = bf16[16,84,128]{2,1,0:T(8,128)(2,1)S(1)} async-done(((bf16[16,84,128]{2,1,0:T(8,128)(2,1)}), bf16[16,84,128]{2,1,0:T(8,128)(2,1)S(1)}, u32[]{:S(2)}, u32[]{:S(2)}) %all-to-all-start) | async-done | bytes 344096 | tf_op jit(solution)/shard_map/all_to_all | solution.py:102
  41.5 10.8 %all-to-all-start.1 = ((bf16[128,2,8,256]{3,2,1,0:T(8,128)(2,1)}), bf16[128,2,8,256]{3,2,1,0:T(8,128)(2,1)S(1)}, u32[]{:S(2)}, u32[]{:S(2)}) async-start(bf16[128,2,8,256]{3,2,1,0:T(8,128)(2,1)} %bitcast.14), calls=%async_computation.1 | async-start | bytes 2097152 | tf_op jit(solution)/shard_map/all_to_all | solution.py:435
  53.2 1.9 collective-permute-start.3
  58.1 4.8 %collective-permute-start.5 = (bf16[1344,128]{1,0:T(8,128)(2,1)S(1)}, bf16[1344,128]{1,0:T(8,128)(2,1)S(1)}, u32[]{:S(2)}, u32[]{:S(2)}) collective-permute-start(bf16[1344,128]{1,0:T(8,128)(2,1)S(1)} %fusion.2), channel_id=1, source_target_pairs={{0,384},{128,0},{256,128},{384,256},{1,385},{129,1},{257,129},{385... | collective-permute-start | bytes 1032200 | tf_op jit(solution)/shard_map/ppermute | solution.py:146
  62.9 1.9 collective-permute-start.4
  64.9 7.5 %collective-permute-done.5 = bf16[1344,128]{1,0:T(8,128)(2,1)S(1)} collective-permute-done((bf16[1344,128]{1,0:T(8,128)(2,1)S(1)}, bf16[1344,128]{1,0:T(8,128)(2,1)S(1)}, u32[]{:S(2)}, u32[]{:S(2)}) %collective-permute-start.5) | collective-permute-done | bytes 344096 | tf_op jit(solution)/shard_map/ppermute | solution.py:146
  72.4 5.6 %collective-permute-start.6 = (bf16[576,128]{1,0:T(8,128)(2,1)S(1)}, bf16[576,128]{1,0:T(8,128)(2,1)S(1)}, u32[]{:S(2)}, u32[]{:S(2)}) collective-permute-start(bf16[576,128]{1,0:T(8,128)(2,1)S(1)} %get-tuple-element.78), channel_id=1, source_target_pairs={{0,384},{128,0},{256,128},{384,256},{1,385},{129,1},{257,129},{385... | collective-permute-start | bytes 442376 | tf_op jit(solution)/shard_map/ppermute | solution.py:146
  78.1 1.9 collective-permute-start.9
  80.0 8.6 %collective-permute-done.9 = bf16[768,128]{1,0:T(8,128)(2,1)S(1)} collective-permute-done((bf16[768,128]{1,0:T(8,128)(2,1)S(1)}, bf16[768,128]{1,0:T(8,128)(2,1)S(1)}, u32[]{:S(2)}, u32[]{:S(2)}) %collective-permute-start.9) | collective-permute-done | bytes 196640 | tf_op jit(solution)/shard_map/ppermute | solution.py:146
  88.8 1.9 collective-permute-start.10
  91.7 2.1 collective-permute-start.7
  93.8 3.7 %collective-permute-start.8 = (bf16[4,576,128]{2,1,0:T(8,128)(2,1)}, bf16[4,576,128]{2,1,0:T(8,128)(2,1)}, u32[]{:S(2)}, u32[]{:S(2)}) collective-permute-start(bf16[4,576,128]{2,1,0:T(8,128)(2,1)} %get-tuple-element.63), channel_id=1, source_target_pairs={{0,3},{1,0},{2,1},{3,2},{4,7},{5,4},{6,5},{7,6},{8,11},{9,8},{10,9... | collective-permute-start | bytes 1769480 | tf_op jit(solution)/shard_map/ppermute | solution.py:146
  98.4 9.6 %all-to-all-done.1 = bf16[128,2,8,256]{3,2,1,0:T(8,128)(2,1)S(1)} async-done(((bf16[128,2,8,256]{3,2,1,0:T(8,128)(2,1)}), bf16[128,2,8,256]{3,2,1,0:T(8,128)(2,1)S(1)}, u32[]{:S(2)}, u32[]{:S(2)}) %all-to-all-start.1) | async-done | bytes 1048608 | tf_op jit(solution)/shard_map/all_to_all | solution.py:435
  109.6 3.1 %collective-permute-done.8 = bf16[4,576,128]{2,1,0:T(8,128)(2,1)} collective-permute-done((bf16[4,576,128]{2,1,0:T(8,128)(2,1)}, bf16[4,576,128]{2,1,0:T(8,128)(2,1)}, u32[]{:S(2)}, u32[]{:S(2)}) %collective-permute-start.8) | collective-permute-done | bytes 589856 | tf_op jit(solution)/shard_map/ppermute | solution.py:146
  112.7 2.4 collective-permute-start.14
  115.2 4.6 %collective-permute-start.13 = (bf16[2,256,768]{2,1,0:T(8,128)(2,1)S(1)}, bf16[2,256,768]{2,1,0:T(8,128)(2,1)S(1)}, u32[]{:S(2)}, u32[]{:S(2)}) collective-permute-start(bf16[2,256,768]{2,1,0:T(8,128)(2,1)S(1)} %embed.1.refs_2_.refs_4_), channel_id=1, source_target_pairs={{0,1},{1,2},{2,3},{3,0},{4,5},{5,6},{6,7},{7,4},{8,9},{9,10},{10,1... | collective-permute-start | bytes 2359304 | tf_op jit(solution)/shard_map/ppermute | solution.py:146
  123.7 5.1 %collective-permute-start.11 = (bf16[2,576,128]{2,1,0:T(8,128)(2,1)S(1)}, bf16[2,576,128]{2,1,0:T(8,128)(2,1)S(1)}, u32[]{:S(2)}, u32[]{:S(2)}) collective-permute-start(bf16[2,576,128]{2,1,0:T(8,128)(2,1)S(1)} %slice.70), channel_id=1, source_target_pairs={{0,1},{1,2},{2,3},{3,0},{4,5},{5,6},{6,7},{7,4},{8,9},{9,10},{10,1... | collective-permute-start | bytes 884744 | tf_op jit(solution)/shard_map/ppermute | solution.py:146
  128.8 12.2 %collective-permute-done.12 = bf16[2,576,128]{2,1,0:T(8,128)(2,1)S(1)} collective-permute-done((bf16[2,576,128]{2,1,0:T(8,128)(2,1)S(1)}, bf16[2,576,128]{2,1,0:T(8,128)(2,1)S(1)}, u32[]{:S(2)}, u32[]{:S(2)}) %collective-permute-start.12) | collective-permute-done | bytes 294944 | tf_op jit(solution)/shard_map/ppermute | solution.py:146
  143.9 1.9 collective-permute-start.17
  145.9 2.3 collective-permute-start.16
  148.2 5.4 %collective-permute-start.15 = (bf16[2,128,768]{2,1,0:T(8,128)(2,1)S(1)}, bf16[2,128,768]{2,1,0:T(8,128)(2,1)S(1)}, u32[]{:S(2)}, u32[]{:S(2)}) collective-permute-start(bf16[2,128,768]{2,1,0:T(8,128)(2,1)S(1)} %slice.72), channel_id=1, source_target_pairs={{0,1},{1,2},{2,3},{3,0},{4,5},{5,6},{6,7},{7,4},{8,9},{9,10},{10,1... | collective-permute-start | bytes 1179656 | tf_op jit(solution)/shard_map/ppermute | solution.py:146
  153.6 4.4 %assemble.3 = (bf16[4,2,96,1152]{3,2,1,0:T(8,128)(2,1)}, bf16[4,2,48,768]{3,2,1,0:T(8,128)(2,1)S(1)}, bf16[4,2,96,384]{3,2,1,0:T(8,128)(2,1)S(1)}, bf16[4,2,96,7...) custom-call(s32[3]{0:T(128)S(1)} %pad_add_fusion.1.at_ref, bf16[4,4,576,128]{3,2,1,0:T(8,128)(2,1)} %copy-done.4, ...), custom_call_target="tpu_custom_call" | custom-call | bytes 9437184 | tf_op jit(solution)/shard_map/assemble/pallas_call | solution.py:185
  158.1 11.9 %self_step.2 = (bf16[2,768,768]{2,1,0:T(8,128)(2,1)}, bf16[2,256,384]{2,1,0:T(8,128)(2,1)S(1)}, f32[2,6,256,128]{3,2,1,0:T(8,128)}) custom-call(bf16[2,256,768]{2,1,0:T(8,128)(2,1)S(1)} %collective-permute-done.13.refs_0_, bf16[2,256,768]{2,1,0:T(8,128)(2,1)S(1)} %collective-permute-done.14.refs_1_, bf16[2,256,768]{2,1,0:T(8,128)(2,1)S(1)} %embed.1.refs_2_.refs_4_, ...), custom_call_target="tpu_custom_call" | custom-call | flops 4831838208 | bytes 5308416 | tf_op jit(solution)/shard_map/self_step/pallas_call | solution.py:348
  170.0 7.7 %self_step.3 = (bf16[2,256,768]{2,1,0:T(8,128)(2,1)S(1)}, f32[2,256,768]{2,1,0:T(8,128)}, bf16[2,256,384]{2,1,0:T(8,128)(2,1)S(1)}) custom-call(bf16[2,128,768]{2,1,0:T(8,128)(2,1)S(1)} %collective-permute-done.15.refs_0_, bf16[2,128,768]{2,1,0:T(8,128)(2,1)S(1)} %collective-permute-done.16.refs_1_, bf16[2,256,384]{2,1,0:T(8,128)(2,1)S(1)} %get-tuple-element.48.refs_2_, ...), custom_call_target="tpu_custom_call" | custom-call | flops 1610612736 | bytes 7667712 | tf_op jit(solution)/shard_map/self_step/pallas_call | solution.py:348
  179.0 7.6 %cross_block.1 = bf16[2,2,32,8,384]{4,3,2,1,0:T(8,128)(2,1)} custom-call(f32[2,256,768]{2,1,0:T(8,128)S(1)} %copy-done.3, bf16[2,256,384]{2,1,0:T(8,128)(2,1)S(1)} %get-tuple-element.53.query_ref, bf16[2,768,768]{2,1,0:T(8,128)(2,1)} %get-tuple-element.54.refs_0_, bf16[2,256,768]{2,1,0:T(8,128)(2,1)S(1)} %get-tuple-element.55.refs_1_, ...), custom_call_target="tpu_custom_call" | custom-call | flops 1912602624 | bytes 3342336 | tf_op jit(solution)/shard_map/cross_block/pallas_call | solution.py:386
  186.7 14.2 %all-to-all-start.2 = ((bf16[128,8,384]{2,1,0:T(8,128)(2,1)}), bf16[128,8,384]{2,1,0:T(8,128)(2,1)S(1)}, u32[]{:S(2)}, u32[]{:S(2)}) async-start(bf16[128,8,384]{2,1,0:T(8,128)(2,1)} %bitcast.41), calls=%async_computation.2 | async-start | bytes 1572864 | tf_op jit(solution)/shard_map/all_to_all | solution.py:457
  201.2 44.1 %all-to-all-done.2 = bf16[128,8,384]{2,1,0:T(8,128)(2,1)S(1)} async-done(((bf16[128,8,384]{2,1,0:T(8,128)(2,1)}), bf16[128,8,384]{2,1,0:T(8,128)(2,1)S(1)}, u32[]{:S(2)}, u32[]{:S(2)}) %all-to-all-start.2) | async-done | bytes 786464 | tf_op jit(solution)/shard_map/all_to_all | solution.py:457
  246.1 15.4 %all_to_all.20 = bf16[4,32,8,384]{3,2,1,0:T(8,128)(2,1)S(1)} all-to-all(bf16[4,32,8,384]{3,2,1,0:T(8,128)(2,1)S(1)} %copy.44), channel_id=1, replica_groups=mesh['x'=4,'z'=16,'c'=2,'tok'=4] {'x'}, dimensions={0} | all-to-all | bytes 1572864 | tf_op jit(solution)/shard_map/all_to_all | solution.py:466
  (78 shorter events, 29.3 us)
Async XLA Ops:
  0.0 30.0 %copy-start = (s32[128]{0:T(128)S(1)}, s32[128]{0:T(128)}, u32[]{:S(2)}) copy-start(s32[128]{0:T(128)} %param.14) | copy-start | bytes 1540
  0.0 29.7 %copy-start.6 = (s32[128,2]{0,1:T(2,128)S(1)}, s32[128,2]{0,1:T(2,128)}, u32[]{:S(2)}) copy-start(s32[128,2]{0,1:T(2,128)} %param.13) | copy-start | bytes 3076
  4.2 37.4 %all-to-all-start = ((bf16[16,84,128]{2,1,0:T(8,128)(2,1)}), bf16[16,84,128]{2,1,0:T(8,128)(2,1)S(1)}, u32[]{:S(2)}, u32[]{:S(2)}) async-start(bf16[16,84,128]{2,1,0:T(8,128)(2,1)} %broadcast_in_dim.26), calls=%async_computation | async-start | bytes 720896 | tf_op jit(solution)/shard_map/all_to_all | solution.py:102
  19.5 12.4 %collective-permute-start.2 = (bf16[32,8,256]{2,1,0:T(8,128)(2,1)S(1)}, bf16[32,8,256]{2,1,0:T(8,128)(2,1)S(1)}, u32[]{:S(2)}, u32[]{:S(2)}) collective-permute-start(bf16[32,8,256]{2,1,0:T(8,128)(2,1)S(1)} %get-tuple-element.65), channel_id=1, source_target_pairs={{0,384},{128,0},{256,128},{384,256},{1,385},{129,1},{257,129},{385... | collective-permute-start | bytes 393224 | tf_op jit(solution)/shard_map/ppermute | solution.py:146
  24.1 9.5 %collective-permute-start.1 = (bf16[32,8,256]{2,1,0:T(8,128)(2,1)S(1)}, bf16[32,8,256]{2,1,0:T(8,128)(2,1)S(1)}, u32[]{:S(2)}, u32[]{:S(2)}) collective-permute-start(bf16[32,8,256]{2,1,0:T(8,128)(2,1)S(1)} %get-tuple-element.66), channel_id=1, source_target_pairs={{0,256},{128,384},{256,0},{384,128},{1,257},{129,385},{257,1},{385... | collective-permute-start | bytes 393224 | tf_op jit(solution)/shard_map/ppermute | solution.py:146
  26.9 8.6 %collective-permute-start = (bf16[32,8,256]{2,1,0:T(8,128)(2,1)S(1)}, bf16[32,8,256]{2,1,0:T(8,128)(2,1)S(1)}, u32[]{:S(2)}, u32[]{:S(2)}) collective-permute-start(bf16[32,8,256]{2,1,0:T(8,128)(2,1)S(1)} %get-tuple-element.67), channel_id=1, source_target_pairs={{0,128},{128,256},{256,384},{384,0},{1,129},{129,257},{257,385},{3... | collective-permute-start | bytes 393224 | tf_op jit(solution)/shard_map/ppermute | solution.py:146
  35.5 16.8 %copy-start.7 = (s32[3]{0:T(128)S(1)}, s32[3]{0:T(128)}, u32[]{:S(2)}) copy-start(s32[3]{0:T(128)} %constant.155) | copy-start | bytes 40
  35.5 17.6 %copy-start.5 = (s32[3,768]{1,0:T(4,128)S(1)}, s32[3,768]{1,0:T(4,128)}, u32[]{:S(2)}) copy-start(s32[3,768]{1,0:T(4,128)} %constant.147.clone) | copy-start | bytes 27652
  41.5 66.4 %all-to-all-start.1 = ((bf16[128,2,8,256]{3,2,1,0:T(8,128)(2,1)}), bf16[128,2,8,256]{3,2,1,0:T(8,128)(2,1)S(1)}, u32[]{:S(2)}, u32[]{:S(2)}) async-start(bf16[128,2,8,256]{3,2,1,0:T(8,128)(2,1)} %bitcast.14), calls=%async_computation.1 | async-start | bytes 2097152 | tf_op jit(solution)/shard_map/all_to_all | solution.py:435
  53.2 3.3 %collective-permute-start.3 = (bf16[8,84,128]{2,1,0:T(8,128)(2,1)S(1)}, bf16[8,84,128]{2,1,0:T(8,128)(2,1)S(1)}, u32[]{:S(2)}, u32[]{:S(2)}) collective-permute-start(bf16[8,84,128]{2,1,0:T(8,128)(2,1)S(1)} %get-tuple-element.75), channel_id=1, source_target_pairs={{0,4},{4,0},{1,5},{5,1},{2,6},{6,2},{3,7},{7,3},{8,12},{12,8},{9,1... | collective-permute-start | bytes 516104 | tf_op jit(solution)/shard_map/ppermute | solution.py:96
  58.1 14.3 %collective-permute-start.5 = (bf16[1344,128]{1,0:T(8,128)(2,1)S(1)}, bf16[1344,128]{1,0:T(8,128)(2,1)S(1)}, u32[]{:S(2)}, u32[]{:S(2)}) collective-permute-start(bf16[1344,128]{1,0:T(8,128)(2,1)S(1)} %fusion.2), channel_id=1, source_target_pairs={{0,384},{128,0},{256,128},{384,256},{1,385},{129,1},{257,129},{385... | collective-permute-start | bytes 1032200 | tf_op jit(solution)/shard_map/ppermute | solution.py:146
  62.9 15.1 %collective-permute-start.4 = (bf16[1344,128]{1,0:T(8,128)(2,1)S(1)}, bf16[1344,128]{1,0:T(8,128)(2,1)S(1)}, u32[]{:S(2)}, u32[]{:S(2)}) collective-permute-start(bf16[1344,128]{1,0:T(8,128)(2,1)S(1)} %fusion.2), channel_id=1, source_target_pairs={{0,128},{128,256},{256,384},{384,0},{1,129},{129,257},{257,385},{3... | collective-permute-start | bytes 1032200 | tf_op jit(solution)/shard_map/ppermute | solution.py:146
  72.4 18.3 %collective-permute-start.6 = (bf16[576,128]{1,0:T(8,128)(2,1)S(1)}, bf16[576,128]{1,0:T(8,128)(2,1)S(1)}, u32[]{:S(2)}, u32[]{:S(2)}) collective-permute-start(bf16[576,128]{1,0:T(8,128)(2,1)S(1)} %get-tuple-element.78), channel_id=1, source_target_pairs={{0,384},{128,0},{256,128},{384,256},{1,385},{129,1},{257,129},{385... | collective-permute-start | bytes 442376 | tf_op jit(solution)/shard_map/ppermute | solution.py:146
  78.1 10.6 %collective-permute-start.9 = (bf16[768,128]{1,0:T(8,128)(2,1)S(1)}, bf16[768,128]{1,0:T(8,128)(2,1)S(1)}, u32[]{:S(2)}, u32[]{:S(2)}) collective-permute-start(bf16[768,128]{1,0:T(8,128)(2,1)S(1)} %get-tuple-element.77), channel_id=1, source_target_pairs={{0,128},{128,256},{256,384},{384,0},{1,129},{129,257},{257,385},{3... | collective-permute-start | bytes 589832 | tf_op jit(solution)/shard_map/ppermute | solution.py:146
  88.8 8.8 %collective-permute-start.10 = (bf16[4,768,128]{2,1,0:T(8,128)(2,1)S(1)}, bf16[4,768,128]{2,1,0:T(8,128)(2,1)S(1)}, u32[]{:S(2)}, u32[]{:S(2)}) collective-permute-start(bf16[4,768,128]{2,1,0:T(8,128)(2,1)S(1)} %get-tuple-element.60), channel_id=1, source_target_pairs={{0,4},{4,0},{1,5},{5,1},{2,6},{6,2},{3,7},{7,3},{8,12},{12,8},{9,1... | collective-permute-start | bytes 2359304 | tf_op jit(solution)/shard_map/ppermute | solution.py:96
  91.7 17.9 %collective-permute-start.7 = (bf16[4,576,128]{2,1,0:T(8,128)(2,1)}, bf16[4,576,128]{2,1,0:T(8,128)(2,1)}, u32[]{:S(2)}, u32[]{:S(2)}) collective-permute-start(bf16[4,576,128]{2,1,0:T(8,128)(2,1)} %get-tuple-element.63), channel_id=1, source_target_pairs={{0,1},{1,2},{2,3},{3,0},{4,5},{5,6},{6,7},{7,4},{8,9},{9,10},{10,1... | collective-permute-start | bytes 1769480 | tf_op jit(solution)/shard_map/ppermute | solution.py:146
  93.8 18.9 %collective-permute-start.8 = (bf16[4,576,128]{2,1,0:T(8,128)(2,1)}, bf16[4,576,128]{2,1,0:T(8,128)(2,1)}, u32[]{:S(2)}, u32[]{:S(2)}) collective-permute-start(bf16[4,576,128]{2,1,0:T(8,128)(2,1)} %get-tuple-element.63), channel_id=1, source_target_pairs={{0,3},{1,0},{2,1},{3,2},{4,7},{5,4},{6,5},{7,6},{8,11},{9,8},{10,9... | collective-permute-start | bytes 1769480 | tf_op jit(solution)/shard_map/ppermute | solution.py:146
  109.0 49.1 %copy-start.1 = (bf16[2,256,768]{2,1,0:T(8,128)(2,1)}, bf16[2,256,768]{2,1,0:T(8,128)(2,1)S(1)}, u32[]{:S(2)}) copy-start(bf16[2,256,768]{2,1,0:T(8,128)(2,1)S(1)} %embed.1.refs_2_.refs_4_) | copy-start | bytes 2359300
  112.7 31.1 %collective-permute-start.14 = (bf16[2,256,768]{2,1,0:T(8,128)(2,1)S(1)}, bf16[2,256,768]{2,1,0:T(8,128)(2,1)S(1)}, u32[]{:S(2)}, u32[]{:S(2)}) collective-permute-start(bf16[2,256,768]{2,1,0:T(8,128)(2,1)S(1)} %embed.1.refs_2_.refs_4_), channel_id=1, source_target_pairs={{0,3},{1,0},{2,1},{3,2},{4,7},{5,4},{6,5},{7,6},{8,11},{9,8},{10,9... | collective-permute-start | bytes 2359304 | tf_op jit(solution)/shard_map/ppermute | solution.py:146
  115.2 28.7 %collective-permute-start.13 = (bf16[2,256,768]{2,1,0:T(8,128)(2,1)S(1)}, bf16[2,256,768]{2,1,0:T(8,128)(2,1)S(1)}, u32[]{:S(2)}, u32[]{:S(2)}) collective-permute-start(bf16[2,256,768]{2,1,0:T(8,128)(2,1)S(1)} %embed.1.refs_2_.refs_4_), channel_id=1, source_target_pairs={{0,1},{1,2},{2,3},{3,0},{4,5},{5,6},{6,7},{7,4},{8,9},{9,10},{10,1... | collective-permute-start | bytes 2359304 | tf_op jit(solution)/shard_map/ppermute | solution.py:146
  121.8 19.3 %collective-permute-start.12 = (bf16[2,576,128]{2,1,0:T(8,128)(2,1)S(1)}, bf16[2,576,128]{2,1,0:T(8,128)(2,1)S(1)}, u32[]{:S(2)}, u32[]{:S(2)}) collective-permute-start(bf16[2,576,128]{2,1,0:T(8,128)(2,1)S(1)} %slice.71), channel_id=1, source_target_pairs={{0,3},{1,0},{2,1},{3,2},{4,7},{5,4},{6,5},{7,6},{8,11},{9,8},{10,9... | collective-permute-start | bytes 884744 | tf_op jit(solution)/shard_map/ppermute | solution.py:146
  123.7 18.6 %collective-permute-start.11 = (bf16[2,576,128]{2,1,0:T(8,128)(2,1)S(1)}, bf16[2,576,128]{2,1,0:T(8,128)(2,1)S(1)}, u32[]{:S(2)}, u32[]{:S(2)}) collective-permute-start(bf16[2,576,128]{2,1,0:T(8,128)(2,1)S(1)} %slice.70), channel_id=1, source_target_pairs={{0,1},{1,2},{2,3},{3,0},{4,5},{5,6},{6,7},{7,4},{8,9},{9,10},{10,1... | collective-permute-start | bytes 884744 | tf_op jit(solution)/shard_map/ppermute | solution.py:146
  143.8 9.8 %copy-start.4 = (bf16[4,4,576,128]{3,2,1,0:T(8,128)(2,1)}, bf16[4,4,576,128]{3,2,1,0:T(8,128)(2,1)S(1)}, u32[]{:S(2)}) copy-start(bf16[4,4,576,128]{3,2,1,0:T(8,128)(2,1)S(1)} %pad_maximum_fusion.mine_ref) | copy-start | bytes 7077892
  143.9 9.7 %collective-permute-start.17 = (bf16[4,4,576,128]{3,2,1,0:T(8,128)(2,1)S(1)}, bf16[4,4,576,128]{3,2,1,0:T(8,128)(2,1)}, u32[]{:S(2)}, u32[]{:S(2)}) collective-permute-start(bf16[4,4,576,128]{3,2,1,0:T(8,128)(2,1)S(1)} %pad_maximum_fusion.mine_ref), channel_id=1, source_target_pairs={{0,4},{4,0},{1,5},{5,1},{2,6},{6,2},{3,7},{7,3},{8,12},{12,8},{9,1... | collective-permute-start | bytes 7077896 | tf_op jit(solution)/shard_map/ppermute | solution.py:96
  145.9 24.1 %collective-permute-start.16 = (bf16[2,128,768]{2,1,0:T(8,128)(2,1)S(1)}, bf16[2,128,768]{2,1,0:T(8,128)(2,1)S(1)}, u32[]{:S(2)}, u32[]{:S(2)}) collective-permute-start(bf16[2,128,768]{2,1,0:T(8,128)(2,1)S(1)} %slice.73), channel_id=1, source_target_pairs={{0,3},{1,0},{2,1},{3,2},{4,7},{5,4},{6,5},{7,6},{8,11},{9,8},{10,9... | collective-permute-start | bytes 1179656 | tf_op jit(solution)/shard_map/ppermute | solution.py:146
  148.2 21.8 %collective-permute-start.15 = (bf16[2,128,768]{2,1,0:T(8,128)(2,1)S(1)}, bf16[2,128,768]{2,1,0:T(8,128)(2,1)S(1)}, u32[]{:S(2)}, u32[]{:S(2)}) collective-permute-start(bf16[2,128,768]{2,1,0:T(8,128)(2,1)S(1)} %slice.72), channel_id=1, source_target_pairs={{0,1},{1,2},{2,3},{3,0},{4,5},{5,6},{6,7},{7,4},{8,9},{9,10},{10,1... | collective-permute-start | bytes 1179656 | tf_op jit(solution)/shard_map/ppermute | solution.py:146
  158.0 11.9 %copy-start.2 = (bf16[4,2,96,768]{3,2,1,0:T(8,128)(2,1)}, bf16[4,2,96,768]{3,2,1,0:T(8,128)(2,1)S(1)}, u32[]{:S(2)}) copy-start(bf16[4,2,96,768]{3,2,1,0:T(8,128)(2,1)S(1)} %get-tuple-element.47) | copy-start | bytes 3538948
  177.6 1.4 copy-start.3
  186.7 58.6 %all-to-all-start.2 = ((bf16[128,8,384]{2,1,0:T(8,128)(2,1)}), bf16[128,8,384]{2,1,0:T(8,128)(2,1)S(1)}, u32[]{:S(2)}, u32[]{:S(2)}) async-start(bf16[128,8,384]{2,1,0:T(8,128)(2,1)} %bitcast.41), calls=%async_computation.2 | async-start | bytes 1572864 | tf_op jit(solution)/shard_map/all_to_all | solution.py:457
